TPU v7x, 256 devices: a whole 4x4x8 slice. The times are simulated.
256 devices in a mesh: store: 32 (over z, x), head: 8 (over y, core).
Axes of the slice: x: 4, y: 4, z: 8, core: 2. Of those that a mesh axis runs over, the one named last changes fastest.
Arguments:
- hidden: bfloat16 [32, 128, 8192], P('store'), may hold values from -6 to 6
- w_query: bfloat16 [8192, 4096], P('store', 'head'), may hold values from -0.0625 to 0.0625
- w_key_value: bfloat16 [8192, 2048], P('store', 'head'), may hold values from -0.0625 to 0.0625
- block_kv: bfloat16 [64, 512, 2048], P('store', None, 'head'), may hold values from -68 to 68
- history_kv: bfloat16 [32, 512, 2048], P('store', 'head'), may hold values from -6 to 6
- block_lists: int32 [32, 8], replicated, may hold values from 0 to 63, as said below
- sel_pos: int32 [32, 128], P('store'), may hold values from 0 to 4095, as said below
- hist_len: int32 [32], P('store'), may hold values from 1 to 512, 8192 in all
Outputs:
- attended: bfloat16 [32, 128, 4096], P('store', None, 'head')
Inputs may be any that keep to these rules, and one draw needn't show every extreme that they name: `block_lists`: of the 8 blocks named by the requests of one index of store (requests r with r // 1 equal), at most 1 have the same owner block // 2, and some owner is named exactly 1 times. `sel_pos`: the positions of one request are distinct and include 8 * 512 - 1.
All inputs are finite; a program needn't handle non-finite values. No bound on the sum of `hist_len` on one device may be relied on, other than what follows from the above.
Results may differ from a plain program's by a relative error of at most 0.011.
The roundings to bfloat16 on the way count: a program that leaves them out, or rounds other values in their place, can miss the bound.
Values may be sent and summed in bfloat16 or wider, within the bound.
No kernel may reach another device: no remote copies, remote signals or barrier semaphores. Data moves between devices by JAX's collectives and lax.ppermute only.
A program may use at most 128 MiB of HBM per device.

v0:
```python
import jax
import jax.numpy as jnp
from jax import lax
from jax.sharding import PartitionSpec as P


def rotate(values, position):
    halfway = values.shape[-1] // 2
    inverse = 500000.0 ** (-(jnp.arange(halfway, dtype=jnp.float32) * 2.0 / values.shape[-1]))
    angles = position.astype(jnp.float32)[:, None] * inverse
    shape_out = (angles.shape[0],) + (1,) * (values.ndim - 2) + (halfway,)
    cosine = jnp.cos(angles).reshape(shape_out)
    sine_part = jnp.sin(angles).reshape(shape_out)
    leading = values[..., :halfway]
    trailing = values[..., halfway:]
    return jnp.concatenate(
        [leading * cosine - trailing * sine_part, trailing * cosine + leading * sine_part], -1
    )


def per_device(hidden, w_query, w_key_value, block_kv, history_kv, block_lists, sel_pos, hist_len):
    request_count = hidden.shape[0]
    sel_rows = hidden.shape[1]
    head_size = w_key_value.shape[1] // 2
    query_width = w_query.shape[1]
    flat = hidden.reshape(-1, hidden.shape[-1])
    qraw = jnp.dot(
        flat,
        lax.all_gather(w_query, "store", axis=0, tiled=True),
        preferred_element_type=jnp.float32,
    )
    fresh = jnp.dot(
        flat,
        lax.all_gather(w_key_value, "store", axis=0, tiled=True),
        preferred_element_type=jnp.float32,
    )
    qraw = qraw.reshape(request_count, sel_rows, query_width)
    fresh = fresh.astype(jnp.bfloat16).reshape(request_count, sel_rows, 2 * head_size)
    my_group = lax.axis_index("store")
    everything = lax.all_gather(block_kv, "store", axis=0, tiled=True)
    my_lists = lax.dynamic_slice_in_dim(block_lists, my_group * request_count, request_count, 0)
    cached = jnp.take(everything, my_lists.reshape(-1), axis=0)
    cached = cached.reshape(request_count, -1, block_kv.shape[-1])
    history = lax.all_to_all(history_kv, "head", split_axis=2, concat_axis=1, tiled=True)
    history_slots = history.shape[1]
    score_scale = head_size ** (-0.5)

    def one_request(inputs):
        query_rows, fresh_rows, cached_rows, past, positions, length = inputs
        query_pos = length + positions
        queries = rotate(query_rows.reshape(sel_rows, -1, head_size), query_pos).astype(
            jnp.bfloat16
        )
        blended = cached_rows.at[positions].set(fresh_rows)
        block_pos = length + jnp.arange(blended.shape[0], dtype=jnp.int32)
        ctx_keys = rotate(blended[:, :head_size].astype(jnp.float32), block_pos).astype(
            jnp.bfloat16
        )
        keys = jnp.concatenate([past[:, :head_size], ctx_keys], 0)
        values = jnp.concatenate([past[:, head_size:], blended[:, head_size:]], 0)
        slots = jnp.arange(history_slots, dtype=jnp.int32)
        key_pos = jnp.concatenate([slots, block_pos], 0)
        live = jnp.concatenate([slots < length, block_pos >= 0], 0)
        allowed = live[None, :] & (key_pos[None, :] <= query_pos[:, None])
        scores = (
            jnp.einsum("sqd,kd->qsk", queries, keys, preferred_element_type=jnp.float32)
            * score_scale
        )
        scores = jnp.where(allowed[None], scores, -jnp.inf)
        row_max = jnp.max(scores, axis=-1, keepdims=True)
        weights = jnp.exp(scores - row_max)
        weights = (weights / jnp.sum(weights, axis=-1, keepdims=True)).astype(jnp.bfloat16)
        mixed = jnp.einsum("qsk,kd->sqd", weights, values, preferred_element_type=jnp.float32)
        return mixed.astype(jnp.bfloat16).reshape(sel_rows, query_width)

    return lax.map(one_request, (qraw, fresh, cached, history, sel_pos, hist_len))


def solution(mesh):
    in_specs = (
        P("store", None, None),
        P("store", "head"),
        P("store", "head"),
        P("store", None, "head"),
        P("store", "head", None),
        P(),
        P("store", None),
        P("store"),
    )
    out_specs = P("store", None, "head")
    return jax.shard_map(
        per_device, mesh=mesh, in_specs=in_specs, out_specs=out_specs, check_vma=False
    )
```

profile of v0, /device:TPU:8, one launch (start us, length us, event | category | flops | bytes accessed | tf_op | source)
XLA Modules:
  0.0 366.6 jit_solution(13594149789940566273)
XLA Ops:
  6.5 0.7 all-gather.6.cloned.1.call-update
  8.8 2.2 copy.40
  11.5 12.4 %reduce.3 = bf16[2048,64]{1,0:T(8,128)(2,1)} reduce(bf16[2048,1,64]{2,1,0:T(2,128)(2,1)S(1)} %bitcast.66, bf16[]{:T(256)} %broadcast.184), dimensions={1}, to_apply=%bitcast.50.reduce_sub_computation | reduce | bytes 524290
  23.9 2.2 reshape.231
  26.0 5.5 %all-to-all-start = ((bf16[8,2,8192]{2,1,0:T(2,128)(2,1)}), bf16[8,2,8192]{2,1,0:T(2,128)(2,1)S(1)}, u32[]{:S(2)}, u32[]{:S(2)}) async-start(bf16[8,2,8192]{2,1,0:T(2,128)(2,1)} %reshape.231), calls=%async_computation | async-start | bytes 524288 | tf_op jit(solution)/shard_map/all_to_all | solution.py:44
  32.6 4.0 %compare_and_fusion = pred[128,4608]{0,1:T(8,128)(4,1)} fusion(s32[128]{0:T(128)S(1)} %get-tuple-element.20, s32[4608]{0:T(1024)S(1)} %pad_add_fusion, pred[4608]{0:T(1024)(128)(4,1)S(1)} %pad_add_fusion.1), kind=kLoop, calls=%fused_computation.12 | loop fusion | flops 1179648 | bytes 613376 | tf_op jit(solution)/shard_map/while/body/eval_jaxpr/and | solution.py:64
  36.8 0.8 all-to-all-done
  39.0 0.8 copy.56
  39.9 54.7 %all-gather.6.cloned.1.call-done = bf16[8192,256]{1,0:T(8,128)(2,1)} async-done(((bf16[256,256]{1,0:T(8,128)(2,1)}), bf16[8192,256]{1,0:T(8,128)(2,1)}) %all-gather.6.cloned.1.call-update) | async-done | bytes 4194320 | tf_op jit(solution)/shard_map/all_gather | solution.py:34
  94.6 2.9 fusion.23
  97.5 95.4 %all-gather.8.cloned.1.call-done = bf16[8192,512]{1,0:T(8,128)(2,1)} async-done(((bf16[256,512]{1,0:T(8,128)(2,1)}), bf16[8192,512]{1,0:T(8,128)(2,1)}) %all-gather.8.cloned.1.call-update) | async-done | bytes 8388624 | tf_op jit(solution)/shard_map/all_gather | solution.py:29
  192.9 11.8 %copy.47 = bf16[512,8192]{1,0:T(8,128)(2,1)} copy(bf16[512,8192]{0,1:T(8,128)(2,1)} %bitcast.63) | data formatting | bytes 16777216 | tf_op jit(solution)/shard_map/dot_general | solution.py:27
  204.7 6.0 %fusion.7 = f32[128,4,128]{0,2,1:T(8,128)S(1)} fusion(bf16[4,128,8192]{2,1,0:T(8,128)(2,1)} %bitcast.64, bf16[1,128,8192]{2,1,0:T(8,128)(2,1)S(1)} %copy-done), kind=kOutput, calls=%fused_computation.13 | convolution fusion | flops 1073741824 | bytes 10747904 | tf_op jit(solution)/shard_map/dot_general | solution.py:27
  210.8 122.4 %all-gather.4.cloned.1.call-done = bf16[64,512,256]{2,1,0:T(8,128)(2,1)} async-done(((bf16[2,512,256]{2,1,0:T(8,128)(2,1)}), bf16[64,512,256]{2,1,0:T(8,128)(2,1)}) %all-gather.4.cloned.1.call-update) | async-done | bytes 16777232 | tf_op jit(solution)/shard_map/all_gather | solution.py:40
  333.2 7.8 %gather_fusion = bf16[8,512,256]{2,1,0:T(8,128)(2,1)} fusion(bf16[64,512,256]{2,1,0:T(8,128)(2,1)} %all-gather.4.cloned.1.call-done, s32[1024]{0:T(1024)S(1)} %pad_clamp_fusion), kind=kCustom, calls=%fused_computation | custom fusion | bytes 4194336 | tf_op jit(solution)/shard_map/jit(_take)/gather | solution.py:42
  341.0 1.9 bitcast_select_fusion.2
  342.9 2.4 scatter_fusion
  345.4 1.1 fusion.42
  346.5 1.3 copy.57
  348.6 4.2 %fusion.27 = (bf16[4096,64]{0,1:T(8,128)(2,1)S(1)}, bf16[4096,64]{0,1:T(8,128)(2,1)S(1)}) fusion(f32[4096,128]{0,1:T(8,128)S(1)} %convert_element_type.39, f32[64]{0:T(128)S(1)} %negate_power_fusion, f32[4096]{0:T(1024)S(1)} %get-tuple-element.44), kind=kLoop, calls=%fused_computation.36 | loop fusion | flops 2359296 | bytes 3162368 | tf_op jit(solution)/shard_map/convert.2
  352.8 1.4 fusion.17
  354.3 3.3 exponential_reduce_fusion
  357.6 1.7 fusion.22
  359.3 0.8 copy.51
  (48 shorter events, 4.8 us)
Async XLA Ops:
  6.5 88.1 %copy-start = (bf16[1,128,8192]{2,1,0:T(8,128)(2,1)S(1)}, bf16[1,128,8192]{2,1,0:T(8,128)(2,1)}, u32[]{:S(2)}) copy-start(bf16[1,128,8192]{2,1,0:T(8,128)(2,1)} %param.8) | copy-start | bytes 6291460
  6.5 88.1 %all-gather.6.cloned.1.call-start = ((), (), s32[]{:S(2)}) async-start(), calls=%async_computation.2 | async-start | bytes 4325376 | tf_op jit(solution)/shard_map/all_gather | solution.py:34
  7.3 185.7 %all-gather.8.cloned.1.call-start = ((), (), s32[]{:S(2)}) async-start(), calls=%async_computation.3 | async-start | bytes 8650752 | tf_op jit(solution)/shard_map/all_gather | solution.py:29
  8.0 24.2 %copy-start.6 = (s32[32,8]{0,1:T(8,128)S(1)}, s32[32,8]{0,1:T(8,128)}, u32[]{:S(2)}) copy-start(s32[32,8]{0,1:T(8,128)} %param.13) | copy-start | bytes 3076
  8.0 24.5 %copy-start.7 = (s32[1,128]{1,0:T(1,128)S(1)}, s32[1,128]{1,0:T(1,128)}, u32[]{:S(2)}) copy-start(s32[1,128]{1,0:T(1,128)} %param.14) | copy-start | bytes 1540
  8.0 325.2 %all-gather.4.cloned.1.call-start = ((), (), s32[]{:S(2)}) async-start(), calls=%async_computation.1 | async-start | bytes 17301504 | tf_op jit(solution)/shard_map/all_gather | solution.py:40
  26.0 11.6 %all-to-all-start = ((bf16[8,2,8192]{2,1,0:T(2,128)(2,1)}), bf16[8,2,8192]{2,1,0:T(2,128)(2,1)S(1)}, u32[]{:S(2)}, u32[]{:S(2)}) async-start(bf16[8,2,8192]{2,1,0:T(2,128)(2,1)} %reshape.231), calls=%async_computation | async-start | bytes 524288 | tf_op jit(solution)/shard_map/all_to_all | solution.py:44
  346.5 1.3 copy-start.2
  352.8 1.4 copy-start.3
  354.2 3.3 copy-start.4
  354.2 3.3 copy-start.5
  357.6 2.5 copy-start.1
Sparse Core Ops, SparseCore 0:
  9.9 84.6 all-gather.5
  97.2 95.6 all-gather.7
  195.5 137.6 all-gather.3
where the time goes:
time: 368 us; the launch traced here: 367 us
  waiting for transfers between devices  275 us (75%)
  local copies, waits for them, and re-layouts  33.1 us (9%)
  other arithmetic  26.3 us (7%)
  between operations  14.1 us (4%)
  matrix products  12.1 us (3%)
  starting transfers between devices  5.57 us (2%)
    all_gather x1, waiting for transfers between devices, per_device(): everything = lax.all_gather(block_kv, 'store', axis=0, tiled=True)  122 us
    all_gather x1, waiting for transfers between devices, per_device(): lax.all_gather(w_query, 'store', axis=0, tiled=True)  95.4 us
    all_gather x1, waiting for transfers between devices, per_device(): lax.all_gather(w_key_value, 'store', axis=0, tiled=True)  54.7 us
    unnamed x1, other arithmetic  12.4 us
    dot_general x1, local copies, waits for them, and re-layouts, per_device(): jnp.dot(flat, lax.all_gather(w_query, 'store', axis=0, tiled=True), prefe...  11.8 us
    unnamed x27, local copies, waits for them, and re-layouts  8.37 us
    gather x1, local copies, waits for them, and re-layouts, per_device(): cached = jnp.take(everything, my_lists.reshape(-1), axis=0)  7.77 us
  transfers between devices with their start and end apart: 4, of which 4 were waited for; matrix products, arithmetic and copies ran while one was open for 12% of the time, Pallas kernels for 0%

commit v1 on v0

v1 whole, which is shorter than its diff:
```python
import jax
import jax.numpy as jnp
import numpy as np
from jax import lax
from jax.sharding import Mesh
from jax.sharding import PartitionSpec as P

NZ, NX, NH = 8, 4, 8
SEL, HEAD, QPER, BLOCK, RET, HIST = 128, 128, 4, 512, 8, 512
CONTEXT = RET * BLOCK
PIECE = BLOCK // NX
FAR = 1 << 20
INVERSE = (500000.0 ** (-(np.arange(64, dtype=np.float64) * 2.0 / 128))).astype(np.float32)


def angles(position):
    return position.astype(jnp.float32)[:, None] * jnp.asarray(INVERSE)


def rotate(values, cosine, sine):
    a, b = values[..., :64], values[..., 64:]
    return jnp.concatenate([a * cosine - b * sine, b * cosine + a * sine], -1)


def per_device(hidden, w_query, w_key_value, block_kv, history_kv, block_lists, sel_pos, hist_len):
    z, x = lax.axis_index("z"), lax.axis_index("x")
    length, sel = hist_len[0], sel_pos[0]

    pieces = block_kv.reshape(2, NX, PIECE, 2 * HEAD).transpose(1, 0, 2, 3)
    pieces = lax.all_to_all(pieces, "x", 0, 0, tiled=True)
    weights = lax.all_gather(jnp.concatenate([w_query, w_key_value], 1), "z", axis=0, tiled=True)
    pieces = lax.all_gather(pieces, "z", axis=0, tiled=True)
    pieces = pieces.reshape(2 * NZ * NX, PIECE, 2 * HEAD)
    row_lists = lax.dynamic_slice_in_dim(block_lists, z * NX, NX, 0).reshape(-1)

    rows = hidden[0].reshape(SEL, NZ, NX, 256).transpose(2, 0, 1, 3).reshape(NX, SEL, NZ * 256)
    rows = lax.all_to_all(rows, "x", 0, 0, tiled=True)
    partial = jnp.dot(rows.reshape(NX * SEL, NZ * 256), weights, preferred_element_type=jnp.float32)
    partial = lax.all_to_all(partial.reshape(NX, SEL, -1), "x", 0, 0, tiled=True)
    projected = jnp.sum(partial, 0)
    qraw, fresh = projected[:, : QPER * HEAD], projected[:, QPER * HEAD :].astype(jnp.bfloat16)

    past = history_kv[0].reshape(HIST // NH, NH, 2 * HEAD).transpose(1, 0, 2)
    past = lax.all_to_all(past, "head", 0, 0, tiled=True).reshape(HIST, 2 * HEAD)

    cached = pieces[row_lists].reshape(NX, RET, PIECE, 2 * HEAD)
    cached = lax.all_to_all(cached, "x", 0, 0, tiled=True).reshape(CONTEXT, 2 * HEAD)
    order = np.arange(CONTEXT, dtype=np.int32).reshape(RET, NX, PIECE).transpose(1, 0, 2).reshape(-1)
    place = jnp.asarray(order)

    replaced = jnp.any(place[:, None] == sel[None, :], axis=1)
    slots = jnp.arange(HIST, dtype=jnp.int32)
    key_pos = jnp.concatenate(
        [jnp.where(slots < length, -1, FAR), jnp.where(replaced, FAR, place), sel]
    )
    qangle, cangle = angles(length + sel), angles(length + place)
    qcos, qsin, ccos, csin = jnp.cos(qangle), jnp.sin(qangle), jnp.cos(cangle), jnp.sin(cangle)

    queries = rotate(qraw.reshape(SEL, QPER, HEAD), qcos[:, None], qsin[:, None])
    queries = queries.astype(jnp.bfloat16).transpose(1, 0, 2)
    fresh_keys = rotate(fresh[:, :HEAD].astype(jnp.float32), qcos, qsin).astype(jnp.bfloat16)
    ctx_keys = rotate(cached[:, :HEAD].astype(jnp.float32), ccos, csin).astype(jnp.bfloat16)
    keys = jnp.concatenate([past[:, :HEAD], ctx_keys, fresh_keys], 0)
    values = jnp.concatenate([past[:, HEAD:], cached[:, HEAD:], fresh[:, HEAD:]], 0)
    scores = jnp.einsum("qsd,kd->qsk", queries, keys, preferred_element_type=jnp.float32)
    scores = scores * (HEAD ** (-0.5))
    scores = jnp.where((key_pos[None, :] <= sel[:, None])[None], scores, -jnp.inf)
    top = jnp.max(scores, axis=-1, keepdims=True)
    mass = jnp.exp(scores - top)
    mass = (mass / jnp.sum(mass, axis=-1, keepdims=True)).astype(jnp.bfloat16)
    mixed = jnp.einsum("qsk,kd->sqd", mass, values, preferred_element_type=jnp.float32)
    return mixed.astype(jnp.bfloat16).reshape(1, SEL, QPER * HEAD)


def solution(mesh):
    split = Mesh(mesh.devices.reshape(NZ, NX, NH), ("z", "x", "head"))
    store = ("z", "x")
    in_specs = (
        P(store, None, None),
        P(store, "head"),
        P(store, "head"),
        P(store, None, "head"),
        P(store, "head", None),
        P(),
        P(store, None),
        P(store),
    )
    return jax.shard_map(
        per_device, mesh=split, in_specs=in_specs, out_specs=P(store, None, "head"), check_vma=False
    )
```

time: 368 us -> 169 us (0.46)
  waiting for transfers between devices: 275 us -> 77.5 us
  blocking collectives: 0 us -> 13.7 us
  starting transfers between devices: 5.57 us -> 17.4 us
  local copies, waits for them, and re-layouts: 33.1 us -> 21.4 us
  other arithmetic: 26.3 us -> 15.2 us
    all_gather x3 -> x2, waiting for transfers between devices: 273 us -> 35.4 us  [the longest x1 35.4 us: per_device(): pieces = lax.all_gather(pieces, 'z', axis=0, tiled=True)]
    all_to_all x1 -> x4, waiting for transfers between devices: 0.84 us -> 42.1 us  [the longest x1 24.6 us: per_device(): rows = lax.all_to_all(rows, 'x', 0, 0, tiled=True)]
    all_to_all x0 -> x1, blocking collectives: none -> 13.7 us  [per_device(): pieces = lax.all_to_all(pieces, 'x', 0, 0, tiled=True)]
    unnamed x1 -> x0, other arithmetic: 12.4 us -> none
    all_to_all x1 -> x4, starting transfers between devices: 5.49 us -> 17.4 us  [the longest x1 4.91 us: per_device(): lax.all_to_all(past, 'head', 0, 0, tiled=True).reshape(HIST, 2 * HEAD)]
    dot_general x1 -> x0, local copies, waits for them, and re-layouts: 11.8 us -> none  [per_device(): jnp.dot(flat, lax.all_gather(w_query, 'store', axis=0, tiled=True), prefe...]
    gather x1, local copies, waits for them, and re-layouts: 7.77 us -> 2.87 us  [per_device(): cached = pieces[row_lists].reshape(NX, RET, PIECE, 2 * HEAD)]
    and x2 -> x0, other arithmetic: 3.98 us -> none  [the longest x1 3.98 us: one_request(): allowed = live[None, :] & (key_pos[None, :] <= query_pos[:, None])]
  transfers between devices with their start and end apart: 4 -> 6, of which waited for: 4 -> 3; matrix products, arithmetic and copies ran while one was open for 12% -> 18% of each run, Pallas kernels for 0% -> 0%
where the time goes in v1:
time: 169 us; the launch traced here: 168 us
  waiting for transfers between devices  77.5 us (46%)
  local copies, waits for them, and re-layouts  21.4 us (13%)
  starting transfers between devices  17.4 us (10%)
  other arithmetic  15.2 us (9%)
  between operations  14.3 us (8%)
  blocking collectives  13.7 us (8%)
  matrix products  8.71 us (5%)
    all_gather x1, waiting for transfers between devices, per_device(): pieces = lax.all_gather(pieces, 'z', axis=0, tiled=True)  35.4 us
    all_to_all x1, waiting for transfers between devices, per_device(): rows = lax.all_to_all(rows, 'x', 0, 0, tiled=True)  24.6 us
    all_to_all x1, waiting for transfers between devices, per_device(): lax.all_to_all(cached, 'x', 0, 0, tiled=True).reshape(CONTEXT, 2 * HEAD)  17.6 us
    all_to_all x1, blocking collectives, per_device(): pieces = lax.all_to_all(pieces, 'x', 0, 0, tiled=True)  13.7 us
    unnamed x23, local copies, waits for them, and re-layouts  6.08 us
    dot_general x1, matrix products, per_device(): jnp.dot(rows.reshape(NX * SEL, NZ * 256), weights, preferred_element_type...  5.45 us
    another operation x2, other arithmetic  5.18 us
    all_to_all x1, starting transfers between devices, per_device(): lax.all_to_all(past, 'head', 0, 0, tiled=True).reshape(HIST, 2 * HEAD)  4.91 us
  transfers between devices with their start and end apart: 6, of which 3 were waited for; matrix products, arithmetic and copies ran while one was open for 18% of the time, Pallas kernels for 0%

profile of v1, /device:TPU:8, one launch (start us, length us, event | category | flops | bytes accessed | tf_op | source)
XLA Modules:
  0.0 168.3 jit_solution(7717548260120719328)
XLA Ops:
  6.5 1.8 %pad_maximum_fusion = bf16[256,768]{1,0:T(8,128)(2,1)} fusion(bf16[256,256]{1,0:T(8,128)(2,1)} %param.12, bf16[256,512]{1,0:T(8,128)(2,1)} %param.11), kind=kLoop, calls=%fused_computation.40 | loop fusion | flops 786432 | bytes 786432 | tf_op jit(solution)/shard_map/concatenate | solution.py:31
  8.4 1.1 copy.122
  9.5 13.7 %all_to_all.25 = bf16[4,2,128,256]{3,2,1,0:T(8,128)(2,1)} all-to-all(bf16[4,2,128,256]{3,2,1,0:T(8,128)(2,1)S(1)} %copy.122), channel_id=1, replica_groups=mesh['z'=8,'x'=4,'head'=8] {'x'}, dimensions={0} | all-to-all | bytes 1048576 | tf_op jit(solution)/shard_map/all_to_all | solution.py:30
  23.2 3.2 %copy.126 = bf16[1,128,8192]{1,2,0:T(8,128)(2,1)S(1)} copy(bf16[1,128,8192]{2,1,0:T(8,128)(2,1)} %param.10) | data formatting | bytes 4194304 | tf_op args[0]
  26.4 1.5 copy.127
  28.0 3.7 %all-to-all-start.3 = ((bf16[4,128,2048]{1,2,0:T(8,128)(2,1)}), bf16[4,128,2048]{1,2,0:T(8,128)(2,1)S(1)}, u32[]{:S(2)}, u32[]{:S(2)}) async-start(bf16[4,128,2048]{1,2,0:T(8,128)(2,1)} %bitcast.51), calls=%async_computation.3 | async-start | bytes 4194304 | tf_op jit(solution)/shard_map/all_to_all | solution.py:37
  32.6 24.6 %all-to-all-done.3 = bf16[4,128,2048]{1,2,0:T(8,128)(2,1)S(1)} async-done(((bf16[4,128,2048]{1,2,0:T(8,128)(2,1)}), bf16[4,128,2048]{1,2,0:T(8,128)(2,1)S(1)}, u32[]{:S(2)}, u32[]{:S(2)}) %all-to-all-start.3) | async-done | bytes 2097184 | tf_op jit(solution)/shard_map/all_to_all | solution.py:37
  57.1 4.9 %all-to-all-start = ((bf16[8,64,256]{2,1,0:T(8,128)(2,1)}), bf16[8,64,256]{2,1,0:T(8,128)(2,1)S(1)}, u32[]{:S(2)}, u32[]{:S(2)}) async-start(bf16[8,64,256]{2,1,0:T(8,128)(2,1)} %copy.120), calls=%async_computation | async-start | bytes 524288 | tf_op jit(solution)/shard_map/all_to_all | solution.py:44
  62.0 2.7 %copy.128 = bf16[4,128,2048]{2,1,0:T(8,128)(2,1)} copy(bf16[4,128,2048]{1,2,0:T(8,128)(2,1)S(1)} %all-to-all-done.3) | data formatting | bytes 4194304 | tf_op jit(solution)/shard_map/all_to_all | solution.py:37
  64.7 5.5 %fusion.41 = f32[768,512]{0,1:T(8,128)} fusion(bf16[512,2048]{1,0:T(8,128)(2,1)} %bitcast.56, bf16[2048,768]{1,0:T(8,128)(2,1)} %all-gather.5.cloned.1.call-done), kind=kOutput, calls=%fused_computation.70 | convolution fusion | flops 1610612736 | bytes 6815744 | tf_op jit(solution)/shard_map/dot_general | solution.py:38
  70.2 4.5 %all-to-all-start.4 = ((f32[4,128,768]{2,1,0:T(8,128)}), f32[4,128,768]{2,1,0:T(8,128)}, u32[]{:S(2)}, u32[]{:S(2)}) async-start(f32[4,128,768]{2,1,0:T(8,128)} %bitcast.12), calls=%async_computation.4 | async-start | bytes 3145728 | tf_op jit(solution)/shard_map/all_to_all | solution.py:39
  75.6 1.3 compare_reduce_fusion
  76.9 35.4 %all-gather.3.cloned.1.call-done = bf16[32,2,128,256]{3,2,1,0:T(8,128)(2,1)} async-done(((bf16[4,2,128,256]{3,2,1,0:T(8,128)(2,1)}), bf16[32,2,128,256]{3,2,1,0:T(8,128)(2,1)}) %all-gather.3.cloned.1.call-update) | async-done | bytes 4194320 | tf_op jit(solution)/shard_map/all_gather | solution.py:32
  112.3 2.9 %gather_fusion = bf16[32,128,256]{2,1,0:T(8,128)(2,1)S(1)} fusion(bf16[64,128,256]{2,1,0:T(8,128)(2,1)} %bitcast.57, s32[1024]{0:T(1024)S(1)} %pad_clamp_fusion), kind=kCustom, calls=%fused_computation | custom fusion | bytes 4194432 | tf_op jit(solution)/shard_map/gather | solution.py:46
  115.2 2.6 %copy.124 = bf16[4,8,128,256]{2,1,3,0:T(8,128)(2,1)} copy(bf16[4,8,128,256]{3,2,1,0:T(8,128)(2,1)S(1)} %bitcast.53) | data formatting | bytes 4194304 | tf_op jit(solution)/shard_map/reshape | solution.py:46
  117.8 4.2 %all-to-all-start.2 = ((bf16[4,8,128,256]{2,1,3,0:T(8,128)(2,1)}), bf16[4,8,128,256]{2,1,3,0:T(8,128)(2,1)S(1)}, u32[]{:S(2)}, u32[]{:S(2)}) async-start(bf16[4,8,128,256]{2,1,3,0:T(8,128)(2,1)} %copy.124), calls=%async_computation.2 | async-start | bytes 4194304 | tf_op jit(solution)/shard_map/all_to_all | solution.py:47
  124.0 1.5 reduce_sum.18
  126.5 1.4 fusion.39
  130.8 17.6 %all-to-all-done.2 = bf16[4,8,128,256]{2,1,3,0:T(8,128)(2,1)S(1)} async-done(((bf16[4,8,128,256]{2,1,3,0:T(8,128)(2,1)}), bf16[4,8,128,256]{2,1,3,0:T(8,128)(2,1)S(1)}, u32[]{:S(2)}, u32[]{:S(2)}) %all-to-all-start.2) | async-done | bytes 2097184 | tf_op jit(solution)/shard_map/all_to_all | solution.py:47
  148.8 1.0 copy.147
  150.1 4.2 %fusion.25 = (bf16[4096,64]{0,1:T(8,128)(2,1)S(1)}, bf16[4096,64]{0,1:T(8,128)(2,1)S(1)}) fusion(f32[4096,128]{0,1:T(8,128)S(1)} %get-tuple-element.8, f32[64]{0:T(128)S(1)} %copy-done.7, f32[4096]{0:T(1024)S(1)} %get-tuple-element.20), kind=kLoop, calls=%fused_computation.36 | loop fusion | flops 2359296 | bytes 3162368 | tf_op jit(solution)/shard_map/convert.2
  154.3 1.5 fusion.14
  155.8 3.1 %fusion.40 = (f32[4,128]{1,0:T(4,128)S(1)}, f32[4,128,4736]{2,1,0:T(8,128)S(1)}) fusion(f32[4,128,4736]{2,1,0:T(8,128)S(1)} %fusion.14, pred[128,4736]{1,0:T(8,128)(4,1)S(1)} %broadcast_compare_fusion), kind=kOutput, calls=%fused_computation.69 | output fusion | flops 9704063 | bytes 20006912 | tf_op jit(solution)/shard_map/sub | solution.py:69
  158.9 1.8 %fusion.23 = bf16[128,4,128]{2,0,1:T(8,128)(2,1)S(1)} fusion(f32[4,128,4736]{2,1,0:T(8,128)S(1)} %get-tuple-element.26, f32[4,128]{1,0:T(4,128)S(1)} %get-tuple-element.25, bf16[128,128]{0,1:T(8,128)(2,1)S(1)} %copy-done.5, bf16[4096,128]{0,1:T(8,128)(2,1)S(1)} %get-tuple-element.7, bf16[512,128]{0,1:T(8,128)(2,1)S(1)} %copy-done.3), kind=kOutput, calls=%fused_computation.34 | convolution fusion | flops 629309440 | bytes 11044864 | tf_op jit(solution)/shard_map/qsk,kd->sqd/dot_general | solution.py:71
  (51 shorter events, 8.4 us)
Async XLA Ops:
  6.5 68.8 %copy-start = (s32[32,8]{0,1:T(8,128)S(1)}, s32[32,8]{0,1:T(8,128)}, u32[]{:S(2)}) copy-start(s32[32,8]{0,1:T(8,128)} %param.15) | copy-start | bytes 3076
  6.5 58.2 %all-gather.5.cloned.1.call-start = ((), (), s32[]{:S(2)}) async-start(), calls=%async_computation.6 | async-start | bytes 3538944 | tf_op jit(solution)/shard_map/all_gather | solution.py:31
  8.4 103.9 %all-gather.3.cloned.1.call-start = ((), (), s32[]{:S(2)}) async-start(), calls=%async_computation.5 | async-start | bytes 4718592 | tf_op jit(solution)/shard_map/all_gather | solution.py:32
  28.0 3.8 %copy-start.2 = (bf16[1,64,2048]{2,1,0:T(8,128)(2,1)S(1)}, bf16[1,64,2048]{2,1,0:T(8,128)(2,1)}, u32[]{:S(2)}) copy-start(bf16[1,64,2048]{2,1,0:T(8,128)(2,1)} %param.14) | copy-start | bytes 786436
  28.0 29.1 %all-to-all-start.3 = ((bf16[4,128,2048]{1,2,0:T(8,128)(2,1)}), bf16[4,128,2048]{1,2,0:T(8,128)(2,1)S(1)}, u32[]{:S(2)}, u32[]{:S(2)}) async-start(bf16[4,128,2048]{1,2,0:T(8,128)(2,1)} %bitcast.51), calls=%async_computation.3 | async-start | bytes 4194304 | tf_op jit(solution)/shard_map/all_to_all | solution.py:37
  57.1 13.0 %all-to-all-start = ((bf16[8,64,256]{2,1,0:T(8,128)(2,1)}), bf16[8,64,256]{2,1,0:T(8,128)(2,1)S(1)}, u32[]{:S(2)}, u32[]{:S(2)}) async-start(bf16[8,64,256]{2,1,0:T(8,128)(2,1)} %copy.120), calls=%async_computation | async-start | bytes 524288 | tf_op jit(solution)/shard_map/all_to_all | solution.py:44
  70.2 5.4 %copy-start.4 = (s32[4096]{0:T(1024)S(1)}, s32[4096]{0:T(1024)}, u32[]{:S(2)}) copy-start(s32[4096]{0:T(1024)} %constant.31.clone) | copy-start | bytes 49156
  70.2 5.5 %copy-start.6 = (s32[1,128]{1,0:T(1,128)S(1)}, s32[1,128]{1,0:T(1,128)}, u32[]{:S(2)}) copy-start(s32[1,128]{1,0:T(1,128)} %param.16) | copy-start | bytes 1540
  70.2 47.6 %all-to-all-start.4 = ((f32[4,128,768]{2,1,0:T(8,128)}), f32[4,128,768]{2,1,0:T(8,128)}, u32[]{:S(2)}, u32[]{:S(2)}) async-start(f32[4,128,768]{2,1,0:T(8,128)} %bitcast.12), calls=%async_computation.4 | async-start | bytes 3145728 | tf_op jit(solution)/shard_map/all_to_all | solution.py:39
  117.8 30.6 %all-to-all-start.2 = ((bf16[4,8,128,256]{2,1,3,0:T(8,128)(2,1)}), bf16[4,8,128,256]{2,1,3,0:T(8,128)(2,1)S(1)}, u32[]{:S(2)}, u32[]{:S(2)}) async-start(bf16[4,8,128,256]{2,1,3,0:T(8,128)(2,1)} %copy.124), calls=%async_computation.2 | async-start | bytes 4194304 | tf_op jit(solution)/shard_map/all_to_all | solution.py:47
  122.4 5.5 %copy-start.7 = (f32[64]{0:T(128)S(1)}, f32[64]{0:T(128)}, u32[]{:S(2)}) copy-start(f32[64]{0:T(128)} %constant.32.clone) | copy-start | bytes 772
  150.0 4.2 %copy-start.1 = (bf16[512,128]{0,1:T(8,128)(2,1)S(1)}, bf16[512,128]{0,1:T(8,128)(2,1)}, u32[]{:S(2)}) copy-start(bf16[512,128]{0,1:T(8,128)(2,1)} %copy.143) | copy-start | bytes 393220
  155.8 3.1 %copy-start.3 = (bf16[512,128]{0,1:T(8,128)(2,1)S(1)}, bf16[512,128]{0,1:T(8,128)(2,1)}, u32[]{:S(2)}) copy-start(bf16[512,128]{0,1:T(8,128)(2,1)} %copy.140) | copy-start | bytes 393220
  155.8 3.1 %copy-start.5 = (bf16[128,128]{0,1:T(8,128)(2,1)S(1)}, bf16[128,128]{0,1:T(8,128)(2,1)}, u32[]{:S(2)}) copy-start(bf16[128,128]{0,1:T(8,128)(2,1)} %get-tuple-element.15) | copy-start | bytes 98308
Sparse Core Ops, SparseCore 0:
  9.1 47.8 all-gather.4
  58.8 53.4 all-gather.2

commit v2 on v1

v2 whole, which is shorter than its diff:
```python
import functools

import jax
import jax.numpy as jnp
import numpy as np
from jax import lax
from jax.experimental import pallas as pl
from jax.experimental.pallas import tpu as pltpu
from jax.sharding import Mesh
from jax.sharding import PartitionSpec as P

NZ, NX, NH = 8, 4, 8
SEL, HEAD, QPER, BLOCK, RET, HIST = 128, 128, 4, 512, 8, 512
CONTEXT = RET * BLOCK
PIECE = BLOCK // NX
WIDE = (QPER + 2) * HEAD
FAR = 1 << 20
FREE = pl.CostEstimate(flops=0, bytes_accessed=0, transcendentals=0)
COST = pl.CostEstimate(flops=5 * 10**10, bytes_accessed=1 << 20, transcendentals=0)
HALF = SEL // 2
KEYS = HIST + CONTEXT + SEL
INVERSE = (500000.0 ** (-(np.arange(64, dtype=np.float64) * 2.0 / 128))).astype(np.float32)
INVERSE = np.concatenate([INVERSE, INVERSE])
UP = [(i, (i + 1) % NZ) for i in range(NZ)]
DOWN = [(i, (i - 1) % NZ) for i in range(NZ)]
SMEM = pl.BlockSpec(memory_space=pltpu.SMEM)
VMEM = pl.BlockSpec(memory_space=pltpu.VMEM)
ANY = pl.BlockSpec(memory_space=pltpu.HBM)
PARAMS = pltpu.CompilerParams(vmem_limit_bytes=56 << 20)


def kernel_call(body, out, inputs, smem=0, scratch=()):
    many = isinstance(out, (list, tuple))
    return pl.pallas_call(
        body,
        out_shape=out,
        in_specs=[SMEM] * smem + [VMEM] * (len(inputs) - smem),
        out_specs=[VMEM] * len(out) if many else VMEM,
        scratch_shapes=scratch,
        compiler_params=PARAMS,
        cost_estimate=FREE,
    )(*inputs)


def after(value, *others):
    return lax.optimization_barrier((value, *others))[0]


def turn(values, cosine, sine):
    return values * cosine + pltpu.roll(values, 64, 1) * sine


def prepare_kernel(
    z_ref, head_ref, hidden, w_query, w_key_value, block, history,
    both, pieces, rows, past, held_both, held_pieces, held_rows, held_past, sems,
):
    loads = [
        [
            (w_query, held_both.at[:, : QPER * HEAD]),
            (w_key_value, held_both.at[:, QPER * HEAD :]),
        ],
        [],
        [],
        [(history.at[:, i * 256 : (i + 1) * 256], held_past.at[i]) for i in range(NH)],
    ]
    for x in range(NX):
        for kind in range(2):
            part = block.at[:, x * PIECE : (x + 1) * PIECE, kind * HEAD : (kind + 1) * HEAD]
            loads[1].append((part, held_pieces.at[x, kind]))
    mine = pl.ds(pl.multiple_of((head_ref[0] & 1) * HALF, HALF), HALF)
    for hop in range(NZ):
        chunk = ((z_ref[0] + hop) & (NZ - 1)) * NX
        for x in range(NX):
            at = pl.multiple_of((chunk + x) * 256, 256)
            to = held_rows.at[x, :, hop * 256 : (hop + 1) * 256]
            loads[2].append((hidden.at[mine, pl.ds(at, 256)], to))
    loads = [
        [pltpu.make_async_copy(*pair, sems.at[group]) for pair in pairs]
        for group, pairs in enumerate(loads)
    ]
    for group in loads:
        for load in group:
            load.start()
    stores = []
    pairs = (held_both, both), (held_pieces, pieces), (held_rows, rows), (held_past, past)
    for group, pair in enumerate(pairs):
        for load in loads[group]:
            load.wait()
        stores.append(pltpu.make_async_copy(*pair, sems.at[4 + group]))
        stores[-1].start()
    for store in stores:
        store.wait()


def waves(position, inverse):
    angle = position.astype(jnp.float32) * inverse
    turns = jnp.floor(angle * np.float32(2 / np.pi) + 0.5)
    rest = angle - turns * np.float32(1.5703125)
    rest = rest - turns * np.float32(4.837512969970703125e-4)
    rest = rest - turns * np.float32(7.54978995489188216e-8)
    square = rest * rest
    sine = np.float32(-1.9515295891e-4) * square + np.float32(8.3321608736e-3)
    sine = (sine * square + np.float32(-1.6666654611e-1)) * square * rest + rest
    cosine = np.float32(2.443315711809948e-5) * square + np.float32(-1.388731625493765e-3)
    cosine = (cosine * square + np.float32(4.166664568298827e-2)) * square * square
    cosine = cosine - np.float32(0.5) * square + np.float32(1.0)
    first = lax.broadcasted_iota(jnp.int32, angle.shape, 1) < 64
    quarter = turns.astype(jnp.int32) + jnp.where(first, 1, 0)
    wave = jnp.where((quarter & 1) == 1, cosine, sine)
    wave = jnp.where((quarter & 2) == 2, -wave, wave)
    other = pltpu.roll(wave, 64, 1)
    return jnp.where(first, wave, other), jnp.where(first, -other, wave)


def pick_kernel(kind, z_ref, lists_ref, *refs):
    sources, out, held, sems = refs[:NZ], *refs[NZ:]
    z = z_ref[0]

    def part(x):
        return pl.ds(x * RET, RET)

    def leaf(at, away, inner, low, high):
        if high - low == 1:
            to = held.at[at]
            pltpu.make_async_copy(sources[low].at[inner], to, sems.at[at >> 3]).start()
            return
        middle = (low + high) // 2

        @pl.when(away < middle)
        def _():
            leaf(at, away, inner, low, middle)

        @pl.when(away >= middle)
        def _():
            leaf(at, away, inner, middle, high)

    def one(at, _):
        block = lists_ref[z * NX + (at >> 3), at & 7]
        inner = ((block & 6) << 1) + 2 * kind + (block & 1)
        leaf(at, ((block >> 3) - z) & (NZ - 1), inner, 0, NZ)
        return 0

    lax.fori_loop(0, NX * RET, one, 0, unroll=4)
    stores = []
    for x in range(NX):
        pltpu.make_async_copy(held.at[part(x)], held.at[part(x)], sems.at[x]).wait()
        stores.append(pltpu.make_async_copy(held.at[part(x)], out.at[part(x)], sems.at[NX + x]))
        stores[-1].start()
    for store in stores:
        store.wait()


def pick(z, block_lists, sources, kind):
    out = pl.pallas_call(
        functools.partial(pick_kernel, kind),
        out_shape=jax.ShapeDtypeStruct((NX * RET, PIECE, HEAD), jnp.bfloat16),
        in_specs=[SMEM, SMEM] + [ANY] * NZ,
        out_specs=ANY,
        scratch_shapes=[
            pltpu.VMEM((NX * RET, PIECE, HEAD), jnp.bfloat16),
            pltpu.SemaphoreType.DMA((2 * NX,)),
        ],
        compiler_params=PARAMS,
        cost_estimate=FREE,
    )(z, block_lists, *sources)
    return out.reshape(NX, RET, PIECE, HEAD)


def project_kernel(head_ref, received, swapped, *refs):
    weights, out, whole, rows, total, sems = refs[:NZ], *refs[NZ:]
    core = head_ref[0] & 1
    loads = [
        pltpu.make_async_copy(weights[hop], whole.at[pl.ds(hop * 256, 256)], sems.at[0])
        for hop in range(NZ)
    ]
    for x in range(NX):
        for source, half in ((received, core), (swapped, 1 - core)):
            at = pl.ds(pl.multiple_of(x * SEL + half * HALF, HALF), HALF)
            loads.append(pltpu.make_async_copy(source.at[x], rows.at[at], sems.at[0]))
    for load in loads:
        load.start()
    for load in loads:
        load.wait()
    stores = []
    for at in range(0, WIDE, 256):
        part = jnp.dot(rows[...], whole[:, at : at + 256], preferred_element_type=jnp.float32)
        total[:, :, at : at + 256] = part.reshape(NX, SEL, 256)
        columns = pl.ds(at, 256)
        stores.append(
            pltpu.make_async_copy(total.at[:, :, columns], out.at[:, :, columns], sems.at[1])
        )
        stores[-1].start()
    for store in stores:
        store.wait()


def queries_kernel(length_ref, partial_ref, column_ref, inverse_ref, query_ref, key_ref, value_ref):
    cosine, sine = waves(column_ref[...] + length_ref[0], inverse_ref[...])
    for part in range(QPER + 2):
        at = slice(part * HEAD, (part + 1) * HEAD)
        total = partial_ref[0, :, at] + partial_ref[1, :, at]
        total = total + partial_ref[2, :, at] + partial_ref[3, :, at]
        if part < QPER:
            query_ref[part * SEL : (part + 1) * SEL] = turn(total, cosine, sine).astype(jnp.bfloat16)
        elif part == QPER:
            fresh = total.astype(jnp.bfloat16).astype(jnp.float32)
            key_ref[...] = turn(fresh, cosine, sine).astype(jnp.bfloat16)
        else:
            value_ref[...] = total.astype(jnp.bfloat16)


def weigh_kernel(
    length_ref, query_ref, raw_ref, past_ref, fresh_ref, row_ref, column_ref, inverse_ref,
    out, raw, keys, place, scores, mass, sem, out_sem,
):
    fetch = pltpu.make_async_copy(raw_ref, raw, sem)
    fetch.start()
    length, inverse, column = length_ref[0], inverse_ref[...], column_ref[...]
    slots = lax.broadcasted_iota(jnp.int32, (1, HIST), 1)
    place[:, :HIST] = jnp.where(slots < length, -1, FAR)
    place[:, HIST + CONTEXT :] = row_ref[...]
    keys[:HIST] = past_ref[:, :HEAD]
    keys[HIST + CONTEXT :] = fresh_ref[...]
    fetch.wait()

    def rotate(step, _):
        rows = lax.broadcasted_iota(jnp.int32, (4 * PIECE, 1), 0)
        base = (step & 1) * (4 * BLOCK) + (step >> 1) * PIECE
        rows = base + (rows >> 7) * BLOCK + (rows & 127)
        at = pl.multiple_of(step * (4 * PIECE), 4 * PIECE)
        cosine, sine = waves(rows + length, inverse)
        key = turn(raw[pl.ds(at, 4 * PIECE)].astype(jnp.float32), cosine, sine)
        keys[pl.ds(at + HIST, 4 * PIECE)] = key.astype(jnp.bfloat16)
        here = lax.broadcasted_iota(jnp.int32, (1, 4 * PIECE), 1)
        here = base + (here >> 7) * BLOCK + (here & 127)
        hits = jnp.max(jnp.where(column == here, 1, 0), axis=0, keepdims=True)
        place[:, pl.ds(at + HIST, 4 * PIECE)] = jnp.where(hits > 0, FAR, here)
        return 0

    lax.fori_loop(0, CONTEXT // (4 * PIECE), rotate, 0)
    scores[...] = lax.dot_general(
        query_ref[...], keys[...], (((1,), (1,)), ((), ())), preferred_element_type=jnp.float32
    ) * np.float32(HEAD**-0.5)

    def sending(at):
        return pltpu.make_async_copy(mass.at[pl.ds(at, SEL)], out.at[pl.ds(at, SEL)], out_sem)

    def soften(step, _):
        at = pl.multiple_of(step * SEL, SEL)
        part = jnp.where(place[...] <= column, scores[pl.ds(at, SEL)], -jnp.inf)
        part = jnp.exp(part - jnp.max(part, axis=1, keepdims=True))
        part = part * (1.0 / jnp.sum(part, axis=1, keepdims=True))
        mass[pl.ds(at, SEL)] = part.astype(jnp.bfloat16)
        sending(at).start()
        return 0

    lax.fori_loop(0, QPER, soften, 0)
    for head in range(QPER):
        sending(head * SEL).wait()


def mix_kernel(mass_ref, value_ref, past_ref, fresh_ref, out_ref, mass, values, sems):
    fetches = [pltpu.make_async_copy(value_ref, values.at[pl.ds(HIST, CONTEXT)], sems.at[QPER])]
    early = [
        pltpu.make_async_copy(past_ref.at[:, HEAD:], values.at[pl.ds(0, HIST)], sems.at[QPER + 1]),
        pltpu.make_async_copy(
            fresh_ref, values.at[pl.ds(HIST + CONTEXT, SEL)], sems.at[QPER + 1]
        ),
    ]
    for fetch in early:
        fetch.start()
    for head in range(QPER):
        rows = pl.ds(head * SEL, SEL)
        fetches.append(pltpu.make_async_copy(mass_ref.at[rows], mass.at[rows], sems.at[head]))
    for fetch in fetches:
        fetch.start()
    for fetch in early:
        fetch.wait()
    fetches[0].wait()
    for pair in range(0, QPER, 2):
        fetches[pair + 1].wait()
        fetches[pair + 2].wait()
        part = mass[pair * SEL : (pair + 2) * SEL]
        mixed = jnp.dot(part, values[...], preferred_element_type=jnp.float32)
        for head in range(2):
            at = (pair + head) * HEAD
            out_ref[:, at : at + HEAD] = mixed[head * SEL : (head + 1) * SEL].astype(jnp.bfloat16)


def per_device(hidden, w_query, w_key_value, block_kv, history_kv, block_lists, sel_pos, hist_len):
    z = lax.axis_index("z").reshape(1)
    sel = sel_pos[0]
    bf16, f32 = jnp.bfloat16, jnp.float32

    head = lax.axis_index("head").reshape(1)
    shapes = (256, WIDE), (NX, 2, 2, PIECE, HEAD), (NX, HALF, NZ * 256), (NH, HIST // NH, 256)
    both, pieces, rows, past = pl.pallas_call(
        prepare_kernel,
        out_shape=[jax.ShapeDtypeStruct(shape, bf16) for shape in shapes],
        in_specs=[SMEM] * 2 + [ANY] * 5,
        out_specs=[ANY] * 4,
        scratch_shapes=[pltpu.VMEM(shape, bf16) for shape in shapes]
        + [pltpu.SemaphoreType.DMA((8,))],
        compiler_params=PARAMS,
        cost_estimate=COST,
    )(z, head, hidden[0], w_query, w_key_value, block_kv, history_kv[0])

    pieces = lax.all_to_all(pieces, "x", 0, 0, tiled=True)
    w_up, w_down = [both], [both]
    for step in range(4):
        w_up.append(lax.ppermute(after(w_up[-1], w_down[max(step - 1, 0)]), "z", UP))
        if step < 3:
            w_down.append(lax.ppermute(after(w_down[-1], w_up[step]), "z", DOWN))
    received = lax.all_to_all(after(rows, pieces, w_up[1], w_down[1]), "x", 0, 0, tiled=True)
    received = after(received, w_up[3], w_down[3])
    swapped = lax.ppermute(received, "head", [(i, i ^ 1) for i in range(NH)])
    weights = w_down + w_up[:0:-1]
    partial = pl.pallas_call(
        project_kernel,
        out_shape=jax.ShapeDtypeStruct((NX, SEL, WIDE), f32),
        in_specs=[SMEM] + [ANY] * (NZ + 2),
        out_specs=ANY,
        scratch_shapes=[
            pltpu.VMEM((NZ * 256, WIDE), bf16),
            pltpu.VMEM((NX * SEL, NZ * 256), bf16),
            pltpu.VMEM((NX, SEL, WIDE), f32),
            pltpu.SemaphoreType.DMA((2,)),
        ],
        compiler_params=PARAMS,
        cost_estimate=COST,
    )(head, received, swapped, *weights)
    own = pieces.reshape(NX * 4, PIECE, HEAD)
    up, down = [own], [own]
    for step in range(4):
        before = up[step - 1] if step > 1 else w_up[3]
        down.append(lax.ppermute(after(down[-1], w_down[3], before), "z", DOWN))
        if step < 3:
            before = (down[step], partial) if step else (w_down[3],)
            up.append(lax.ppermute(after(up[-1], w_up[4], *before), "z", UP))
    held = down + up[:0:-1]

    partial = lax.all_to_all(partial, "x", 0, 0, tiled=True)
    past = lax.all_to_all(after(past, partial), "head", 0, 0, tiled=True).reshape(HIST, 2 * HEAD)
    column, inverse = sel.reshape(SEL, 1), jnp.asarray(INVERSE).reshape(1, HEAD)
    queries, fresh_keys, fresh_values = kernel_call(
        queries_kernel,
        [
            jax.ShapeDtypeStruct((QPER * SEL, HEAD), bf16),
            jax.ShapeDtypeStruct((SEL, HEAD), bf16),
            jax.ShapeDtypeStruct((SEL, HEAD), bf16),
        ],
        [hist_len, partial, column, inverse],
        smem=1,
    )

    raw = lax.all_to_all(pick(z, block_lists, held, 0), "x", 0, 0, tiled=True)
    mass = pl.pallas_call(
        weigh_kernel,
        out_shape=jax.ShapeDtypeStruct((QPER * SEL, KEYS), bf16),
        in_specs=[SMEM, VMEM, ANY] + [VMEM] * 5,
        out_specs=ANY,
        scratch_shapes=[
            pltpu.VMEM((CONTEXT, HEAD), bf16),
            pltpu.VMEM((KEYS, HEAD), bf16),
            pltpu.VMEM((1, KEYS), jnp.int32),
            pltpu.VMEM((QPER * SEL, KEYS), f32),
            pltpu.VMEM((QPER * SEL, KEYS), bf16),
            pltpu.SemaphoreType.DMA,
            pltpu.SemaphoreType.DMA,
        ],
        compiler_params=pltpu.CompilerParams(vmem_limit_bytes=56 << 20),
        cost_estimate=FREE,
    )(hist_len, queries, raw.reshape(CONTEXT, HEAD), past, fresh_keys, sel_pos, column, inverse)
    values = lax.all_to_all(pick(z, block_lists, held, 1), "x", 0, 0, tiled=True)
    values = values.reshape(CONTEXT, HEAD)
    mixed = pl.pallas_call(
        mix_kernel,
        out_shape=jax.ShapeDtypeStruct((SEL, QPER * HEAD), bf16),
        in_specs=[ANY] * 4,
        out_specs=VMEM,
        scratch_shapes=[
            pltpu.VMEM((QPER * SEL, KEYS), bf16),
            pltpu.VMEM((KEYS, HEAD), bf16),
            pltpu.SemaphoreType.DMA((QPER + 2,)),
        ],
        compiler_params=PARAMS,
        cost_estimate=FREE,
    )(mass, values, past, fresh_values)
    return mixed[None]


def solution(mesh):
    split = Mesh(mesh.devices.reshape(NZ, NX, NH), ("z", "x", "head"))
    store = ("z", "x")
    in_specs = (
        P(store, None, None),
        P(store, "head"),
        P(store, "head"),
        P(store, None, "head"),
        P(store, "head", None),
        P(),
        P(store, None),
        P(store),
    )
    return jax.shard_map(
        per_device, mesh=split, in_specs=in_specs, out_specs=P(store, None, "head"), check_vma=False
    )
```

time: 169 us -> 147 us (0.87); the launches traced: 168 us -> 145 us
  Pallas kernels: 0 us -> 34 us
  starting transfers between devices: 17.4 us -> 48.9 us
  waiting for transfers between devices: 77.5 us -> 56.4 us
  local copies, waits for them, and re-layouts: 21.4 us -> 4.21 us
  other arithmetic: 15.2 us -> 0 us
  blocking collectives: 13.7 us -> 0 us
  between operations: 14.3 us -> 1.08 us
  matrix products: 8.71 us -> 0 us
    ppermute x0 -> x15, waiting for transfers between devices: none -> 40.3 us  [the longest x4 28.6 us: per_device(): lax.ppermute(after(w_up[-1], w_down[max(step - 1, 0)]), 'z', UP)]
    all_gather x2 -> x0, waiting for transfers between devices: 35.4 us -> none  [the longest x1 35.4 us: per_device(): pieces = lax.all_gather(pieces, 'z', axis=0, tiled=True)]
    pallas_call x0 -> x7, Pallas kernels: none -> 34 us  [the longest x1 12.7 us: per_device(): pl.pallas_call(weigh_kernel, out_shape=jax.ShapeDtypeStruct((QPER * SEL,...]
    all_to_all x4 -> x6, waiting for transfers between devices: 42.1 us -> 16 us  [the longest x1 11.6 us: per_device(): raw = lax.all_to_all(pick(z, block_lists, held, 0), 'x', 0, 0, tiled=True)]
    ppermute x0 -> x15, starting transfers between devices: none -> 24.8 us  [the longest x4 12.2 us: per_device(): down.append(lax.ppermute(after(down[-1], w_down[3], before), 'z', DOWN))]
    all_to_all x1 -> x0, blocking collectives: 13.7 us -> none  [per_device(): pieces = lax.all_to_all(pieces, 'x', 0, 0, tiled=True)]
    dot_general x3 -> x0, matrix products: 8.71 us -> none  [the longest x1 5.45 us: per_device(): jnp.dot(rows.reshape(NX * SEL, NZ * 256), weights, preferred_element_type...]
    all_to_all x4 -> x6, starting transfers between devices: 17.4 us -> 24.1 us  [the longest x1 4.92 us: per_device(): lax.all_to_all(after(past, partial), 'head', 0, 0, tiled=True)]
  transfers between devices with their start and end apart: 6 -> 21, of which waited for: 3 -> 11; matrix products, arithmetic and copies ran while one was open for 18% -> 1% of each run, Pallas kernels for 0% -> 19%
where the time goes in v2:
time: 147 us; the launch traced here: 145 us
  waiting for transfers between devices  56.4 us (38%)
  starting transfers between devices  48.9 us (33%)
  Pallas kernels  34 us (23%)
  local copies, waits for them, and re-layouts  4.21 us (3%)
    ppermute x4, waiting for transfers between devices, per_device(): lax.ppermute(after(w_up[-1], w_down[max(step - 1, 0)]), 'z', UP)  28.6 us
    pallas_call x1, Pallas kernels, per_device(): pl.pallas_call(weigh_kernel, out_shape=jax.ShapeDtypeStruct((QPER * SEL,...  12.7 us
    ppermute x4, starting transfers between devices, per_device(): down.append(lax.ppermute(after(down[-1], w_down[3], before), 'z', DOWN))  12.2 us
    ppermute x3, waiting for transfers between devices, per_device(): up.append(lax.ppermute(after(up[-1], w_up[4], *before), 'z', UP))  11.7 us
    all_to_all x1, waiting for transfers between devices, per_device(): raw = lax.all_to_all(pick(z, block_lists, held, 0), 'x', 0, 0, tiled=True)  11.6 us
    ppermute x3, starting transfers between devices, per_device(): w_down.append(lax.ppermute(after(w_down[-1], w_up[step]), 'z', DOWN))  10.5 us
    pallas_call x2, Pallas kernels, pick(): pl.pallas_call(functools.partial(pick_kernel, kind), out_shape=jax.ShapeD...  6.7 us
    pallas_call x1, Pallas kernels, per_device(): pl.pallas_call(project_kernel, out_shape=jax.ShapeDtypeStruct((NX, SEL, W...  5.27 us
  transfers between devices with their start and end apart: 21, of which 11 were waited for; matrix products, arithmetic and copies ran while one was open for 1% of the time, Pallas kernels for 19%

profile of v2, /device:TPU:8, one launch (start us, length us, event | category | flops | bytes accessed | tf_op | source)
XLA Modules:
  0.0 144.5 jit_solution(5638180595408994756)
XLA Ops:
  0.0 2.6 %shard_map.91 = (bf16[256,768]{1,0:T(8,128)(2,1)}, bf16[4,2,2,128,128]{4,3,2,1,0:T(8,128)(2,1)}, bf16[4,64,2048]{2,1,0:T(8,128)(2,1)}, bf16[8,64,256]{2,1,0:T(8,128)(2,1)}) custom-call(s32[1]{0:T(128)} %bitcast.1.z_ref, s32[1]{0:T(128)} %bitcast.head_ref, bf16[128,8192]{1,0:T(8,128)(2,1)} %bitcast.23, bf16[256,512]{1,0:T(8,128)(2,1)} %w_query.1, ...), custom_call_target="tpu_custom_call" | custom-call | flops 49999998976 | bytes 1048576 | tf_op jit(solution)/shard_map/pallas_call | solution.py:297
  4.6 4.0 %collective-permute-start.1 = (bf16[256,768]{1,0:T(8,128)(2,1)}, bf16[256,768]{1,0:T(8,128)(2,1)S(1)}, u32[]{:S(2)}, u32[]{:S(2)}) collective-permute-start(bf16[256,768]{1,0:T(8,128)(2,1)} %get-tuple-element.31.refs_0_), channel_id=1, source_target_pairs={{0,224},{32,0},{64,32},{96,64},{128,96},{160,128},{192,160},{224,1... | collective-permute-start | bytes 1179656 | tf_op jit(solution)/shard_map/ppermute | solution.py:313
  8.6 4.3 %all-to-all-start = ((bf16[4,2,2,128,128]{4,3,2,1,0:T(8,128)(2,1)}), bf16[4,2,2,128,128]{4,3,2,1,0:T(8,128)(2,1)S(1)}, u32[]{:S(2)}, u32[]{:S(2)}) async-start(bf16[4,2,2,128,128]{4,3,2,1,0:T(8,128)(2,1)} %get-tuple-element.29), calls=%async_computation | async-start | bytes 1048576 | tf_op jit(solution)/shard_map/all_to_all | solution.py:308
  12.9 4.9 %collective-permute-done.refs_7_ = bf16[256,768]{1,0:T(8,128)(2,1)S(1)} collective-permute-done((bf16[256,768]{1,0:T(8,128)(2,1)}, bf16[256,768]{1,0:T(8,128)(2,1)S(1)}, u32[]{:S(2)}, u32[]{:S(2)}) %collective-permute-start) | collective-permute-done | bytes 393248 | tf_op jit(solution)/shard_map/ppermute | solution.py:311
  17.9 3.2 %collective-permute-start.4 = (bf16[256,768]{1,0:T(8,128)(2,1)S(1)}, bf16[256,768]{1,0:T(8,128)(2,1)S(1)}, u32[]{:S(2)}, u32[]{:S(2)}) collective-permute-start(bf16[256,768]{1,0:T(8,128)(2,1)S(1)} %collective-permute-done.1.refs_1_), channel_id=1, source_target_pairs={{0,224},{32,0},{64,32},{96,64},{128,96},{160,128},{192,160},{224,1... | collective-permute-start | bytes 1179656 | tf_op jit(solution)/shard_map/ppermute | solution.py:313
  22.1 3.5 %all-to-all-start.1 = ((bf16[4,64,2048]{2,1,0:T(8,128)(2,1)}), bf16[4,64,2048]{2,1,0:T(8,128)(2,1)S(1)}, u32[]{:S(2)}, u32[]{:S(2)}) async-start(bf16[4,64,2048]{2,1,0:T(8,128)(2,1)} %get-tuple-element.32), calls=%async_computation.1 | async-start | bytes 2097152 | tf_op jit(solution)/shard_map/all_to_all | solution.py:314
  25.6 3.7 %collective-permute-done.2.refs_6_ = bf16[256,768]{1,0:T(8,128)(2,1)S(1)} collective-permute-done((bf16[256,768]{1,0:T(8,128)(2,1)S(1)}, bf16[256,768]{1,0:T(8,128)(2,1)S(1)}, u32[]{:S(2)}, u32[]{:S(2)}) %collective-permute-start.2) | collective-permute-done | bytes 393248 | tf_op jit(solution)/shard_map/ppermute | solution.py:311
  29.4 3.2 %collective-permute-start.5 = (bf16[256,768]{1,0:T(8,128)(2,1)S(1)}, bf16[256,768]{1,0:T(8,128)(2,1)}, u32[]{:S(2)}, u32[]{:S(2)}) collective-permute-start(bf16[256,768]{1,0:T(8,128)(2,1)S(1)} %collective-permute-done.4.refs_2_), channel_id=1, source_target_pairs={{0,224},{32,0},{64,32},{96,64},{128,96},{160,128},{192,160},{224,1... | collective-permute-start | bytes 1179656 | tf_op jit(solution)/shard_map/ppermute | solution.py:313
  32.6 7.3 %collective-permute-done.3.refs_5_ = bf16[256,768]{1,0:T(8,128)(2,1)S(1)} collective-permute-done((bf16[256,768]{1,0:T(8,128)(2,1)S(1)}, bf16[256,768]{1,0:T(8,128)(2,1)S(1)}, u32[]{:S(2)}, u32[]{:S(2)}) %collective-permute-start.3) | collective-permute-done | bytes 393248 | tf_op jit(solution)/shard_map/ppermute | solution.py:311
  43.1 12.6 %collective-permute-done.7.refs_4_ = bf16[256,768]{1,0:T(8,128)(2,1)S(1)} collective-permute-done((bf16[256,768]{1,0:T(8,128)(2,1)}, bf16[256,768]{1,0:T(8,128)(2,1)S(1)}, u32[]{:S(2)}, u32[]{:S(2)}) %collective-permute-start.7) | collective-permute-done | bytes 393248 | tf_op jit(solution)/shard_map/ppermute | solution.py:311
  55.7 3.2 %collective-permute-start.9 = (bf16[16,128,128]{2,1,0:T(8,128)(2,1)S(1)}, bf16[16,128,128]{2,1,0:T(8,128)(2,1)}, u32[]{:S(2)}, u32[]{:S(2)}) collective-permute-start(bf16[16,128,128]{2,1,0:T(8,128)(2,1)S(1)} %collective-permute-done.8.refs_1_), channel_id=1, source_target_pairs={{0,224},{32,0},{64,32},{96,64},{128,96},{160,128},{192,160},{224,1... | collective-permute-start | bytes 1572872 | tf_op jit(solution)/shard_map/ppermute | solution.py:336
  60.0 5.3 %shard_map.92 = f32[4,128,768]{2,1,0:T(8,128)} custom-call(s32[1]{0:T(128)} %bitcast.head_ref, bf16[4,64,2048]{2,1,0:T(8,128)(2,1)} %copy-done.9, bf16[4,64,2048]{2,1,0:T(8,128)(2,1)} %copy-done.12, bf16[256,768]{1,0:T(8,128)(2,1)} %get-tuple-element.31.refs_0_, bf16[256,768]{1,0:T(8,128)(2,1)} %copy-done.14, bf16[256,768]{1,0:T(8,128)(2,1)} %copy-done.16, ...), custom_call_target="tpu_custom_call" | custom-call | flops 49999998976 | bytes 1048576 | tf_op jit(solution)/shard_map/pallas_call | solution.py:318
  65.3 4.3 %all-to-all-start.2 = ((f32[4,128,768]{2,1,0:T(8,128)}), f32[4,128,768]{2,1,0:T(8,128)S(1)}, u32[]{:S(2)}, u32[]{:S(2)}) async-start(f32[4,128,768]{2,1,0:T(8,128)} %shard_map.92), calls=%async_computation.2 | async-start | bytes 3145728 | tf_op jit(solution)/shard_map/all_to_all | solution.py:342
  70.1 3.3 %collective-permute-start.11 = (bf16[16,128,128]{2,1,0:T(8,128)(2,1)}, bf16[16,128,128]{2,1,0:T(8,128)(2,1)S(1)}, u32[]{:S(2)}, u32[]{:S(2)}) collective-permute-start(bf16[16,128,128]{2,1,0:T(8,128)(2,1)} %collective-permute-done.9.refs_2_), channel_id=1, source_target_pairs={{0,224},{32,0},{64,32},{96,64},{128,96},{160,128},{192,160},{224,1... | collective-permute-start | bytes 1572872 | tf_op jit(solution)/shard_map/ppermute | solution.py:336
  73.4 10.1 %collective-permute-done.12.refs_6_ = bf16[16,128,128]{2,1,0:T(8,128)(2,1)S(1)} collective-permute-done((bf16[16,128,128]{2,1,0:T(8,128)(2,1)S(1)}, bf16[16,128,128]{2,1,0:T(8,128)(2,1)S(1)}, u32[]{:S(2)}, u32[]{:S(2)}) %collective-permute-start.12) | collective-permute-done | bytes 524320 | tf_op jit(solution)/shard_map/ppermute | solution.py:339
  83.5 3.4 %collective-permute-start.13 = (bf16[16,128,128]{2,1,0:T(8,128)(2,1)S(1)}, bf16[16,128,128]{2,1,0:T(8,128)(2,1)}, u32[]{:S(2)}, u32[]{:S(2)}) collective-permute-start(bf16[16,128,128]{2,1,0:T(8,128)(2,1)S(1)} %collective-permute-done.11.refs_3_), channel_id=1, source_target_pairs={{0,224},{32,0},{64,32},{96,64},{128,96},{160,128},{192,160},{224,1... | collective-permute-start | bytes 1572872 | tf_op jit(solution)/shard_map/ppermute | solution.py:336
  89.5 4.9 %all-to-all-start.4 = ((bf16[8,64,256]{2,1,0:T(8,128)(2,1)}), bf16[8,64,256]{2,1,0:T(8,128)(2,1)S(1)}, u32[]{:S(2)}, u32[]{:S(2)}) async-start(bf16[8,64,256]{2,1,0:T(8,128)(2,1)} %get-tuple-element.48), calls=%async_computation.4 | async-start | bytes 524288 | tf_op jit(solution)/shard_map/all_to_all | solution.py:343
  96.2 3.3 %shard_map.94 = bf16[32,128,128]{2,1,0:T(8,128)(2,1)} custom-call(s32[1]{0:T(128)} %bitcast.1.z_ref, s32[32,8]{1,0:T(8,128)} %copy.11.lists_ref, bf16[16,128,128]{2,1,0:T(8,128)(2,1)} %bitcast.14, bf16[16,128,128]{2,1,0:T(8,128)(2,1)} %copy-done.5, bf16[16,128,128]{2,1,0:T(8,128)(2,1)} %collective-permute-done.9.refs_2_, bf16[16,128,128]{2,1,0:T(8,128)(2,1)} %copy-done.8, ...), custom_call_target="tpu_custom_call" | custom-call | tf_op jit(solution)/shard_map/pallas_call | solution.py:154
  100.5 3.5 %all-to-all-start.3 = ((bf16[4,8,128,128]{3,2,1,0:T(8,128)(2,1)}), bf16[4,8,128,128]{3,2,1,0:T(8,128)(2,1)S(1)}, u32[]{:S(2)}, u32[]{:S(2)}) async-start(bf16[4,8,128,128]{3,2,1,0:T(8,128)(2,1)} %bitcast.19), calls=%async_computation.3 | async-start | bytes 2097152 | tf_op jit(solution)/shard_map/all_to_all | solution.py:356
  104.0 3.4 %shard_map.96 = bf16[32,128,128]{2,1,0:T(8,128)(2,1)} custom-call(s32[1]{0:T(128)} %bitcast.1.z_ref, s32[32,8]{1,0:T(8,128)} %copy.11.lists_ref, bf16[16,128,128]{2,1,0:T(8,128)(2,1)} %bitcast.15, bf16[16,128,128]{2,1,0:T(8,128)(2,1)} %copy-done.5, bf16[16,128,128]{2,1,0:T(8,128)(2,1)} %collective-permute-done.9.refs_2_, bf16[16,128,128]{2,1,0:T(8,128)(2,1)} %copy-done.8, ...), custom_call_target="tpu_custom_call" | custom-call | tf_op jit(solution)/shard_map/pallas_call | solution.py:154
  107.4 11.6 %all-to-all-done.3 = bf16[4,8,128,128]{3,2,1,0:T(8,128)(2,1)S(1)} async-done(((bf16[4,8,128,128]{3,2,1,0:T(8,128)(2,1)}), bf16[4,8,128,128]{3,2,1,0:T(8,128)(2,1)S(1)}, u32[]{:S(2)}, u32[]{:S(2)}) %all-to-all-start.3) | async-done | bytes 1048608 | tf_op jit(solution)/shard_map/all_to_all | solution.py:356
  119.0 3.5 %all-to-all-start.5 = ((bf16[4,8,128,128]{3,2,1,0:T(8,128)(2,1)}), bf16[4,8,128,128]{3,2,1,0:T(8,128)(2,1)S(1)}, u32[]{:S(2)}, u32[]{:S(2)}) async-start(bf16[4,8,128,128]{3,2,1,0:T(8,128)(2,1)} %bitcast.17), calls=%async_computation.5 | async-start | bytes 2097152 | tf_op jit(solution)/shard_map/all_to_all | solution.py:374
  126.3 12.7 %shard_map.95.mass_ref = bf16[512,4736]{1,0:T(8,128)(2,1)} custom-call(s32[1]{0:T(128)S(6)} %copy.14.length_ref, bf16[512,128]{1,0:T(8,128)(2,1)} %get-tuple-element.39.query_ref, bf16[4096,128]{1,0:T(8,128)(2,1)} %bitcast.16, bf16[512,256]{1,0:T(8,128)(2,1)} %bitcast.20, bf16[128,128]{1,0:T(8,128)(2,1)} %get-tuple-element.49.fresh_ref, s32[1,128]{1,0:T(1,128)} %row_ref.1, ...), custom_call_target="tpu_custom_call" | custom-call | tf_op jit(solution)/shard_map/pallas_call | solution.py:357
  140.0 4.4 %shard_map.97 = bf16[128,512]{1,0:T(8,128)(2,1)} custom-call(bf16[512,4736]{1,0:T(8,128)(2,1)} %shard_map.95.mass_ref, bf16[4096,128]{1,0:T(8,128)(2,1)} %bitcast.18, bf16[512,256]{1,0:T(8,128)(2,1)} %bitcast.21, bf16[128,128]{1,0:T(8,128)(2,1)} %get-tuple-element.50.fresh_ref), custom_call_target="tpu_custom_call" | custom-call | tf_op jit(solution)/shard_map/pallas_call | solution.py:376
  (65 shorter events, 17.0 us)
Async XLA Ops:
  2.6 15.3 %collective-permute-start = (bf16[256,768]{1,0:T(8,128)(2,1)}, bf16[256,768]{1,0:T(8,128)(2,1)S(1)}, u32[]{:S(2)}, u32[]{:S(2)}) collective-permute-start(bf16[256,768]{1,0:T(8,128)(2,1)} %get-tuple-element.31.refs_0_), channel_id=1, source_target_pairs={{0,32},{32,64},{64,96},{96,128},{128,160},{160,192},{192,224},{224... | collective-permute-start | bytes 1179656 | tf_op jit(solution)/shard_map/ppermute | solution.py:311
  4.6 13.3 %collective-permute-start.1 = (bf16[256,768]{1,0:T(8,128)(2,1)}, bf16[256,768]{1,0:T(8,128)(2,1)S(1)}, u32[]{:S(2)}, u32[]{:S(2)}) collective-permute-start(bf16[256,768]{1,0:T(8,128)(2,1)} %get-tuple-element.31.refs_0_), channel_id=1, source_target_pairs={{0,224},{32,0},{64,32},{96,64},{128,96},{160,128},{192,160},{224,1... | collective-permute-start | bytes 1179656 | tf_op jit(solution)/shard_map/ppermute | solution.py:313
  8.6 13.5 %all-to-all-start = ((bf16[4,2,2,128,128]{4,3,2,1,0:T(8,128)(2,1)}), bf16[4,2,2,128,128]{4,3,2,1,0:T(8,128)(2,1)S(1)}, u32[]{:S(2)}, u32[]{:S(2)}) async-start(bf16[4,2,2,128,128]{4,3,2,1,0:T(8,128)(2,1)} %get-tuple-element.29), calls=%async_computation | async-start | bytes 1048576 | tf_op jit(solution)/shard_map/all_to_all | solution.py:308
  17.8 41.1 %copy-start.13 = (bf16[256,768]{1,0:T(8,128)(2,1)}, bf16[256,768]{1,0:T(8,128)(2,1)S(1)}, u32[]{:S(2)}) copy-start(bf16[256,768]{1,0:T(8,128)(2,1)S(1)} %collective-permute-done.refs_7_) | copy-start | bytes 1179652
  17.8 11.5 %collective-permute-start.2 = (bf16[256,768]{1,0:T(8,128)(2,1)S(1)}, bf16[256,768]{1,0:T(8,128)(2,1)S(1)}, u32[]{:S(2)}, u32[]{:S(2)}) collective-permute-start(bf16[256,768]{1,0:T(8,128)(2,1)S(1)} %collective-permute-done.refs_7_), channel_id=1, source_target_pairs={{0,32},{32,64},{64,96},{96,128},{128,160},{160,192},{192,224},{224... | collective-permute-start | bytes 1179656 | tf_op jit(solution)/shard_map/ppermute | solution.py:311
  17.9 41.1 %copy-start.14 = (bf16[256,768]{1,0:T(8,128)(2,1)}, bf16[256,768]{1,0:T(8,128)(2,1)S(1)}, u32[]{:S(2)}) copy-start(bf16[256,768]{1,0:T(8,128)(2,1)S(1)} %collective-permute-done.1.refs_1_) | copy-start | bytes 1179652
  17.9 11.5 %collective-permute-start.4 = (bf16[256,768]{1,0:T(8,128)(2,1)S(1)}, bf16[256,768]{1,0:T(8,128)(2,1)S(1)}, u32[]{:S(2)}, u32[]{:S(2)}) collective-permute-start(bf16[256,768]{1,0:T(8,128)(2,1)S(1)} %collective-permute-done.1.refs_1_), channel_id=1, source_target_pairs={{0,224},{32,0},{64,32},{96,64},{128,96},{160,128},{192,160},{224,1... | collective-permute-start | bytes 1179656 | tf_op jit(solution)/shard_map/ppermute | solution.py:313
  22.1 43.2 %copy-start.1 = (bf16[4,2,2,128,128]{4,3,2,1,0:T(8,128)(2,1)}, bf16[4,2,2,128,128]{4,3,2,1,0:T(8,128)(2,1)S(1)}, u32[]{:S(2)}) copy-start(bf16[4,2,2,128,128]{4,3,2,1,0:T(8,128)(2,1)S(1)} %all-to-all-done) | copy-start | bytes 1572868
  22.1 18.6 %all-to-all-start.1 = ((bf16[4,64,2048]{2,1,0:T(8,128)(2,1)}), bf16[4,64,2048]{2,1,0:T(8,128)(2,1)S(1)}, u32[]{:S(2)}, u32[]{:S(2)}) async-start(bf16[4,64,2048]{2,1,0:T(8,128)(2,1)} %get-tuple-element.32), calls=%async_computation.1 | async-start | bytes 2097152 | tf_op jit(solution)/shard_map/all_to_all | solution.py:314
  29.4 10.6 %collective-permute-start.3 = (bf16[256,768]{1,0:T(8,128)(2,1)S(1)}, bf16[256,768]{1,0:T(8,128)(2,1)S(1)}, u32[]{:S(2)}, u32[]{:S(2)}) collective-permute-start(bf16[256,768]{1,0:T(8,128)(2,1)S(1)} %collective-permute-done.2.refs_6_), channel_id=1, source_target_pairs={{0,32},{32,64},{64,96},{96,128},{128,160},{160,192},{192,224},{224... | collective-permute-start | bytes 1179656 | tf_op jit(solution)/shard_map/ppermute | solution.py:311
  29.4 11.3 %collective-permute-start.5 = (bf16[256,768]{1,0:T(8,128)(2,1)S(1)}, bf16[256,768]{1,0:T(8,128)(2,1)}, u32[]{:S(2)}, u32[]{:S(2)}) collective-permute-start(bf16[256,768]{1,0:T(8,128)(2,1)S(1)} %collective-permute-done.4.refs_2_), channel_id=1, source_target_pairs={{0,224},{32,0},{64,32},{96,64},{128,96},{160,128},{192,160},{224,1... | collective-permute-start | bytes 1179656 | tf_op jit(solution)/shard_map/ppermute | solution.py:313
  40.7 18.2 %collective-permute-start.6 = (bf16[4,64,2048]{2,1,0:T(8,128)(2,1)S(1)}, bf16[4,64,2048]{2,1,0:T(8,128)(2,1)S(1)}, u32[]{:S(2)}, u32[]{:S(2)}) collective-permute-start(bf16[4,64,2048]{2,1,0:T(8,128)(2,1)S(1)} %all-to-all-done.1.received), channel_id=1, source_target_pairs={{0,1},{1,0},{2,3},{3,2},{4,5},{5,4},{6,7},{7,6},{8,9},{9,8},{10,11... | collective-permute-start | bytes 3145736 | tf_op jit(solution)/shard_map/ppermute | solution.py:316
  40.8 14.9 %collective-permute-start.8 = (bf16[16,128,128]{2,1,0:T(8,128)(2,1)S(1)}, bf16[16,128,128]{2,1,0:T(8,128)(2,1)S(1)}, u32[]{:S(2)}, u32[]{:S(2)}) collective-permute-start(bf16[16,128,128]{2,1,0:T(8,128)(2,1)S(1)} %bitcast.12), channel_id=1, source_target_pairs={{0,224},{32,0},{64,32},{96,64},{128,96},{160,128},{192,160},{224,1... | collective-permute-start | bytes 1572872 | tf_op jit(solution)/shard_map/ppermute | solution.py:336
  43.1 12.6 %collective-permute-start.7 = (bf16[256,768]{1,0:T(8,128)(2,1)}, bf16[256,768]{1,0:T(8,128)(2,1)S(1)}, u32[]{:S(2)}, u32[]{:S(2)}) collective-permute-start(bf16[256,768]{1,0:T(8,128)(2,1)} %copy-done.17), channel_id=1, source_target_pairs={{0,32},{32,64},{64,96},{96,128},{128,160},{160,192},{192,224},{224... | collective-permute-start | bytes 1179656 | tf_op jit(solution)/shard_map/ppermute | solution.py:311
  55.7 14.4 %collective-permute-start.10 = (bf16[16,128,128]{2,1,0:T(8,128)(2,1)S(1)}, bf16[16,128,128]{2,1,0:T(8,128)(2,1)S(1)}, u32[]{:S(2)}, u32[]{:S(2)}) collective-permute-start(bf16[16,128,128]{2,1,0:T(8,128)(2,1)S(1)} %bitcast.13), channel_id=1, source_target_pairs={{0,32},{32,64},{64,96},{96,128},{128,160},{160,192},{192,224},{224... | collective-permute-start | bytes 1572872 | tf_op jit(solution)/shard_map/ppermute | solution.py:339
  55.7 14.4 %collective-permute-start.9 = (bf16[16,128,128]{2,1,0:T(8,128)(2,1)S(1)}, bf16[16,128,128]{2,1,0:T(8,128)(2,1)}, u32[]{:S(2)}, u32[]{:S(2)}) collective-permute-start(bf16[16,128,128]{2,1,0:T(8,128)(2,1)S(1)} %collective-permute-done.8.refs_1_), channel_id=1, source_target_pairs={{0,224},{32,0},{64,32},{96,64},{128,96},{160,128},{192,160},{224,1... | collective-permute-start | bytes 1572872 | tf_op jit(solution)/shard_map/ppermute | solution.py:336
  65.3 24.2 %all-to-all-start.2 = ((f32[4,128,768]{2,1,0:T(8,128)}), f32[4,128,768]{2,1,0:T(8,128)S(1)}, u32[]{:S(2)}, u32[]{:S(2)}) async-start(f32[4,128,768]{2,1,0:T(8,128)} %shard_map.92), calls=%async_computation.2 | async-start | bytes 3145728 | tf_op jit(solution)/shard_map/all_to_all | solution.py:342
  70.1 13.4 %collective-permute-start.12 = (bf16[16,128,128]{2,1,0:T(8,128)(2,1)S(1)}, bf16[16,128,128]{2,1,0:T(8,128)(2,1)S(1)}, u32[]{:S(2)}, u32[]{:S(2)}) collective-permute-start(bf16[16,128,128]{2,1,0:T(8,128)(2,1)S(1)} %collective-permute-done.10.refs_7_), channel_id=1, source_target_pairs={{0,32},{32,64},{64,96},{96,128},{128,160},{160,192},{192,224},{224... | collective-permute-start | bytes 1572872 | tf_op jit(solution)/shard_map/ppermute | solution.py:339
  70.1 13.4 %collective-permute-start.11 = (bf16[16,128,128]{2,1,0:T(8,128)(2,1)}, bf16[16,128,128]{2,1,0:T(8,128)(2,1)S(1)}, u32[]{:S(2)}, u32[]{:S(2)}) collective-permute-start(bf16[16,128,128]{2,1,0:T(8,128)(2,1)} %collective-permute-done.9.refs_2_), channel_id=1, source_target_pairs={{0,224},{32,0},{64,32},{96,64},{128,96},{160,128},{192,160},{224,1... | collective-permute-start | bytes 1572872 | tf_op jit(solution)/shard_map/ppermute | solution.py:336
  83.5 12.6 %collective-permute-start.14 = (bf16[16,128,128]{2,1,0:T(8,128)(2,1)S(1)}, bf16[16,128,128]{2,1,0:T(8,128)(2,1)}, u32[]{:S(2)}, u32[]{:S(2)}) collective-permute-start(bf16[16,128,128]{2,1,0:T(8,128)(2,1)S(1)} %collective-permute-done.12.refs_6_), channel_id=1, source_target_pairs={{0,32},{32,64},{64,96},{96,128},{128,160},{160,192},{192,224},{224... | collective-permute-start | bytes 1572872 | tf_op jit(solution)/shard_map/ppermute | solution.py:339
  83.5 12.6 %collective-permute-start.13 = (bf16[16,128,128]{2,1,0:T(8,128)(2,1)S(1)}, bf16[16,128,128]{2,1,0:T(8,128)(2,1)}, u32[]{:S(2)}, u32[]{:S(2)}) collective-permute-start(bf16[16,128,128]{2,1,0:T(8,128)(2,1)S(1)} %collective-permute-done.11.refs_3_), channel_id=1, source_target_pairs={{0,224},{32,0},{64,32},{96,64},{128,96},{160,128},{192,160},{224,1... | collective-permute-start | bytes 1572872 | tf_op jit(solution)/shard_map/ppermute | solution.py:336
  89.5 11.0 %all-to-all-start.4 = ((bf16[8,64,256]{2,1,0:T(8,128)(2,1)}), bf16[8,64,256]{2,1,0:T(8,128)(2,1)S(1)}, u32[]{:S(2)}, u32[]{:S(2)}) async-start(bf16[8,64,256]{2,1,0:T(8,128)(2,1)} %get-tuple-element.48), calls=%async_computation.4 | async-start | bytes 524288 | tf_op jit(solution)/shard_map/all_to_all | solution.py:343
  100.5 18.5 %all-to-all-start.3 = ((bf16[4,8,128,128]{3,2,1,0:T(8,128)(2,1)}), bf16[4,8,128,128]{3,2,1,0:T(8,128)(2,1)S(1)}, u32[]{:S(2)}, u32[]{:S(2)}) async-start(bf16[4,8,128,128]{3,2,1,0:T(8,128)(2,1)} %bitcast.19), calls=%async_computation.3 | async-start | bytes 2097152 | tf_op jit(solution)/shard_map/all_to_all | solution.py:356
  119.0 20.0 %all-to-all-start.5 = ((bf16[4,8,128,128]{3,2,1,0:T(8,128)(2,1)}), bf16[4,8,128,128]{3,2,1,0:T(8,128)(2,1)S(1)}, u32[]{:S(2)}, u32[]{:S(2)}) async-start(bf16[4,8,128,128]{3,2,1,0:T(8,128)(2,1)} %bitcast.17), calls=%async_computation.5 | async-start | bytes 2097152 | tf_op jit(solution)/shard_map/all_to_all | solution.py:374
  (16 other events, 178.9 us)

commit v3 on v2

--- a/solution.py
+++ b/solution.py
@@ -13,6 +13,7 @@
 SEL, HEAD, QPER, BLOCK, RET, HIST = 128, 128, 4, 512, 8, 512
 CONTEXT = RET * BLOCK
 PIECE = BLOCK // NX
+STEP = 4 * PIECE
 WIDE = (QPER + 2) * HEAD
 FAR = 1 << 20
 FREE = pl.CostEstimate(flops=0, bytes_accessed=0, transcendentals=0)
@@ -25,8 +26,12 @@
 DOWN = [(i, (i - 1) % NZ) for i in range(NZ)]
 SMEM = pl.BlockSpec(memory_space=pltpu.SMEM)
 VMEM = pl.BlockSpec(memory_space=pltpu.VMEM)
-ANY = pl.BlockSpec(memory_space=pltpu.HBM)
-PARAMS = pltpu.CompilerParams(vmem_limit_bytes=56 << 20)
+HBM = pl.BlockSpec(memory_space=pltpu.HBM)
+ANY = pl.BlockSpec(memory_space=pl.ANY)
+
+
+def grant(mebibytes):
+    return pltpu.CompilerParams(vmem_limit_bytes=mebibytes << 20)
 
 
 def kernel_call(body, out, inputs, smem=0, scratch=()):
@@ -37,7 +42,7 @@
         in_specs=[SMEM] * smem + [VMEM] * (len(inputs) - smem),
         out_specs=[VMEM] * len(out) if many else VMEM,
         scratch_shapes=scratch,
-        compiler_params=PARAMS,
+        compiler_params=grant(16),
         cost_estimate=FREE,
     )(*inputs)
 
@@ -140,7 +145,7 @@
         leaf(at, ((block >> 3) - z) & (NZ - 1), inner, 0, NZ)
         return 0
 
-    lax.fori_loop(0, NX * RET, one, 0, unroll=4)
+    lax.fori_loop(0, NX * RET, one, 0, unroll=8)
     stores = []
     for x in range(NX):
         pltpu.make_async_copy(held.at[part(x)], held.at[part(x)], sems.at[x]).wait()
@@ -154,13 +159,13 @@
     out = pl.pallas_call(
         functools.partial(pick_kernel, kind),
         out_shape=jax.ShapeDtypeStruct((NX * RET, PIECE, HEAD), jnp.bfloat16),
-        in_specs=[SMEM, SMEM] + [ANY] * NZ,
-        out_specs=ANY,
+        in_specs=[SMEM, SMEM] + [HBM] * NZ,
+        out_specs=HBM,
         scratch_shapes=[
             pltpu.VMEM((NX * RET, PIECE, HEAD), jnp.bfloat16),
             pltpu.SemaphoreType.DMA((2 * NX,)),
         ],
-        compiler_params=PARAMS,
+        compiler_params=grant(56),
         cost_estimate=FREE,
     )(z, block_lists, *sources)
     return out.reshape(NX, RET, PIECE, HEAD)
@@ -209,45 +214,69 @@
             value_ref[...] = total.astype(jnp.bfloat16)
 
 
-def weigh_kernel(
-    length_ref, query_ref, raw_ref, past_ref, fresh_ref, row_ref, column_ref, inverse_ref,
-    out, raw, keys, place, scores, mass, sem, out_sem,
+def tables_kernel(
+    length_ref, row_ref, column_ref, inverse_ref, out, place_ref, tables, sems
 ):
-    fetch = pltpu.make_async_copy(raw_ref, raw, sem)
-    fetch.start()
     length, inverse, column = length_ref[0], inverse_ref[...], column_ref[...]
     slots = lax.broadcasted_iota(jnp.int32, (1, HIST), 1)
-    place[:, :HIST] = jnp.where(slots < length, -1, FAR)
-    place[:, HIST + CONTEXT :] = row_ref[...]
+    place_ref[:, :HIST] = jnp.where(slots < length, -1, FAR)
+    place_ref[:, HIST + CONTEXT :] = row_ref[...]
+
+    def sending(step):
+        some = pl.ds(pl.multiple_of(step * STEP, STEP), STEP)
+        return pltpu.make_async_copy(tables.at[:, some], out.at[:, some], sems.at[step])
+
+    def one(step, _):
+        rows = lax.broadcasted_iota(jnp.int32, (STEP, 1), 0)
+        base = (step & 1) * (4 * BLOCK) + (step >> 1) * PIECE
+        rows = base + (rows >> 7) * BLOCK + (rows & 127)
+        at = pl.multiple_of(step * STEP, STEP)
+        some = pl.ds(at, STEP)
+        tables[0, some], tables[1, some] = waves(rows + length, inverse)
+        sending(step).start()
+        here = lax.broadcasted_iota(jnp.int32, (1, STEP), 1)
+        here = base + (here >> 7) * BLOCK + (here & 127)
+        hits = jnp.max(jnp.where(column == here, 1, 0), axis=0, keepdims=True)
+        place_ref[:, pl.ds(at + HIST, STEP)] = jnp.where(hits > 0, FAR, here)
+        return 0
+
+    lax.fori_loop(0, CONTEXT // STEP, one, 0)
+    for step in range(CONTEXT // STEP):
+        sending(step).wait()
+
+
+def weigh_kernel(
+    query_ref, raw_ref, tables_ref, place_ref, past_ref, fresh_ref, column_ref,
+    out, tables, keys, scores, mass, sems, sem,
+):
+    def fetching(step):
+        some = pl.ds(pl.multiple_of(step * STEP, STEP), STEP)
+        return pltpu.make_async_copy(tables_ref.at[:, some], tables.at[:, some], sems.at[step])
+
+    for step in range(CONTEXT // STEP):
+        fetching(step).start()
     keys[:HIST] = past_ref[:, :HEAD]
     keys[HIST + CONTEXT :] = fresh_ref[...]
-    fetch.wait()
 
     def rotate(step, _):
-        rows = lax.broadcasted_iota(jnp.int32, (4 * PIECE, 1), 0)
-        base = (step & 1) * (4 * BLOCK) + (step >> 1) * PIECE
-        rows = base + (rows >> 7) * BLOCK + (rows & 127)
-        at = pl.multiple_of(step * (4 * PIECE), 4 * PIECE)
-        cosine, sine = waves(rows + length, inverse)
-        key = turn(raw[pl.ds(at, 4 * PIECE)].astype(jnp.float32), cosine, sine)
-        keys[pl.ds(at + HIST, 4 * PIECE)] = key.astype(jnp.bfloat16)
-        here = lax.broadcasted_iota(jnp.int32, (1, 4 * PIECE), 1)
-        here = base + (here >> 7) * BLOCK + (here & 127)
-        hits = jnp.max(jnp.where(column == here, 1, 0), axis=0, keepdims=True)
-        place[:, pl.ds(at + HIST, 4 * PIECE)] = jnp.where(hits > 0, FAR, here)
+        at = pl.multiple_of(step * STEP, STEP)
+        some = pl.ds(at, STEP)
+        fetching(step).wait()
+        key = turn(raw_ref[some].astype(jnp.float32), tables[0, some], tables[1, some])
+        keys[pl.ds(at + HIST, STEP)] = key.astype(jnp.bfloat16)
         return 0
 
-    lax.fori_loop(0, CONTEXT // (4 * PIECE), rotate, 0)
+    lax.fori_loop(0, CONTEXT // STEP, rotate, 0)
     scores[...] = lax.dot_general(
         query_ref[...], keys[...], (((1,), (1,)), ((), ())), preferred_element_type=jnp.float32
     ) * np.float32(HEAD**-0.5)
 
     def sending(at):
-        return pltpu.make_async_copy(mass.at[pl.ds(at, SEL)], out.at[pl.ds(at, SEL)], out_sem)
+        return pltpu.make_async_copy(mass.at[pl.ds(at, SEL)], out.at[pl.ds(at, SEL)], sem)
 
     def soften(step, _):
         at = pl.multiple_of(step * SEL, SEL)
-        part = jnp.where(place[...] <= column, scores[pl.ds(at, SEL)], -jnp.inf)
+        part = jnp.where(place_ref[...] <= column_ref[...], scores[pl.ds(at, SEL)], -jnp.inf)
         part = jnp.exp(part - jnp.max(part, axis=1, keepdims=True))
         part = part * (1.0 / jnp.sum(part, axis=1, keepdims=True))
         mass[pl.ds(at, SEL)] = part.astype(jnp.bfloat16)
@@ -259,37 +288,19 @@
         sending(head * SEL).wait()
 
 
-def mix_kernel(mass_ref, value_ref, past_ref, fresh_ref, out_ref, mass, values, sems):
-    fetches = [pltpu.make_async_copy(value_ref, values.at[pl.ds(HIST, CONTEXT)], sems.at[QPER])]
-    early = [
-        pltpu.make_async_copy(past_ref.at[:, HEAD:], values.at[pl.ds(0, HIST)], sems.at[QPER + 1]),
-        pltpu.make_async_copy(
-            fresh_ref, values.at[pl.ds(HIST + CONTEXT, SEL)], sems.at[QPER + 1]
-        ),
-    ]
-    for fetch in early:
-        fetch.start()
+def mix_kernel(mass_ref, value_ref, past_ref, fresh_ref, out_ref):
+    late = HIST + CONTEXT
+    mixed = jnp.dot(mass_ref[:, :HIST], past_ref[:, HEAD:], preferred_element_type=jnp.float32)
+    mixed += jnp.dot(mass_ref[:, late:], fresh_ref[...], preferred_element_type=jnp.float32)
+    mixed += jnp.dot(mass_ref[:, HIST:late], value_ref[...], preferred_element_type=jnp.float32)
     for head in range(QPER):
-        rows = pl.ds(head * SEL, SEL)
-        fetches.append(pltpu.make_async_copy(mass_ref.at[rows], mass.at[rows], sems.at[head]))
-    for fetch in fetches:
-        fetch.start()
-    for fetch in early:
-        fetch.wait()
-    fetches[0].wait()
-    for pair in range(0, QPER, 2):
-        fetches[pair + 1].wait()
-        fetches[pair + 2].wait()
-        part = mass[pair * SEL : (pair + 2) * SEL]
-        mixed = jnp.dot(part, values[...], preferred_element_type=jnp.float32)
-        for head in range(2):
-            at = (pair + head) * HEAD
-            out_ref[:, at : at + HEAD] = mixed[head * SEL : (head + 1) * SEL].astype(jnp.bfloat16)
+        part = mixed[head * SEL : (head + 1) * SEL]
+        out_ref[:, head * HEAD : (head + 1) * HEAD] = part.astype(jnp.bfloat16)
 
 
 def per_device(hidden, w_query, w_key_value, block_kv, history_kv, block_lists, sel_pos, hist_len):
     z = lax.axis_index("z").reshape(1)
-    sel = sel_pos[0]
+    column, inverse = sel_pos[0].reshape(SEL, 1), jnp.asarray(INVERSE).reshape(1, HEAD)
     bf16, f32 = jnp.bfloat16, jnp.float32
 
     head = lax.axis_index("head").reshape(1)
@@ -297,11 +308,11 @@
     both, pieces, rows, past = pl.pallas_call(
         prepare_kernel,
         out_shape=[jax.ShapeDtypeStruct(shape, bf16) for shape in shapes],
-        in_specs=[SMEM] * 2 + [ANY] * 5,
-        out_specs=[ANY] * 4,
+        in_specs=[SMEM] * 2 + [HBM] * 5,
+        out_specs=[HBM] * 4,
         scratch_shapes=[pltpu.VMEM(shape, bf16) for shape in shapes]
         + [pltpu.SemaphoreType.DMA((8,))],
-        compiler_params=PARAMS,
+        compiler_params=grant(56),
         cost_estimate=COST,
     )(z, head, hidden[0], w_query, w_key_value, block_kv, history_kv[0])
 
@@ -312,36 +323,52 @@
         if step < 3:
             w_down.append(lax.ppermute(after(w_down[-1], w_up[step]), "z", DOWN))
     received = lax.all_to_all(after(rows, pieces, w_up[1], w_down[1]), "x", 0, 0, tiled=True)
+    past = lax.all_to_all(after(past, received), "head", 0, 0, tiled=True).reshape(HIST, 2 * HEAD)
     received = after(received, w_up[3], w_down[3])
     swapped = lax.ppermute(received, "head", [(i, i ^ 1) for i in range(NH)])
     weights = w_down + w_up[:0:-1]
+    own = pieces.reshape(NX * 4, PIECE, HEAD)
+    up, down = [own], [own]
+    for step in range(2):
+        down.append(lax.ppermute(after(down[-1], w_down[3], w_up[3]), "z", DOWN))
+        if step == 0:
+            up.append(lax.ppermute(after(up[-1], w_up[4], w_down[3], past), "z", UP))
+
     partial = pl.pallas_call(
         project_kernel,
         out_shape=jax.ShapeDtypeStruct((NX, SEL, WIDE), f32),
-        in_specs=[SMEM] + [ANY] * (NZ + 2),
-        out_specs=ANY,
+        in_specs=[SMEM] + [ANY] * 2 + [HBM] * NZ,
+        out_specs=HBM,
         scratch_shapes=[
             pltpu.VMEM((NZ * 256, WIDE), bf16),
             pltpu.VMEM((NX * SEL, NZ * 256), bf16),
             pltpu.VMEM((NX, SEL, WIDE), f32),
             pltpu.SemaphoreType.DMA((2,)),
         ],
-        compiler_params=PARAMS,
+        compiler_params=grant(56),
         cost_estimate=COST,
-    )(head, received, swapped, *weights)
-    own = pieces.reshape(NX * 4, PIECE, HEAD)
-    up, down = [own], [own]
-    for step in range(4):
-        before = up[step - 1] if step > 1 else w_up[3]
-        down.append(lax.ppermute(after(down[-1], w_down[3], before), "z", DOWN))
-        if step < 3:
-            before = (down[step], partial) if step else (w_down[3],)
-            up.append(lax.ppermute(after(up[-1], w_up[4], *before), "z", UP))
+    )(head, after(received, past), swapped, *weights)
+    up.append(lax.ppermute(after(up[1], down[1], partial), "z", UP))
+    up.append(lax.ppermute(after(up[2], down[2]), "z", UP))
+    down.append(lax.ppermute(after(down[2], up[1]), "z", DOWN))
+    tables, place = pl.pallas_call(
+        tables_kernel,
+        out_shape=[
+            jax.ShapeDtypeStruct((2, CONTEXT, HEAD), f32),
+            jax.ShapeDtypeStruct((1, KEYS), jnp.int32),
+        ],
+        in_specs=[SMEM] + [VMEM] * 3,
+        out_specs=[HBM, VMEM],
+        scratch_shapes=[
+            pltpu.VMEM((2, CONTEXT, HEAD), f32),
+            pltpu.SemaphoreType.DMA((CONTEXT // STEP,)),
+        ],
+        compiler_params=grant(56),
+        cost_estimate=FREE,
+    )(after(hist_len, down[2]), sel_pos, column, inverse)
+    down.append(lax.ppermute(after(down[3], up[2], place), "z", DOWN))
     held = down + up[:0:-1]
-
     partial = lax.all_to_all(partial, "x", 0, 0, tiled=True)
-    past = lax.all_to_all(after(past, partial), "head", 0, 0, tiled=True).reshape(HIST, 2 * HEAD)
-    column, inverse = sel.reshape(SEL, 1), jnp.asarray(INVERSE).reshape(1, HEAD)
     queries, fresh_keys, fresh_values = kernel_call(
         queries_kernel,
         [
@@ -357,35 +384,25 @@
     mass = pl.pallas_call(
         weigh_kernel,
         out_shape=jax.ShapeDtypeStruct((QPER * SEL, KEYS), bf16),
-        in_specs=[SMEM, VMEM, ANY] + [VMEM] * 5,
-        out_specs=ANY,
+        in_specs=[VMEM] * 2 + [HBM] + [VMEM] * 4,
+        out_specs=HBM,
         scratch_shapes=[
-            pltpu.VMEM((CONTEXT, HEAD), bf16),
+            pltpu.VMEM((2, CONTEXT, HEAD), f32),
             pltpu.VMEM((KEYS, HEAD), bf16),
-            pltpu.VMEM((1, KEYS), jnp.int32),
             pltpu.VMEM((QPER * SEL, KEYS), f32),
             pltpu.VMEM((QPER * SEL, KEYS), bf16),
+            pltpu.SemaphoreType.DMA((CONTEXT // STEP,)),
             pltpu.SemaphoreType.DMA,
-            pltpu.SemaphoreType.DMA,
-        ],
-        compiler_params=pltpu.CompilerParams(vmem_limit_bytes=56 << 20),
+        ],
+        compiler_params=grant(56),
         cost_estimate=FREE,
-    )(hist_len, queries, raw.reshape(CONTEXT, HEAD), past, fresh_keys, sel_pos, column, inverse)
-    values = lax.all_to_all(pick(z, block_lists, held, 1), "x", 0, 0, tiled=True)
-    values = values.reshape(CONTEXT, HEAD)
-    mixed = pl.pallas_call(
+    )(queries, raw.reshape(CONTEXT, HEAD), tables, place, past, fresh_keys, column)
+    values = lax.all_to_all(pick(after(z, queries), block_lists, held, 1), "x", 0, 0, tiled=True)
+    mixed = kernel_call(
         mix_kernel,
-        out_shape=jax.ShapeDtypeStruct((SEL, QPER * HEAD), bf16),
-        in_specs=[ANY] * 4,
-        out_specs=VMEM,
-        scratch_shapes=[
-            pltpu.VMEM((QPER * SEL, KEYS), bf16),
-            pltpu.VMEM((KEYS, HEAD), bf16),
-            pltpu.SemaphoreType.DMA((QPER + 2,)),
-        ],
-        compiler_params=PARAMS,
-        cost_estimate=FREE,
-    )(mass, values, past, fresh_values)
+        jax.ShapeDtypeStruct((SEL, QPER * HEAD), bf16),
+        [mass, values.reshape(CONTEXT, HEAD), past, fresh_values],
+    )
     return mixed[None]
 
 

time: 147 us -> 137 us (0.932); the launches traced: 145 us -> 136 us
  waiting for transfers between devices: 56.4 us -> 40.3 us
  blocking collectives: 0 us -> 10.9 us
  starting transfers between devices: 48.9 us -> 45.6 us
  local copies, waits for them, and re-layouts: 4.21 us -> 6.18 us
  Pallas kernels: 34 us -> 32.2 us
    ppermute x4, waiting for transfers between devices: 28.6 us -> 7.91 us  [per_device(): lax.ppermute(after(w_up[-1], w_down[max(step - 1, 0)]), 'z', UP)]
    all_to_all x0 -> x1, blocking collectives: none -> 10.9 us  [per_device(): lax.all_to_all(after(past, received), 'head', 0, 0, tiled=True)]
    all_to_all x1, waiting for transfers between devices: 0.01 us -> 6.51 us  [per_device(): lax.all_to_all(after(rows, pieces, w_up[1], w_down[1]), 'x', 0, 0, tiled=...]
    all_to_all x2 -> x1, starting transfers between devices: 8.43 us -> 3.52 us  [per_device(): lax.all_to_all(pick(after(z, queries), block_lists, held, 1), 'x', 0, 0,...]
    all_to_all x1, waiting for transfers between devices: 11.6 us -> 7 us  [per_device(): raw = lax.all_to_all(pick(z, block_lists, held, 0), 'x', 0, 0, tiled=True)]
    ppermute x3, waiting for transfers between devices: 0.01 us -> 4.4 us  [per_device(): w_down.append(lax.ppermute(after(w_down[-1], w_up[step]), 'z', DOWN))]
    pallas_call x1, Pallas kernels: 12.7 us -> 9.37 us  [per_device(): pl.pallas_call(weigh_kernel, out_shape=jax.ShapeDtypeStruct((QPER * SEL,...]
    all_to_all x1, waiting for transfers between devices: 2.49 us -> 0.01 us  [per_device(): partial = lax.all_to_all(partial, 'x', 0, 0, tiled=True)]
  transfers between devices with their start and end apart: 21 -> 20, of which waited for: 11 -> 11; matrix products, arithmetic and copies ran while one was open for 1% -> 1% of each run, Pallas kernels for 19% -> 20%
where the time goes in v3:
time: 137 us; the launch traced here: 136 us
  starting transfers between devices  45.6 us (33%)
  waiting for transfers between devices  40.3 us (29%)
  Pallas kernels  32.2 us (24%)
  blocking collectives  10.9 us (8%)
  local copies, waits for them, and re-layouts  6.18 us (5%)
    ppermute x3, starting transfers between devices, per_device(): w_down.append(lax.ppermute(after(w_down[-1], w_up[step]), 'z', DOWN))  12.4 us
    all_to_all x1, blocking collectives, per_device(): lax.all_to_all(after(past, received), 'head', 0, 0, tiled=True)  10.9 us
    pallas_call x1, Pallas kernels, per_device(): pl.pallas_call(weigh_kernel, out_shape=jax.ShapeDtypeStruct((QPER * SEL,...  9.37 us
    ppermute x1, waiting for transfers between devices, per_device(): up.append(lax.ppermute(after(up[2], down[2]), 'z', UP))  8.5 us
    ppermute x4, waiting for transfers between devices, per_device(): lax.ppermute(after(w_up[-1], w_down[max(step - 1, 0)]), 'z', UP)  7.91 us
    all_to_all x1, waiting for transfers between devices, per_device(): raw = lax.all_to_all(pick(z, block_lists, held, 0), 'x', 0, 0, tiled=True)  7 us
    pallas_call x2, Pallas kernels, pick(): pl.pallas_call(functools.partial(pick_kernel, kind), out_shape=jax.ShapeD...  6.62 us
    all_to_all x1, waiting for transfers between devices, per_device(): lax.all_to_all(after(rows, pieces, w_up[1], w_down[1]), 'x', 0, 0, tiled=...  6.51 us
  transfers between devices with their start and end apart: 20, of which 11 were waited for; matrix products, arithmetic and copies ran while one was open for 1% of the time, Pallas kernels for 20%

profile of v3, /device:TPU:8, one launch (start us, length us, event | category | flops | bytes accessed | tf_op | source)
XLA Modules:
  0.0 136.2 jit_solution(10039279403534771571)
XLA Ops:
  2.5 5.9 %collective-permute-start.1 = (bf16[256,768]{1,0:T(8,128)(2,1)}, bf16[256,768]{1,0:T(8,128)(2,1)S(1)}, u32[]{:S(2)}, u32[]{:S(2)}) collective-permute-start(bf16[256,768]{1,0:T(8,128)(2,1)} %get-tuple-element.36.refs_0_), channel_id=1, source_target_pairs={{0,224},{32,0},{64,32},{96,64},{128,96},{160,128},{192,160},{224,1... | collective-permute-start | bytes 1179656 | tf_op jit(solution)/shard_map/ppermute | solution.py:324
  8.5 4.3 %all-to-all-start = ((bf16[4,2,2,128,128]{4,3,2,1,0:T(8,128)(2,1)}), bf16[4,2,2,128,128]{4,3,2,1,0:T(8,128)(2,1)S(1)}, u32[]{:S(2)}, u32[]{:S(2)}) async-start(bf16[4,2,2,128,128]{4,3,2,1,0:T(8,128)(2,1)} %get-tuple-element.34), calls=%async_computation | async-start | bytes 1048576 | tf_op jit(solution)/shard_map/all_to_all | solution.py:319
  12.8 4.4 %collective-permute-done.1.refs_1_ = bf16[256,768]{1,0:T(8,128)(2,1)S(1)} collective-permute-done((bf16[256,768]{1,0:T(8,128)(2,1)}, bf16[256,768]{1,0:T(8,128)(2,1)S(1)}, u32[]{:S(2)}, u32[]{:S(2)}) %collective-permute-start.1) | collective-permute-done | bytes 393248 | tf_op jit(solution)/shard_map/ppermute | solution.py:324
  17.2 3.3 %collective-permute-done.refs_7_ = bf16[256,768]{1,0:T(8,128)(2,1)S(1)} collective-permute-done((bf16[256,768]{1,0:T(8,128)(2,1)}, bf16[256,768]{1,0:T(8,128)(2,1)S(1)}, u32[]{:S(2)}, u32[]{:S(2)}) %collective-permute-start) | collective-permute-done | bytes 393248 | tf_op jit(solution)/shard_map/ppermute | solution.py:322
  22.0 3.0 %collective-permute-start.4 = (bf16[256,768]{1,0:T(8,128)(2,1)S(1)}, bf16[256,768]{1,0:T(8,128)(2,1)S(1)}, u32[]{:S(2)}, u32[]{:S(2)}) collective-permute-start(bf16[256,768]{1,0:T(8,128)(2,1)S(1)} %collective-permute-done.1.refs_1_), channel_id=1, source_target_pairs={{0,224},{32,0},{64,32},{96,64},{128,96},{160,128},{192,160},{224,1... | collective-permute-start | bytes 1179656 | tf_op jit(solution)/shard_map/ppermute | solution.py:324
  24.9 3.5 %all-to-all-start.1 = ((bf16[4,64,2048]{2,1,0:T(8,128)(2,1)}), bf16[4,64,2048]{2,1,0:T(8,128)(2,1)S(1)}, u32[]{:S(2)}, u32[]{:S(2)}) async-start(bf16[4,64,2048]{2,1,0:T(8,128)(2,1)} %get-tuple-element.37), calls=%async_computation.1 | async-start | bytes 2097152 | tf_op jit(solution)/shard_map/all_to_all | solution.py:325
  28.4 2.9 %collective-permute-done.2.refs_6_ = bf16[256,768]{1,0:T(8,128)(2,1)S(1)} collective-permute-done((bf16[256,768]{1,0:T(8,128)(2,1)S(1)}, bf16[256,768]{1,0:T(8,128)(2,1)S(1)}, u32[]{:S(2)}, u32[]{:S(2)}) %collective-permute-start.2) | collective-permute-done | bytes 393248 | tf_op jit(solution)/shard_map/ppermute | solution.py:322
  31.4 3.6 %collective-permute-start.5 = (bf16[256,768]{1,0:T(8,128)(2,1)S(1)}, bf16[256,768]{1,0:T(8,128)(2,1)}, u32[]{:S(2)}, u32[]{:S(2)}) collective-permute-start(bf16[256,768]{1,0:T(8,128)(2,1)S(1)} %collective-permute-done.4.refs_2_), channel_id=1, source_target_pairs={{0,224},{32,0},{64,32},{96,64},{128,96},{160,128},{192,160},{224,1... | collective-permute-start | bytes 1179656 | tf_op jit(solution)/shard_map/ppermute | solution.py:324
  34.9 6.5 %all-to-all-done.1.received = bf16[4,64,2048]{2,1,0:T(8,128)(2,1)S(1)} async-done(((bf16[4,64,2048]{2,1,0:T(8,128)(2,1)}), bf16[4,64,2048]{2,1,0:T(8,128)(2,1)S(1)}, u32[]{:S(2)}, u32[]{:S(2)}) %all-to-all-start.1) | async-done | bytes 1048608 | tf_op jit(solution)/shard_map/all_to_all | solution.py:325
  41.6 2.9 %collective-permute-start.8 = (bf16[16,128,128]{2,1,0:T(8,128)(2,1)S(1)}, bf16[16,128,128]{2,1,0:T(8,128)(2,1)S(1)}, u32[]{:S(2)}, u32[]{:S(2)}) collective-permute-start(bf16[16,128,128]{2,1,0:T(8,128)(2,1)S(1)} %bitcast.15), channel_id=1, source_target_pairs={{0,224},{32,0},{64,32},{96,64},{128,96},{160,128},{192,160},{224,1... | collective-permute-start | bytes 1572872 | tf_op jit(solution)/shard_map/ppermute | solution.py:333
  44.5 10.9 %all_to_all.30 = bf16[8,64,256]{2,1,0:T(8,128)(2,1)} all-to-all(bf16[8,64,256]{2,1,0:T(8,128)(2,1)S(1)} %copy-done.13), channel_id=1, replica_groups=mesh['z'=8,'x'=4,'head'=8] {'head'}, dimensions={0} | all-to-all | bytes 524288 | tf_op jit(solution)/shard_map/all_to_all | solution.py:326
  57.1 3.2 %collective-permute-start.9 = (bf16[16,128,128]{2,1,0:T(8,128)(2,1)S(1)}, bf16[16,128,128]{2,1,0:T(8,128)(2,1)}, u32[]{:S(2)}, u32[]{:S(2)}) collective-permute-start(bf16[16,128,128]{2,1,0:T(8,128)(2,1)S(1)} %collective-permute-done.8.refs_1_), channel_id=1, source_target_pairs={{0,224},{32,0},{64,32},{96,64},{128,96},{160,128},{192,160},{224,1... | collective-permute-start | bytes 1572872 | tf_op jit(solution)/shard_map/ppermute | solution.py:333
  61.4 5.3 %shard_map.92 = f32[4,128,768]{2,1,0:T(8,128)} custom-call(s32[1]{0:T(128)} %bitcast.head_ref, bf16[4,64,2048]{2,1,0:T(8,128)(2,1)} %copy-done.12, bf16[4,64,2048]{2,1,0:T(8,128)(2,1)} %copy-done.16, bf16[256,768]{1,0:T(8,128)(2,1)} %get-tuple-element.36.refs_0_, bf16[256,768]{1,0:T(8,128)(2,1)} %copy-done.17, bf16[256,768]{1,0:T(8,128)(2,1)} %copy-done.20, ...), custom_call_target="tpu_custom_call" | custom-call | flops 49999998976 | bytes 1048576 | tf_op jit(solution)/shard_map/pallas_call | solution.py:337
  66.7 4.3 %all-to-all-start.3 = ((f32[4,128,768]{2,1,0:T(8,128)}), f32[4,128,768]{2,1,0:T(8,128)S(1)}, u32[]{:S(2)}, u32[]{:S(2)}) async-start(f32[4,128,768]{2,1,0:T(8,128)} %shard_map.92), calls=%async_computation.3 | async-start | bytes 3145728 | tf_op jit(solution)/shard_map/all_to_all | solution.py:371
  71.4 3.3 %collective-permute-start.11 = (bf16[16,128,128]{2,1,0:T(8,128)(2,1)}, bf16[16,128,128]{2,1,0:T(8,128)(2,1)S(1)}, u32[]{:S(2)}, u32[]{:S(2)}) collective-permute-start(bf16[16,128,128]{2,1,0:T(8,128)(2,1)} %collective-permute-done.9.refs_2_), channel_id=1, source_target_pairs={{0,224},{32,0},{64,32},{96,64},{128,96},{160,128},{192,160},{224,1... | collective-permute-start | bytes 1572872 | tf_op jit(solution)/shard_map/ppermute | solution.py:353
  76.1 6.1 %shard_map.94 = (f32[2,4096,128]{2,1,0:T(8,128)}, s32[1,4736]{1,0:T(1,128)}) custom-call(s32[1]{0:T(128)S(6)} %copy.15.length_ref, s32[1,128]{1,0:T(1,128)} %row_ref.1, s32[128,1]{1,0:T(8,128)} %copy.10.column_ref, f32[1,128]{1,0:T(1,128)} %constant.16.inverse_ref), custom_call_target="tpu_custom_call" | custom-call | tf_op jit(solution)/shard_map/pallas_call | solution.py:354
  84.9 3.4 %collective-permute-start.13 = (bf16[16,128,128]{2,1,0:T(8,128)(2,1)S(1)}, bf16[16,128,128]{2,1,0:T(8,128)(2,1)}, u32[]{:S(2)}, u32[]{:S(2)}) collective-permute-start(bf16[16,128,128]{2,1,0:T(8,128)(2,1)S(1)} %collective-permute-done.11.refs_3_), channel_id=1, source_target_pairs={{0,224},{32,0},{64,32},{96,64},{128,96},{160,128},{192,160},{224,1... | collective-permute-start | bytes 1572872 | tf_op jit(solution)/shard_map/ppermute | solution.py:369
  89.0 8.5 %collective-permute-done.14.refs_5_ = bf16[16,128,128]{2,1,0:T(8,128)(2,1)} collective-permute-done((bf16[16,128,128]{2,1,0:T(8,128)(2,1)S(1)}, bf16[16,128,128]{2,1,0:T(8,128)(2,1)}, u32[]{:S(2)}, u32[]{:S(2)}) %collective-permute-start.14) | collective-permute-done | bytes 524320 | tf_op jit(solution)/shard_map/ppermute | solution.py:352
  97.5 3.3 %shard_map.95 = bf16[32,128,128]{2,1,0:T(8,128)(2,1)} custom-call(s32[1]{0:T(128)} %bitcast.1.z_ref, s32[32,8]{1,0:T(8,128)} %copy.12.lists_ref, bf16[16,128,128]{2,1,0:T(8,128)(2,1)} %bitcast.17, bf16[16,128,128]{2,1,0:T(8,128)(2,1)} %copy-done.8, bf16[16,128,128]{2,1,0:T(8,128)(2,1)} %collective-permute-done.9.refs_2_, bf16[16,128,128]{2,1,0:T(8,128)(2,1)} %copy-done.11, ...), custom_call_target="tpu_custom_call" | custom-call | tf_op jit(solution)/shard_map/pallas_call | solution.py:159
  100.9 4.6 %all-to-all-start.4 = ((bf16[4,8,128,128]{3,2,1,0:T(8,128)(2,1)}), bf16[4,8,128,128]{3,2,1,0:T(8,128)(2,1)S(1)}, u32[]{:S(2)}, u32[]{:S(2)}) async-start(bf16[4,8,128,128]{3,2,1,0:T(8,128)(2,1)} %bitcast.20), calls=%async_computation.4 | async-start | bytes 2097152 | tf_op jit(solution)/shard_map/all_to_all | solution.py:383
  107.0 3.3 %shard_map.97 = bf16[32,128,128]{2,1,0:T(8,128)(2,1)} custom-call(s32[1]{0:T(128)} %bitcast.1.z_ref, s32[32,8]{1,0:T(8,128)} %copy.12.lists_ref, bf16[16,128,128]{2,1,0:T(8,128)(2,1)} %bitcast.18, bf16[16,128,128]{2,1,0:T(8,128)(2,1)} %copy-done.8, bf16[16,128,128]{2,1,0:T(8,128)(2,1)} %collective-permute-done.9.refs_2_, bf16[16,128,128]{2,1,0:T(8,128)(2,1)} %copy-done.11, ...), custom_call_target="tpu_custom_call" | custom-call | tf_op jit(solution)/shard_map/pallas_call | solution.py:159
  110.3 7.0 %all-to-all-done.4 = bf16[4,8,128,128]{3,2,1,0:T(8,128)(2,1)S(1)} async-done(((bf16[4,8,128,128]{3,2,1,0:T(8,128)(2,1)}), bf16[4,8,128,128]{3,2,1,0:T(8,128)(2,1)S(1)}, u32[]{:S(2)}, u32[]{:S(2)}) %all-to-all-start.4) | async-done | bytes 1048608 | tf_op jit(solution)/shard_map/all_to_all | solution.py:383
  117.3 3.5 %all-to-all-start.5 = ((bf16[4,8,128,128]{3,2,1,0:T(8,128)(2,1)}), bf16[4,8,128,128]{3,2,1,0:T(8,128)(2,1)S(1)}, u32[]{:S(2)}, u32[]{:S(2)}) async-start(bf16[4,8,128,128]{3,2,1,0:T(8,128)(2,1)} %bitcast.21), calls=%async_computation.5 | async-start | bytes 2097152 | tf_op jit(solution)/shard_map/all_to_all | solution.py:400
  120.9 9.4 %shard_map.96.mass_ref = bf16[512,4736]{1,0:T(8,128)(2,1)} custom-call(bf16[512,128]{1,0:T(8,128)(2,1)} %copy-done.3, bf16[4096,128]{1,0:T(8,128)(2,1)} %bitcast.19, f32[2,4096,128]{2,1,0:T(8,128)} %get-tuple-element.57.tables_ref, s32[1,4736]{1,0:T(1,128)} %get-tuple-element.54.place_ref, bf16[512,256]{1,0:T(8,128)(2,1)} %bitcast.13, ...), custom_call_target="tpu_custom_call" | custom-call | tf_op jit(solution)/shard_map/pallas_call | solution.py:384
  (71 shorter events, 18.9 us)
Async XLA Ops:
  2.5 41.9 %copy-start.13 = (bf16[8,64,256]{2,1,0:T(8,128)(2,1)S(1)}, bf16[8,64,256]{2,1,0:T(8,128)(2,1)}, u32[]{:S(2)}) copy-start(bf16[8,64,256]{2,1,0:T(8,128)(2,1)} %get-tuple-element.44) | copy-start | bytes 786436
  2.5 14.6 %collective-permute-start.1 = (bf16[256,768]{1,0:T(8,128)(2,1)}, bf16[256,768]{1,0:T(8,128)(2,1)S(1)}, u32[]{:S(2)}, u32[]{:S(2)}) collective-permute-start(bf16[256,768]{1,0:T(8,128)(2,1)} %get-tuple-element.36.refs_0_), channel_id=1, source_target_pairs={{0,224},{32,0},{64,32},{96,64},{128,96},{160,128},{192,160},{224,1... | collective-permute-start | bytes 1179656 | tf_op jit(solution)/shard_map/ppermute | solution.py:324
  8.5 12.0 %collective-permute-start = (bf16[256,768]{1,0:T(8,128)(2,1)}, bf16[256,768]{1,0:T(8,128)(2,1)S(1)}, u32[]{:S(2)}, u32[]{:S(2)}) collective-permute-start(bf16[256,768]{1,0:T(8,128)(2,1)} %get-tuple-element.36.refs_0_), channel_id=1, source_target_pairs={{0,32},{32,64},{64,96},{96,128},{128,160},{160,192},{192,224},{224... | collective-permute-start | bytes 1179656 | tf_op jit(solution)/shard_map/ppermute | solution.py:322
  8.5 13.5 %all-to-all-start = ((bf16[4,2,2,128,128]{4,3,2,1,0:T(8,128)(2,1)}), bf16[4,2,2,128,128]{4,3,2,1,0:T(8,128)(2,1)S(1)}, u32[]{:S(2)}, u32[]{:S(2)}) async-start(bf16[4,2,2,128,128]{4,3,2,1,0:T(8,128)(2,1)} %get-tuple-element.34), calls=%async_computation | async-start | bytes 1048576 | tf_op jit(solution)/shard_map/all_to_all | solution.py:319
  17.2 43.2 %copy-start.17 = (bf16[256,768]{1,0:T(8,128)(2,1)}, bf16[256,768]{1,0:T(8,128)(2,1)S(1)}, u32[]{:S(2)}) copy-start(bf16[256,768]{1,0:T(8,128)(2,1)S(1)} %collective-permute-done.1.refs_1_) | copy-start | bytes 1179652
  20.5 10.9 %collective-permute-start.2 = (bf16[256,768]{1,0:T(8,128)(2,1)S(1)}, bf16[256,768]{1,0:T(8,128)(2,1)S(1)}, u32[]{:S(2)}, u32[]{:S(2)}) collective-permute-start(bf16[256,768]{1,0:T(8,128)(2,1)S(1)} %collective-permute-done.refs_7_), channel_id=1, source_target_pairs={{0,32},{32,64},{64,96},{96,128},{128,160},{160,192},{192,224},{224... | collective-permute-start | bytes 1179656 | tf_op jit(solution)/shard_map/ppermute | solution.py:322
  22.0 44.7 %copy-start.6 = (bf16[4,2,2,128,128]{4,3,2,1,0:T(8,128)(2,1)}, bf16[4,2,2,128,128]{4,3,2,1,0:T(8,128)(2,1)S(1)}, u32[]{:S(2)}) copy-start(bf16[4,2,2,128,128]{4,3,2,1,0:T(8,128)(2,1)S(1)} %all-to-all-done) | copy-start | bytes 1572868
  22.0 9.4 %collective-permute-start.4 = (bf16[256,768]{1,0:T(8,128)(2,1)S(1)}, bf16[256,768]{1,0:T(8,128)(2,1)S(1)}, u32[]{:S(2)}, u32[]{:S(2)}) collective-permute-start(bf16[256,768]{1,0:T(8,128)(2,1)S(1)} %collective-permute-done.1.refs_1_), channel_id=1, source_target_pairs={{0,224},{32,0},{64,32},{96,64},{128,96},{160,128},{192,160},{224,1... | collective-permute-start | bytes 1179656 | tf_op jit(solution)/shard_map/ppermute | solution.py:324
  24.9 16.5 %all-to-all-start.1 = ((bf16[4,64,2048]{2,1,0:T(8,128)(2,1)}), bf16[4,64,2048]{2,1,0:T(8,128)(2,1)S(1)}, u32[]{:S(2)}, u32[]{:S(2)}) async-start(bf16[4,64,2048]{2,1,0:T(8,128)(2,1)} %get-tuple-element.37), calls=%async_computation.1 | async-start | bytes 2097152 | tf_op jit(solution)/shard_map/all_to_all | solution.py:325
  31.3 10.1 %collective-permute-start.3 = (bf16[256,768]{1,0:T(8,128)(2,1)S(1)}, bf16[256,768]{1,0:T(8,128)(2,1)}, u32[]{:S(2)}, u32[]{:S(2)}) collective-permute-start(bf16[256,768]{1,0:T(8,128)(2,1)S(1)} %collective-permute-done.2.refs_6_), channel_id=1, source_target_pairs={{0,32},{32,64},{64,96},{96,128},{128,160},{160,192},{192,224},{224... | collective-permute-start | bytes 1179656 | tf_op jit(solution)/shard_map/ppermute | solution.py:322
  31.4 10.1 %collective-permute-start.5 = (bf16[256,768]{1,0:T(8,128)(2,1)S(1)}, bf16[256,768]{1,0:T(8,128)(2,1)}, u32[]{:S(2)}, u32[]{:S(2)}) collective-permute-start(bf16[256,768]{1,0:T(8,128)(2,1)S(1)} %collective-permute-done.4.refs_2_), channel_id=1, source_target_pairs={{0,224},{32,0},{64,32},{96,64},{128,96},{160,128},{192,160},{224,1... | collective-permute-start | bytes 1179656 | tf_op jit(solution)/shard_map/ppermute | solution.py:324
  41.5 18.9 %collective-permute-start.6 = (bf16[4,64,2048]{2,1,0:T(8,128)(2,1)S(1)}, bf16[4,64,2048]{2,1,0:T(8,128)(2,1)S(1)}, u32[]{:S(2)}, u32[]{:S(2)}) collective-permute-start(bf16[4,64,2048]{2,1,0:T(8,128)(2,1)S(1)} %all-to-all-done.1.received), channel_id=1, source_target_pairs={{0,1},{1,0},{2,3},{3,2},{4,5},{5,4},{6,7},{7,6},{8,9},{9,8},{10,11... | collective-permute-start | bytes 3145736 | tf_op jit(solution)/shard_map/ppermute | solution.py:328
  41.6 15.5 %collective-permute-start.8 = (bf16[16,128,128]{2,1,0:T(8,128)(2,1)S(1)}, bf16[16,128,128]{2,1,0:T(8,128)(2,1)S(1)}, u32[]{:S(2)}, u32[]{:S(2)}) collective-permute-start(bf16[16,128,128]{2,1,0:T(8,128)(2,1)S(1)} %bitcast.15), channel_id=1, source_target_pairs={{0,224},{32,0},{64,32},{96,64},{128,96},{160,128},{192,160},{224,1... | collective-permute-start | bytes 1572872 | tf_op jit(solution)/shard_map/ppermute | solution.py:333
  44.5 12.6 %collective-permute-start.7 = (bf16[256,768]{1,0:T(8,128)(2,1)}, bf16[256,768]{1,0:T(8,128)(2,1)S(1)}, u32[]{:S(2)}, u32[]{:S(2)}) collective-permute-start(bf16[256,768]{1,0:T(8,128)(2,1)} %collective-permute-done.3.refs_5_), channel_id=1, source_target_pairs={{0,32},{32,64},{64,96},{96,128},{128,160},{160,192},{192,224},{224... | collective-permute-start | bytes 1179656 | tf_op jit(solution)/shard_map/ppermute | solution.py:322
  57.1 14.4 %collective-permute-start.10 = (bf16[16,128,128]{2,1,0:T(8,128)(2,1)S(1)}, bf16[16,128,128]{2,1,0:T(8,128)(2,1)S(1)}, u32[]{:S(2)}, u32[]{:S(2)}) collective-permute-start(bf16[16,128,128]{2,1,0:T(8,128)(2,1)S(1)} %bitcast.16), channel_id=1, source_target_pairs={{0,32},{32,64},{64,96},{96,128},{128,160},{160,192},{192,224},{224... | collective-permute-start | bytes 1572872 | tf_op jit(solution)/shard_map/ppermute | solution.py:335
  57.1 14.4 %collective-permute-start.9 = (bf16[16,128,128]{2,1,0:T(8,128)(2,1)S(1)}, bf16[16,128,128]{2,1,0:T(8,128)(2,1)}, u32[]{:S(2)}, u32[]{:S(2)}) collective-permute-start(bf16[16,128,128]{2,1,0:T(8,128)(2,1)S(1)} %collective-permute-done.8.refs_1_), channel_id=1, source_target_pairs={{0,224},{32,0},{64,32},{96,64},{128,96},{160,128},{192,160},{224,1... | collective-permute-start | bytes 1572872 | tf_op jit(solution)/shard_map/ppermute | solution.py:333
  66.7 34.1 %all-to-all-start.3 = ((f32[4,128,768]{2,1,0:T(8,128)}), f32[4,128,768]{2,1,0:T(8,128)S(1)}, u32[]{:S(2)}, u32[]{:S(2)}) async-start(f32[4,128,768]{2,1,0:T(8,128)} %shard_map.92), calls=%async_computation.3 | async-start | bytes 3145728 | tf_op jit(solution)/shard_map/all_to_all | solution.py:371
  71.4 26.1 %copy-start.9 = (bf16[16,128,128]{2,1,0:T(8,128)(2,1)}, bf16[16,128,128]{2,1,0:T(8,128)(2,1)S(1)}, u32[]{:S(2)}) copy-start(bf16[16,128,128]{2,1,0:T(8,128)(2,1)S(1)} %collective-permute-done.10.refs_7_) | copy-start | bytes 1572868
  71.4 13.4 %collective-permute-start.12 = (bf16[16,128,128]{2,1,0:T(8,128)(2,1)S(1)}, bf16[16,128,128]{2,1,0:T(8,128)(2,1)S(1)}, u32[]{:S(2)}, u32[]{:S(2)}) collective-permute-start(bf16[16,128,128]{2,1,0:T(8,128)(2,1)S(1)} %collective-permute-done.10.refs_7_), channel_id=1, source_target_pairs={{0,32},{32,64},{64,96},{96,128},{128,160},{160,192},{192,224},{224... | collective-permute-start | bytes 1572872 | tf_op jit(solution)/shard_map/ppermute | solution.py:351
  71.4 13.4 %collective-permute-start.11 = (bf16[16,128,128]{2,1,0:T(8,128)(2,1)}, bf16[16,128,128]{2,1,0:T(8,128)(2,1)S(1)}, u32[]{:S(2)}, u32[]{:S(2)}) collective-permute-start(bf16[16,128,128]{2,1,0:T(8,128)(2,1)} %collective-permute-done.9.refs_2_), channel_id=1, source_target_pairs={{0,224},{32,0},{64,32},{96,64},{128,96},{160,128},{192,160},{224,1... | collective-permute-start | bytes 1572872 | tf_op jit(solution)/shard_map/ppermute | solution.py:353
  84.9 12.6 %collective-permute-start.14 = (bf16[16,128,128]{2,1,0:T(8,128)(2,1)S(1)}, bf16[16,128,128]{2,1,0:T(8,128)(2,1)}, u32[]{:S(2)}, u32[]{:S(2)}) collective-permute-start(bf16[16,128,128]{2,1,0:T(8,128)(2,1)S(1)} %collective-permute-done.12.refs_6_), channel_id=1, source_target_pairs={{0,32},{32,64},{64,96},{96,128},{128,160},{160,192},{192,224},{224... | collective-permute-start | bytes 1572872 | tf_op jit(solution)/shard_map/ppermute | solution.py:352
  84.9 12.6 %collective-permute-start.13 = (bf16[16,128,128]{2,1,0:T(8,128)(2,1)S(1)}, bf16[16,128,128]{2,1,0:T(8,128)(2,1)}, u32[]{:S(2)}, u32[]{:S(2)}) collective-permute-start(bf16[16,128,128]{2,1,0:T(8,128)(2,1)S(1)} %collective-permute-done.11.refs_3_), channel_id=1, source_target_pairs={{0,224},{32,0},{64,32},{96,64},{128,96},{160,128},{192,160},{224,1... | collective-permute-start | bytes 1572872 | tf_op jit(solution)/shard_map/ppermute | solution.py:369
  100.9 16.5 %all-to-all-start.4 = ((bf16[4,8,128,128]{3,2,1,0:T(8,128)(2,1)}), bf16[4,8,128,128]{3,2,1,0:T(8,128)(2,1)S(1)}, u32[]{:S(2)}, u32[]{:S(2)}) async-start(bf16[4,8,128,128]{3,2,1,0:T(8,128)(2,1)} %bitcast.20), calls=%async_computation.4 | async-start | bytes 2097152 | tf_op jit(solution)/shard_map/all_to_all | solution.py:383
  117.3 14.4 %all-to-all-start.5 = ((bf16[4,8,128,128]{3,2,1,0:T(8,128)(2,1)}), bf16[4,8,128,128]{3,2,1,0:T(8,128)(2,1)S(1)}, u32[]{:S(2)}, u32[]{:S(2)}) async-start(bf16[4,8,128,128]{3,2,1,0:T(8,128)(2,1)} %bitcast.21), calls=%async_computation.5 | async-start | bytes 2097152 | tf_op jit(solution)/shard_map/all_to_all | solution.py:400
  (18 other events, 171.0 us)

commit v4 on v3

--- a/solution.py
+++ b/solution.py
@@ -55,15 +55,26 @@
     return values * cosine + pltpu.roll(values, 64, 1) * sine
 
 
+def pack_kernel(w_query, w_key_value, both, held, sem):
+    at = QPER * HEAD
+    loads = [
+        pltpu.make_async_copy(w_query, held.at[:, :at], sem),
+        pltpu.make_async_copy(w_key_value, held.at[:, at:], sem),
+    ]
+    for load in loads:
+        load.start()
+    for load in loads:
+        load.wait()
+    store = pltpu.make_async_copy(held, both, sem)
+    store.start()
+    store.wait()
+
+
 def prepare_kernel(
-    z_ref, head_ref, hidden, w_query, w_key_value, block, history,
-    both, pieces, rows, past, held_both, held_pieces, held_rows, held_past, sems,
+    z_ref, head_ref, hidden, block, history,
+    pieces, rows, past, held_pieces, held_rows, held_past, sems,
 ):
     loads = [
-        [
-            (w_query, held_both.at[:, : QPER * HEAD]),
-            (w_key_value, held_both.at[:, QPER * HEAD :]),
-        ],
         [],
         [],
         [(history.at[:, i * 256 : (i + 1) * 256], held_past.at[i]) for i in range(NH)],
@@ -71,14 +82,14 @@
     for x in range(NX):
         for kind in range(2):
             part = block.at[:, x * PIECE : (x + 1) * PIECE, kind * HEAD : (kind + 1) * HEAD]
-            loads[1].append((part, held_pieces.at[x, kind]))
+            loads[0].append((part, held_pieces.at[x, kind]))
     mine = pl.ds(pl.multiple_of((head_ref[0] & 1) * HALF, HALF), HALF)
     for hop in range(NZ):
         chunk = ((z_ref[0] + hop) & (NZ - 1)) * NX
         for x in range(NX):
             at = pl.multiple_of((chunk + x) * 256, 256)
             to = held_rows.at[x, :, hop * 256 : (hop + 1) * 256]
-            loads[2].append((hidden.at[mine, pl.ds(at, 256)], to))
+            loads[1].append((hidden.at[mine, pl.ds(at, 256)], to))
     loads = [
         [pltpu.make_async_copy(*pair, sems.at[group]) for pair in pairs]
         for group, pairs in enumerate(loads)
@@ -87,11 +98,11 @@
         for load in group:
             load.start()
     stores = []
-    pairs = (held_both, both), (held_pieces, pieces), (held_rows, rows), (held_past, past)
+    pairs = (held_pieces, pieces), (held_rows, rows), (held_past, past)
     for group, pair in enumerate(pairs):
         for load in loads[group]:
             load.wait()
-        stores.append(pltpu.make_async_copy(*pair, sems.at[4 + group]))
+        stores.append(pltpu.make_async_copy(*pair, sems.at[3 + group]))
         stores[-1].start()
     for store in stores:
         store.wait()
@@ -118,16 +129,12 @@
 
 
 def pick_kernel(kind, z_ref, lists_ref, *refs):
-    sources, out, held, sems = refs[:NZ], *refs[NZ:]
+    sources, out, sem = refs[:NZ], *refs[NZ:]
     z = z_ref[0]
-
-    def part(x):
-        return pl.ds(x * RET, RET)
 
     def leaf(at, away, inner, low, high):
         if high - low == 1:
-            to = held.at[at]
-            pltpu.make_async_copy(sources[low].at[inner], to, sems.at[at >> 3]).start()
+            pltpu.make_async_copy(sources[low].at[inner], out.at[at], sem).start()
             return
         middle = (low + high) // 2
 
@@ -145,27 +152,18 @@
         leaf(at, ((block >> 3) - z) & (NZ - 1), inner, 0, NZ)
         return 0
 
-    lax.fori_loop(0, NX * RET, one, 0, unroll=8)
-    stores = []
-    for x in range(NX):
-        pltpu.make_async_copy(held.at[part(x)], held.at[part(x)], sems.at[x]).wait()
-        stores.append(pltpu.make_async_copy(held.at[part(x)], out.at[part(x)], sems.at[NX + x]))
-        stores[-1].start()
-    for store in stores:
-        store.wait()
+    lax.fori_loop(0, NX * RET, one, 0, unroll=4)
+    pltpu.make_async_copy(out, out, sem).wait()
 
 
 def pick(z, block_lists, sources, kind):
     out = pl.pallas_call(
         functools.partial(pick_kernel, kind),
         out_shape=jax.ShapeDtypeStruct((NX * RET, PIECE, HEAD), jnp.bfloat16),
-        in_specs=[SMEM, SMEM] + [HBM] * NZ,
+        in_specs=[SMEM, SMEM] + [VMEM] * NZ,
         out_specs=HBM,
-        scratch_shapes=[
-            pltpu.VMEM((NX * RET, PIECE, HEAD), jnp.bfloat16),
-            pltpu.SemaphoreType.DMA((2 * NX,)),
-        ],
-        compiler_params=grant(56),
+        scratch_shapes=[pltpu.SemaphoreType.DMA],
+        compiler_params=grant(8),
         cost_estimate=FREE,
     )(z, block_lists, *sources)
     return out.reshape(NX, RET, PIECE, HEAD)
@@ -304,35 +302,42 @@
     bf16, f32 = jnp.bfloat16, jnp.float32
 
     head = lax.axis_index("head").reshape(1)
-    shapes = (256, WIDE), (NX, 2, 2, PIECE, HEAD), (NX, HALF, NZ * 256), (NH, HIST // NH, 256)
-    both, pieces, rows, past = pl.pallas_call(
+    both = pl.pallas_call(
+        pack_kernel,
+        out_shape=jax.ShapeDtypeStruct((256, WIDE), bf16),
+        in_specs=[HBM] * 2,
+        out_specs=HBM,
+        scratch_shapes=[pltpu.VMEM((256, WIDE), bf16), pltpu.SemaphoreType.DMA],
+        compiler_params=grant(56),
+        cost_estimate=FREE,
+    )(w_query, w_key_value)
+    shapes = (NX, 2, 2, PIECE, HEAD), (NX, HALF, NZ * 256), (NH, HIST // NH, 256)
+    pieces, rows, past = pl.pallas_call(
         prepare_kernel,
         out_shape=[jax.ShapeDtypeStruct(shape, bf16) for shape in shapes],
-        in_specs=[SMEM] * 2 + [HBM] * 5,
-        out_specs=[HBM] * 4,
+        in_specs=[SMEM] * 2 + [HBM] * 3,
+        out_specs=[HBM] * 3,
         scratch_shapes=[pltpu.VMEM(shape, bf16) for shape in shapes]
-        + [pltpu.SemaphoreType.DMA((8,))],
+        + [pltpu.SemaphoreType.DMA((6,))],
         compiler_params=grant(56),
         cost_estimate=COST,
-    )(z, head, hidden[0], w_query, w_key_value, block_kv, history_kv[0])
+    )(z, head, after(hidden[0], both), block_kv, history_kv[0])
 
     pieces = lax.all_to_all(pieces, "x", 0, 0, tiled=True)
-    w_up, w_down = [both], [both]
-    for step in range(4):
+    own = pieces.reshape(NX * 4, PIECE, HEAD)
+    w_up, w_down, up, down = [both], [both], [own], [own]
+    for step in range(3):
+        w_down.append(lax.ppermute(after(w_down[-1], w_up[step]), "z", DOWN))
         w_up.append(lax.ppermute(after(w_up[-1], w_down[max(step - 1, 0)]), "z", UP))
-        if step < 3:
-            w_down.append(lax.ppermute(after(w_down[-1], w_up[step]), "z", DOWN))
+    down.append(lax.ppermute(after(own, w_down[3], w_up[3]), "z", DOWN))
+    w_up.append(lax.ppermute(after(w_up[3], w_down[2]), "z", UP))
     received = lax.all_to_all(after(rows, pieces, w_up[1], w_down[1]), "x", 0, 0, tiled=True)
     past = lax.all_to_all(after(past, received), "head", 0, 0, tiled=True).reshape(HIST, 2 * HEAD)
     received = after(received, w_up[3], w_down[3])
     swapped = lax.ppermute(received, "head", [(i, i ^ 1) for i in range(NH)])
     weights = w_down + w_up[:0:-1]
-    own = pieces.reshape(NX * 4, PIECE, HEAD)
-    up, down = [own], [own]
-    for step in range(2):
-        down.append(lax.ppermute(after(down[-1], w_down[3], w_up[3]), "z", DOWN))
-        if step == 0:
-            up.append(lax.ppermute(after(up[-1], w_up[4], w_down[3], past), "z", UP))
+    down.append(lax.ppermute(after(down[1], w_down[3], w_up[3]), "z", DOWN))
+    up.append(lax.ppermute(after(own, w_up[4], w_down[3], past), "z", UP))
 
     partial = pl.pallas_call(
         project_kernel,
@@ -363,7 +368,7 @@
             pltpu.VMEM((2, CONTEXT, HEAD), f32),
             pltpu.SemaphoreType.DMA((CONTEXT // STEP,)),
         ],
-        compiler_params=grant(56),
+        compiler_params=grant(16),
         cost_estimate=FREE,
     )(after(hist_len, down[2]), sel_pos, column, inverse)
     down.append(lax.ppermute(after(down[3], up[2], place), "z", DOWN))

time: 137 us -> 136 us (level)
  waiting for transfers between devices: 40.3 us -> 37.9 us
  local copies, waits for them, and re-layouts: 6.18 us -> 8.23 us
    ppermute x4 -> x3, waiting for transfers between devices: 7.91 us -> 15 us  [per_device(): lax.ppermute(after(w_up[-1], w_down[max(step - 1, 0)]), 'z', UP)]
    all_to_all x1, waiting for transfers between devices: 6.51 us -> 0.01 us  [per_device(): lax.all_to_all(after(rows, pieces, w_up[1], w_down[1]), 'x', 0, 0, tiled=...]
    ppermute x3, waiting for transfers between devices: 4.4 us -> 0.01 us  [per_device(): w_down.append(lax.ppermute(after(w_down[-1], w_up[step]), 'z', DOWN))]
    unnamed x45 -> x37, local copies, waits for them, and re-layouts: 5.44 us -> 8.12 us
    pallas_call x0 -> x1, Pallas kernels: none -> 1.75 us  [per_device(): pl.pallas_call(pack_kernel, out_shape=jax.ShapeDtypeStruct((256, WIDE), b...]
    ppermute x3 -> x4, waiting for transfers between devices: 0.41 us -> 1.99 us  [the longest x1 1.7 us: per_device(): w_up.append(lax.ppermute(after(w_up[3], w_down[2]), 'z', UP))]
    ppermute x3 -> x4, starting transfers between devices: 6.11 us -> 5.73 us  [the longest x1 3.23 us: per_device(): down.append(lax.ppermute(after(down[1], w_down[3], w_up[3]), 'z', DOWN))]
  transfers between devices with their start and end apart: 20 -> 20, of which waited for: 11 -> 10; matrix products, arithmetic and copies ran while one was open for 1% -> 0% of each run, Pallas kernels for 20% -> 21%
where the time goes in v4:
time: 136 us
  starting transfers between devices  45.4 us (33%)
  waiting for transfers between devices  37.9 us (28%)
  Pallas kernels  32.4 us (24%)
  blocking collectives  10.9 us (8%)
  local copies, waits for them, and re-layouts  8.23 us (6%)
    ppermute x3, waiting for transfers between devices, per_device(): lax.ppermute(after(w_up[-1], w_down[max(step - 1, 0)]), 'z', UP)  15 us
    ppermute x3, starting transfers between devices, per_device(): w_down.append(lax.ppermute(after(w_down[-1], w_up[step]), 'z', DOWN))  12.4 us
    all_to_all x1, blocking collectives, per_device(): lax.all_to_all(after(past, received), 'head', 0, 0, tiled=True)  10.9 us
    ppermute x1, waiting for transfers between devices, per_device(): up.append(lax.ppermute(after(up[2], down[2]), 'z', UP))  9.37 us
    pallas_call x1, Pallas kernels, per_device(): pl.pallas_call(weigh_kernel, out_shape=jax.ShapeDtypeStruct((QPER * SEL,...  9.35 us
    unnamed x37, local copies, waits for them, and re-layouts  8.12 us
    all_to_all x1, waiting for transfers between devices, per_device(): raw = lax.all_to_all(pick(z, block_lists, held, 0), 'x', 0, 0, tiled=True)  7.28 us
    pallas_call x2, Pallas kernels, pick(): pl.pallas_call(functools.partial(pick_kernel, kind), out_shape=jax.ShapeD...  6.22 us
  transfers between devices with their start and end apart: 20, of which 10 were waited for; matrix products, arithmetic and copies ran while one was open for 0% of the time, Pallas kernels for 21%

profile of v4, /device:TPU:8, one launch (start us, length us, event | category | flops | bytes accessed | tf_op | source)
XLA Modules:
  0.0 135.7 jit_solution(16005261222390995110)
XLA Ops:
  1.8 5.9 %collective-permute-start.1 = (bf16[256,768]{1,0:T(8,128)(2,1)}, bf16[256,768]{1,0:T(8,128)(2,1)S(1)}, u32[]{:S(2)}, u32[]{:S(2)}) collective-permute-start(bf16[256,768]{1,0:T(8,128)(2,1)} %shard_map.91.refs_0_), channel_id=1, source_target_pairs={{0,224},{32,0},{64,32},{96,64},{128,96},{160,128},{192,160},{224,1... | collective-permute-start | bytes 1179656 | tf_op jit(solution)/shard_map/ppermute | solution.py:330
  7.7 2.5 %shard_map.92 = (bf16[4,2,2,128,128]{4,3,2,1,0:T(8,128)(2,1)}, bf16[4,64,2048]{2,1,0:T(8,128)(2,1)}, bf16[8,64,256]{2,1,0:T(8,128)(2,1)}) custom-call(s32[1]{0:T(128)} %bitcast.1.z_ref, s32[1]{0:T(128)} %bitcast.head_ref, bf16[128,8192]{1,0:T(8,128)(2,1)} %bitcast.20, bf16[2,512,256]{2,1,0:T(8,128)(2,1)} %block.1, bf16[64,2048]{1,0:T(8,128)(2,1)} %bitcast.21), custom_call_target="tpu_custom_call" | custom-call | flops 49999998976 | bytes 1048576 | tf_op jit(solution)/shard_map/pallas_call | solution.py:315
  10.2 4.4 %all-to-all-start = ((bf16[4,2,2,128,128]{4,3,2,1,0:T(8,128)(2,1)}), bf16[4,2,2,128,128]{4,3,2,1,0:T(8,128)(2,1)S(1)}, u32[]{:S(2)}, u32[]{:S(2)}) async-start(bf16[4,2,2,128,128]{4,3,2,1,0:T(8,128)(2,1)} %get-tuple-element.35), calls=%async_computation | async-start | bytes 1048576 | tf_op jit(solution)/shard_map/all_to_all | solution.py:326
  14.6 5.1 %collective-permute-done.refs_7_ = bf16[256,768]{1,0:T(8,128)(2,1)S(1)} collective-permute-done((bf16[256,768]{1,0:T(8,128)(2,1)}, bf16[256,768]{1,0:T(8,128)(2,1)S(1)}, u32[]{:S(2)}, u32[]{:S(2)}) %collective-permute-start) | collective-permute-done | bytes 393248 | tf_op jit(solution)/shard_map/ppermute | solution.py:331
  19.7 3.2 %collective-permute-start.4 = (bf16[256,768]{1,0:T(8,128)(2,1)S(1)}, bf16[256,768]{1,0:T(8,128)(2,1)}, u32[]{:S(2)}, u32[]{:S(2)}) collective-permute-start(bf16[256,768]{1,0:T(8,128)(2,1)S(1)} %collective-permute-done.1.refs_1_), channel_id=1, source_target_pairs={{0,224},{32,0},{64,32},{96,64},{128,96},{160,128},{192,160},{224,1... | collective-permute-start | bytes 1179656 | tf_op jit(solution)/shard_map/ppermute | solution.py:330
  23.8 3.5 %all-to-all-start.1 = ((bf16[4,64,2048]{2,1,0:T(8,128)(2,1)}), bf16[4,64,2048]{2,1,0:T(8,128)(2,1)S(1)}, u32[]{:S(2)}, u32[]{:S(2)}) async-start(bf16[4,64,2048]{2,1,0:T(8,128)(2,1)} %get-tuple-element.37), calls=%async_computation.1 | async-start | bytes 2097152 | tf_op jit(solution)/shard_map/all_to_all | solution.py:334
  27.3 3.2 %collective-permute-done.2.refs_6_ = bf16[256,768]{1,0:T(8,128)(2,1)S(1)} collective-permute-done((bf16[256,768]{1,0:T(8,128)(2,1)S(1)}, bf16[256,768]{1,0:T(8,128)(2,1)S(1)}, u32[]{:S(2)}, u32[]{:S(2)}) %collective-permute-start.2) | collective-permute-done | bytes 393248 | tf_op jit(solution)/shard_map/ppermute | solution.py:331
  30.6 3.2 %collective-permute-start.5 = (bf16[256,768]{1,0:T(8,128)(2,1)}, bf16[256,768]{1,0:T(8,128)(2,1)}, u32[]{:S(2)}, u32[]{:S(2)}) collective-permute-start(bf16[256,768]{1,0:T(8,128)(2,1)} %collective-permute-done.4.refs_2_), channel_id=1, source_target_pairs={{0,224},{32,0},{64,32},{96,64},{128,96},{160,128},{192,160},{224,1... | collective-permute-start | bytes 1179656 | tf_op jit(solution)/shard_map/ppermute | solution.py:330
  33.8 6.7 %collective-permute-done.3.refs_5_ = bf16[256,768]{1,0:T(8,128)(2,1)S(1)} collective-permute-done((bf16[256,768]{1,0:T(8,128)(2,1)S(1)}, bf16[256,768]{1,0:T(8,128)(2,1)S(1)}, u32[]{:S(2)}, u32[]{:S(2)}) %collective-permute-start.3) | collective-permute-done | bytes 393248 | tf_op jit(solution)/shard_map/ppermute | solution.py:331
  41.4 2.5 %collective-permute-start.8 = (bf16[16,128,128]{2,1,0:T(8,128)(2,1)S(1)}, bf16[16,128,128]{2,1,0:T(8,128)(2,1)S(1)}, u32[]{:S(2)}, u32[]{:S(2)}) collective-permute-start(bf16[16,128,128]{2,1,0:T(8,128)(2,1)S(1)} %bitcast.12), channel_id=1, source_target_pairs={{0,224},{32,0},{64,32},{96,64},{128,96},{160,128},{192,160},{224,1... | collective-permute-start | bytes 1572872 | tf_op jit(solution)/shard_map/ppermute | solution.py:332
  43.9 10.9 %all_to_all.30 = bf16[8,64,256]{2,1,0:T(8,128)(2,1)} all-to-all(bf16[8,64,256]{2,1,0:T(8,128)(2,1)S(1)} %copy-done.10), channel_id=1, replica_groups=mesh['z'=8,'x'=4,'head'=8] {'head'}, dimensions={0} | all-to-all | bytes 524288 | tf_op jit(solution)/shard_map/all_to_all | solution.py:335
  56.5 3.2 %collective-permute-start.9 = (bf16[16,128,128]{2,1,0:T(8,128)(2,1)S(1)}, bf16[16,128,128]{2,1,0:T(8,128)(2,1)}, u32[]{:S(2)}, u32[]{:S(2)}) collective-permute-start(bf16[16,128,128]{2,1,0:T(8,128)(2,1)S(1)} %collective-permute-done.8.refs_1_), channel_id=1, source_target_pairs={{0,224},{32,0},{64,32},{96,64},{128,96},{160,128},{192,160},{224,1... | collective-permute-start | bytes 1572872 | tf_op jit(solution)/shard_map/ppermute | solution.py:339
  60.8 5.3 %shard_map.93 = f32[4,128,768]{2,1,0:T(8,128)} custom-call(s32[1]{0:T(128)} %bitcast.head_ref, bf16[4,64,2048]{2,1,0:T(8,128)(2,1)} %copy-done.9, bf16[4,64,2048]{2,1,0:T(8,128)(2,1)} %copy-done.12, bf16[256,768]{1,0:T(8,128)(2,1)} %shard_map.91.refs_0_, bf16[256,768]{1,0:T(8,128)(2,1)} %copy-done.13, bf16[256,768]{1,0:T(8,128)(2,1)} %collective-permute-done.4.refs_2_, ...), custom_call_target="tpu_custom_call" | custom-call | flops 49999998976 | bytes 1048576 | tf_op jit(solution)/shard_map/pallas_call | solution.py:342
  66.1 4.4 %all-to-all-start.3 = ((f32[4,128,768]{2,1,0:T(8,128)}), f32[4,128,768]{2,1,0:T(8,128)S(1)}, u32[]{:S(2)}, u32[]{:S(2)}) async-start(f32[4,128,768]{2,1,0:T(8,128)} %shard_map.93), calls=%async_computation.3 | async-start | bytes 3145728 | tf_op jit(solution)/shard_map/all_to_all | solution.py:376
  70.9 3.3 %collective-permute-start.11 = (bf16[16,128,128]{2,1,0:T(8,128)(2,1)}, bf16[16,128,128]{2,1,0:T(8,128)(2,1)}, u32[]{:S(2)}, u32[]{:S(2)}) collective-permute-start(bf16[16,128,128]{2,1,0:T(8,128)(2,1)} %collective-permute-done.9.refs_2_), channel_id=1, source_target_pairs={{0,224},{32,0},{64,32},{96,64},{128,96},{160,128},{192,160},{224,1... | collective-permute-start | bytes 1572872 | tf_op jit(solution)/shard_map/ppermute | solution.py:358
  74.9 5.0 %shard_map.95 = (f32[2,4096,128]{2,1,0:T(8,128)S(1)}, s32[1,4736]{1,0:T(1,128)S(1)}) custom-call(s32[1]{0:T(128)S(6)} %copy.15.length_ref, s32[1,128]{1,0:T(1,128)S(1)} %copy-done.7, s32[128,1]{1,0:T(8,128)S(1)} %copy.10.column_ref, f32[1,128]{1,0:T(1,128)S(1)} %copy-done.8), custom_call_target="tpu_custom_call" | custom-call | tf_op jit(solution)/shard_map/pallas_call | solution.py:359
  84.4 3.4 %collective-permute-start.13 = (bf16[16,128,128]{2,1,0:T(8,128)(2,1)}, bf16[16,128,128]{2,1,0:T(8,128)(2,1)}, u32[]{:S(2)}, u32[]{:S(2)}) collective-permute-start(bf16[16,128,128]{2,1,0:T(8,128)(2,1)} %collective-permute-done.11.refs_3_), channel_id=1, source_target_pairs={{0,224},{32,0},{64,32},{96,64},{128,96},{160,128},{192,160},{224,1... | collective-permute-start | bytes 1572872 | tf_op jit(solution)/shard_map/ppermute | solution.py:374
  87.9 9.4 %collective-permute-done.14.refs_5_ = bf16[16,128,128]{2,1,0:T(8,128)(2,1)} collective-permute-done((bf16[16,128,128]{2,1,0:T(8,128)(2,1)}, bf16[16,128,128]{2,1,0:T(8,128)(2,1)}, u32[]{:S(2)}, u32[]{:S(2)}) %collective-permute-start.14) | collective-permute-done | bytes 524320 | tf_op jit(solution)/shard_map/ppermute | solution.py:357
  97.3 3.1 %shard_map.96 = bf16[32,128,128]{2,1,0:T(8,128)(2,1)} custom-call(s32[1]{0:T(128)} %bitcast.1.z_ref, s32[32,8]{1,0:T(8,128)S(1)} %copy.12.lists_ref, bf16[16,128,128]{2,1,0:T(8,128)(2,1)S(1)} %bitcast.14, bf16[16,128,128]{2,1,0:T(8,128)(2,1)S(1)} %collective-permute-done.8.refs_1_, bf16[16,128,128]{2,1,0:T(8,128)(2,1)} %collective-permute-done.9.refs_2_, ...), custom_call_target="tpu_custom_call" | custom-call | tf_op jit(solution)/shard_map/pallas_call | solution.py:160
  100.4 4.5 %all-to-all-start.4 = ((bf16[4,8,128,128]{3,2,1,0:T(8,128)(2,1)}), bf16[4,8,128,128]{3,2,1,0:T(8,128)(2,1)}, u32[]{:S(2)}, u32[]{:S(2)}) async-start(bf16[4,8,128,128]{3,2,1,0:T(8,128)(2,1)} %bitcast.7), calls=%async_computation.4 | async-start | bytes 2097152 | tf_op jit(solution)/shard_map/all_to_all | solution.py:388
  106.5 3.2 %shard_map.98 = bf16[32,128,128]{2,1,0:T(8,128)(2,1)} custom-call(s32[1]{0:T(128)} %bitcast.1.z_ref, s32[32,8]{1,0:T(8,128)S(1)} %copy.12.lists_ref, bf16[16,128,128]{2,1,0:T(8,128)(2,1)S(1)} %bitcast.15, bf16[16,128,128]{2,1,0:T(8,128)(2,1)S(1)} %collective-permute-done.8.refs_1_, bf16[16,128,128]{2,1,0:T(8,128)(2,1)} %collective-permute-done.9.refs_2_, ...), custom_call_target="tpu_custom_call" | custom-call | tf_op jit(solution)/shard_map/pallas_call | solution.py:160
  109.6 7.3 %all-to-all-done.4 = bf16[4,8,128,128]{3,2,1,0:T(8,128)(2,1)} async-done(((bf16[4,8,128,128]{3,2,1,0:T(8,128)(2,1)}), bf16[4,8,128,128]{3,2,1,0:T(8,128)(2,1)}, u32[]{:S(2)}, u32[]{:S(2)}) %all-to-all-start.4) | async-done | bytes 1048608 | tf_op jit(solution)/shard_map/all_to_all | solution.py:388
  116.9 3.5 %all-to-all-start.5 = ((bf16[4,8,128,128]{3,2,1,0:T(8,128)(2,1)}), bf16[4,8,128,128]{3,2,1,0:T(8,128)(2,1)S(1)}, u32[]{:S(2)}, u32[]{:S(2)}) async-start(bf16[4,8,128,128]{3,2,1,0:T(8,128)(2,1)} %bitcast.9), calls=%async_computation.5 | async-start | bytes 2097152 | tf_op jit(solution)/shard_map/all_to_all | solution.py:405
  120.4 9.4 %shard_map.97.mass_ref = bf16[512,4736]{1,0:T(8,128)(2,1)} custom-call(bf16[512,128]{1,0:T(8,128)(2,1)} %copy-done.4, bf16[4096,128]{1,0:T(8,128)(2,1)} %bitcast.8.raw_ref, f32[2,4096,128]{2,1,0:T(8,128)} %copy-done.1, s32[1,4736]{1,0:T(1,128)} %copy-done.6, bf16[512,256]{1,0:T(8,128)(2,1)} %bitcast.17, bf16[128,128]{1,0:T(8,128)(2,1)} %copy-done.5, ...), custom_call_target="tpu_custom_call" | custom-call | tf_op jit(solution)/shard_map/pallas_call | solution.py:389
  (64 shorter events, 18.6 us)
Async XLA Ops:
  1.8 17.9 %collective-permute-start.1 = (bf16[256,768]{1,0:T(8,128)(2,1)}, bf16[256,768]{1,0:T(8,128)(2,1)S(1)}, u32[]{:S(2)}, u32[]{:S(2)}) collective-permute-start(bf16[256,768]{1,0:T(8,128)(2,1)} %shard_map.91.refs_0_), channel_id=1, source_target_pairs={{0,224},{32,0},{64,32},{96,64},{128,96},{160,128},{192,160},{224,1... | collective-permute-start | bytes 1179656 | tf_op jit(solution)/shard_map/ppermute | solution.py:330
  7.7 12.0 %collective-permute-start = (bf16[256,768]{1,0:T(8,128)(2,1)}, bf16[256,768]{1,0:T(8,128)(2,1)S(1)}, u32[]{:S(2)}, u32[]{:S(2)}) collective-permute-start(bf16[256,768]{1,0:T(8,128)(2,1)} %shard_map.91.refs_0_), channel_id=1, source_target_pairs={{0,32},{32,64},{64,96},{96,128},{128,160},{160,192},{192,224},{224... | collective-permute-start | bytes 1179656 | tf_op jit(solution)/shard_map/ppermute | solution.py:331
  10.2 33.7 %copy-start.10 = (bf16[8,64,256]{2,1,0:T(8,128)(2,1)S(1)}, bf16[8,64,256]{2,1,0:T(8,128)(2,1)}, u32[]{:S(2)}) copy-start(bf16[8,64,256]{2,1,0:T(8,128)(2,1)} %get-tuple-element.44) | copy-start | bytes 786436
  10.2 13.6 %all-to-all-start = ((bf16[4,2,2,128,128]{4,3,2,1,0:T(8,128)(2,1)}), bf16[4,2,2,128,128]{4,3,2,1,0:T(8,128)(2,1)S(1)}, u32[]{:S(2)}, u32[]{:S(2)}) async-start(bf16[4,2,2,128,128]{4,3,2,1,0:T(8,128)(2,1)} %get-tuple-element.35), calls=%async_computation | async-start | bytes 1048576 | tf_op jit(solution)/shard_map/all_to_all | solution.py:326
  19.7 40.1 %copy-start.14 = (bf16[256,768]{1,0:T(8,128)(2,1)}, bf16[256,768]{1,0:T(8,128)(2,1)S(1)}, u32[]{:S(2)}) copy-start(bf16[256,768]{1,0:T(8,128)(2,1)S(1)} %collective-permute-done.refs_7_) | copy-start | bytes 1179652
  19.7 10.9 %collective-permute-start.2 = (bf16[256,768]{1,0:T(8,128)(2,1)S(1)}, bf16[256,768]{1,0:T(8,128)(2,1)S(1)}, u32[]{:S(2)}, u32[]{:S(2)}) collective-permute-start(bf16[256,768]{1,0:T(8,128)(2,1)S(1)} %collective-permute-done.refs_7_), channel_id=1, source_target_pairs={{0,32},{32,64},{64,96},{96,128},{128,160},{160,192},{192,224},{224... | collective-permute-start | bytes 1179656 | tf_op jit(solution)/shard_map/ppermute | solution.py:331
  19.7 40.0 %copy-start.13 = (bf16[256,768]{1,0:T(8,128)(2,1)}, bf16[256,768]{1,0:T(8,128)(2,1)S(1)}, u32[]{:S(2)}) copy-start(bf16[256,768]{1,0:T(8,128)(2,1)S(1)} %collective-permute-done.1.refs_1_) | copy-start | bytes 1179652
  19.7 10.9 %collective-permute-start.4 = (bf16[256,768]{1,0:T(8,128)(2,1)S(1)}, bf16[256,768]{1,0:T(8,128)(2,1)}, u32[]{:S(2)}, u32[]{:S(2)}) collective-permute-start(bf16[256,768]{1,0:T(8,128)(2,1)S(1)} %collective-permute-done.1.refs_1_), channel_id=1, source_target_pairs={{0,224},{32,0},{64,32},{96,64},{128,96},{160,128},{192,160},{224,1... | collective-permute-start | bytes 1179656 | tf_op jit(solution)/shard_map/ppermute | solution.py:330
  23.8 17.5 %all-to-all-start.1 = ((bf16[4,64,2048]{2,1,0:T(8,128)(2,1)}), bf16[4,64,2048]{2,1,0:T(8,128)(2,1)S(1)}, u32[]{:S(2)}, u32[]{:S(2)}) async-start(bf16[4,64,2048]{2,1,0:T(8,128)(2,1)} %get-tuple-element.37), calls=%async_computation.1 | async-start | bytes 2097152 | tf_op jit(solution)/shard_map/all_to_all | solution.py:334
  30.6 10.0 %collective-permute-start.3 = (bf16[256,768]{1,0:T(8,128)(2,1)S(1)}, bf16[256,768]{1,0:T(8,128)(2,1)S(1)}, u32[]{:S(2)}, u32[]{:S(2)}) collective-permute-start(bf16[256,768]{1,0:T(8,128)(2,1)S(1)} %collective-permute-done.2.refs_6_), channel_id=1, source_target_pairs={{0,32},{32,64},{64,96},{96,128},{128,160},{160,192},{192,224},{224... | collective-permute-start | bytes 1179656 | tf_op jit(solution)/shard_map/ppermute | solution.py:331
  30.6 10.7 %collective-permute-start.5 = (bf16[256,768]{1,0:T(8,128)(2,1)}, bf16[256,768]{1,0:T(8,128)(2,1)}, u32[]{:S(2)}, u32[]{:S(2)}) collective-permute-start(bf16[256,768]{1,0:T(8,128)(2,1)} %collective-permute-done.4.refs_2_), channel_id=1, source_target_pairs={{0,224},{32,0},{64,32},{96,64},{128,96},{160,128},{192,160},{224,1... | collective-permute-start | bytes 1179656 | tf_op jit(solution)/shard_map/ppermute | solution.py:330
  41.3 18.4 %collective-permute-start.6 = (bf16[4,64,2048]{2,1,0:T(8,128)(2,1)S(1)}, bf16[4,64,2048]{2,1,0:T(8,128)(2,1)S(1)}, u32[]{:S(2)}, u32[]{:S(2)}) collective-permute-start(bf16[4,64,2048]{2,1,0:T(8,128)(2,1)S(1)} %all-to-all-done.1.received), channel_id=1, source_target_pairs={{0,1},{1,0},{2,3},{3,2},{4,5},{5,4},{6,7},{7,6},{8,9},{9,8},{10,11... | collective-permute-start | bytes 3145736 | tf_op jit(solution)/shard_map/ppermute | solution.py:337
  41.4 15.1 %collective-permute-start.8 = (bf16[16,128,128]{2,1,0:T(8,128)(2,1)S(1)}, bf16[16,128,128]{2,1,0:T(8,128)(2,1)S(1)}, u32[]{:S(2)}, u32[]{:S(2)}) collective-permute-start(bf16[16,128,128]{2,1,0:T(8,128)(2,1)S(1)} %bitcast.12), channel_id=1, source_target_pairs={{0,224},{32,0},{64,32},{96,64},{128,96},{160,128},{192,160},{224,1... | collective-permute-start | bytes 1572872 | tf_op jit(solution)/shard_map/ppermute | solution.py:332
  43.9 12.6 %collective-permute-start.7 = (bf16[256,768]{1,0:T(8,128)(2,1)}, bf16[256,768]{1,0:T(8,128)(2,1)S(1)}, u32[]{:S(2)}, u32[]{:S(2)}) collective-permute-start(bf16[256,768]{1,0:T(8,128)(2,1)} %copy-done.16), channel_id=1, source_target_pairs={{0,32},{32,64},{64,96},{96,128},{128,160},{160,192},{192,224},{224... | collective-permute-start | bytes 1179656 | tf_op jit(solution)/shard_map/ppermute | solution.py:333
  56.5 14.4 %collective-permute-start.10 = (bf16[16,128,128]{2,1,0:T(8,128)(2,1)S(1)}, bf16[16,128,128]{2,1,0:T(8,128)(2,1)S(1)}, u32[]{:S(2)}, u32[]{:S(2)}) collective-permute-start(bf16[16,128,128]{2,1,0:T(8,128)(2,1)S(1)} %bitcast.13), channel_id=1, source_target_pairs={{0,32},{32,64},{64,96},{96,128},{128,160},{160,192},{192,224},{224... | collective-permute-start | bytes 1572872 | tf_op jit(solution)/shard_map/ppermute | solution.py:340
  56.5 14.4 %collective-permute-start.9 = (bf16[16,128,128]{2,1,0:T(8,128)(2,1)S(1)}, bf16[16,128,128]{2,1,0:T(8,128)(2,1)}, u32[]{:S(2)}, u32[]{:S(2)}) collective-permute-start(bf16[16,128,128]{2,1,0:T(8,128)(2,1)S(1)} %collective-permute-done.8.refs_1_), channel_id=1, source_target_pairs={{0,224},{32,0},{64,32},{96,64},{128,96},{160,128},{192,160},{224,1... | collective-permute-start | bytes 1572872 | tf_op jit(solution)/shard_map/ppermute | solution.py:339
  66.1 34.3 %all-to-all-start.3 = ((f32[4,128,768]{2,1,0:T(8,128)}), f32[4,128,768]{2,1,0:T(8,128)S(1)}, u32[]{:S(2)}, u32[]{:S(2)}) async-start(f32[4,128,768]{2,1,0:T(8,128)} %shard_map.93), calls=%async_computation.3 | async-start | bytes 3145728 | tf_op jit(solution)/shard_map/all_to_all | solution.py:376
  70.9 13.6 %collective-permute-start.12 = (bf16[16,128,128]{2,1,0:T(8,128)(2,1)S(1)}, bf16[16,128,128]{2,1,0:T(8,128)(2,1)}, u32[]{:S(2)}, u32[]{:S(2)}) collective-permute-start(bf16[16,128,128]{2,1,0:T(8,128)(2,1)S(1)} %collective-permute-done.10.refs_7_), channel_id=1, source_target_pairs={{0,32},{32,64},{64,96},{96,128},{128,160},{160,192},{192,224},{224... | collective-permute-start | bytes 1572872 | tf_op jit(solution)/shard_map/ppermute | solution.py:356
  70.9 13.6 %collective-permute-start.11 = (bf16[16,128,128]{2,1,0:T(8,128)(2,1)}, bf16[16,128,128]{2,1,0:T(8,128)(2,1)}, u32[]{:S(2)}, u32[]{:S(2)}) collective-permute-start(bf16[16,128,128]{2,1,0:T(8,128)(2,1)} %collective-permute-done.9.refs_2_), channel_id=1, source_target_pairs={{0,224},{32,0},{64,32},{96,64},{128,96},{160,128},{192,160},{224,1... | collective-permute-start | bytes 1572872 | tf_op jit(solution)/shard_map/ppermute | solution.py:358
  74.9 30.0 %copy-start.3 = (s32[128,1]{1,0:T(8,128)}, s32[128,1]{1,0:T(8,128)S(1)}, u32[]{:S(2)}) copy-start(s32[128,1]{1,0:T(8,128)S(1)} %copy.10.column_ref) | copy-start | bytes 1540
  84.4 12.9 %collective-permute-start.14 = (bf16[16,128,128]{2,1,0:T(8,128)(2,1)}, bf16[16,128,128]{2,1,0:T(8,128)(2,1)}, u32[]{:S(2)}, u32[]{:S(2)}) collective-permute-start(bf16[16,128,128]{2,1,0:T(8,128)(2,1)} %collective-permute-done.12.refs_6_), channel_id=1, source_target_pairs={{0,32},{32,64},{64,96},{96,128},{128,160},{160,192},{192,224},{224... | collective-permute-start | bytes 1572872 | tf_op jit(solution)/shard_map/ppermute | solution.py:357
  84.4 12.9 %collective-permute-start.13 = (bf16[16,128,128]{2,1,0:T(8,128)(2,1)}, bf16[16,128,128]{2,1,0:T(8,128)(2,1)}, u32[]{:S(2)}, u32[]{:S(2)}) collective-permute-start(bf16[16,128,128]{2,1,0:T(8,128)(2,1)} %collective-permute-done.11.refs_3_), channel_id=1, source_target_pairs={{0,224},{32,0},{64,32},{96,64},{128,96},{160,128},{192,160},{224,1... | collective-permute-start | bytes 1572872 | tf_op jit(solution)/shard_map/ppermute | solution.py:374
  100.4 16.5 %all-to-all-start.4 = ((bf16[4,8,128,128]{3,2,1,0:T(8,128)(2,1)}), bf16[4,8,128,128]{3,2,1,0:T(8,128)(2,1)}, u32[]{:S(2)}, u32[]{:S(2)}) async-start(bf16[4,8,128,128]{3,2,1,0:T(8,128)(2,1)} %bitcast.7), calls=%async_computation.4 | async-start | bytes 2097152 | tf_op jit(solution)/shard_map/all_to_all | solution.py:388
  116.9 14.4 %all-to-all-start.5 = ((bf16[4,8,128,128]{3,2,1,0:T(8,128)(2,1)}), bf16[4,8,128,128]{3,2,1,0:T(8,128)(2,1)S(1)}, u32[]{:S(2)}, u32[]{:S(2)}) async-start(bf16[4,8,128,128]{3,2,1,0:T(8,128)(2,1)} %bitcast.9), calls=%async_computation.5 | async-start | bytes 2097152 | tf_op jit(solution)/shard_map/all_to_all | solution.py:405
  (14 other events, 90.7 us)

commit v5 on v4

--- a/solution.py
+++ b/solution.py
@@ -244,8 +244,8 @@
 
 
 def weigh_kernel(
-    query_ref, raw_ref, tables_ref, place_ref, past_ref, fresh_ref, column_ref,
-    out, tables, keys, scores, mass, sems, sem,
+    query_ref, raw_ref, tables_ref, place_ref, past_ref, fresh_ref, value_ref, column_ref,
+    out, early_ref, tables, keys, scores, mass, sems, sem,
 ):
     def fetching(step):
         some = pl.ds(pl.multiple_of(step * STEP, STEP), STEP)
@@ -277,8 +277,14 @@
         part = jnp.where(place_ref[...] <= column_ref[...], scores[pl.ds(at, SEL)], -jnp.inf)
         part = jnp.exp(part - jnp.max(part, axis=1, keepdims=True))
         part = part * (1.0 / jnp.sum(part, axis=1, keepdims=True))
-        mass[pl.ds(at, SEL)] = part.astype(jnp.bfloat16)
+        part = part.astype(jnp.bfloat16)
+        mass[pl.ds(at, SEL)] = part[:, HIST : HIST + CONTEXT]
         sending(at).start()
+        early = jnp.dot(part[:, :HIST], past_ref[:, HEAD:], preferred_element_type=jnp.float32)
+        early += jnp.dot(
+            part[:, HIST + CONTEXT :], value_ref[...], preferred_element_type=jnp.float32
+        )
+        early_ref[pl.ds(at, SEL)] = early
         return 0
 
     lax.fori_loop(0, QPER, soften, 0)
@@ -286,11 +292,10 @@
         sending(head * SEL).wait()
 
 
-def mix_kernel(mass_ref, value_ref, past_ref, fresh_ref, out_ref):
-    late = HIST + CONTEXT
-    mixed = jnp.dot(mass_ref[:, :HIST], past_ref[:, HEAD:], preferred_element_type=jnp.float32)
-    mixed += jnp.dot(mass_ref[:, late:], fresh_ref[...], preferred_element_type=jnp.float32)
-    mixed += jnp.dot(mass_ref[:, HIST:late], value_ref[...], preferred_element_type=jnp.float32)
+def mix_kernel(mass_ref, value_ref, early_ref, out_ref):
+    mixed = early_ref[...] + jnp.dot(
+        mass_ref[...], value_ref[...], preferred_element_type=jnp.float32
+    )
     for head in range(QPER):
         part = mixed[head * SEL : (head + 1) * SEL]
         out_ref[:, head * HEAD : (head + 1) * HEAD] = part.astype(jnp.bfloat16)
@@ -386,27 +391,30 @@
     )
 
     raw = lax.all_to_all(pick(z, block_lists, held, 0), "x", 0, 0, tiled=True)
-    mass = pl.pallas_call(
+    mass, early = pl.pallas_call(
         weigh_kernel,
-        out_shape=jax.ShapeDtypeStruct((QPER * SEL, KEYS), bf16),
-        in_specs=[VMEM] * 2 + [HBM] + [VMEM] * 4,
-        out_specs=HBM,
+        out_shape=[
+            jax.ShapeDtypeStruct((QPER * SEL, CONTEXT), bf16),
+            jax.ShapeDtypeStruct((QPER * SEL, HEAD), f32),
+        ],
+        in_specs=[VMEM] * 2 + [HBM] + [VMEM] * 5,
+        out_specs=[HBM, VMEM],
         scratch_shapes=[
             pltpu.VMEM((2, CONTEXT, HEAD), f32),
             pltpu.VMEM((KEYS, HEAD), bf16),
             pltpu.VMEM((QPER * SEL, KEYS), f32),
-            pltpu.VMEM((QPER * SEL, KEYS), bf16),
+            pltpu.VMEM((QPER * SEL, CONTEXT), bf16),
             pltpu.SemaphoreType.DMA((CONTEXT // STEP,)),
             pltpu.SemaphoreType.DMA,
         ],
         compiler_params=grant(56),
         cost_estimate=FREE,
-    )(queries, raw.reshape(CONTEXT, HEAD), tables, place, past, fresh_keys, column)
+    )(queries, raw.reshape(CONTEXT, HEAD), tables, place, past, fresh_keys, fresh_values, column)
     values = lax.all_to_all(pick(after(z, queries), block_lists, held, 1), "x", 0, 0, tiled=True)
     mixed = kernel_call(
         mix_kernel,
         jax.ShapeDtypeStruct((SEL, QPER * HEAD), bf16),
-        [mass, values.reshape(CONTEXT, HEAD), past, fresh_values],
+        [mass, values.reshape(CONTEXT, HEAD), early],
     )
     return mixed[None]
 

time: 136 us -> 137 us (level)
  waiting for transfers between devices: 37.9 us -> 36.2 us
  local copies, waits for them, and re-layouts: 8.23 us -> 9.62 us
    unnamed x37 -> x39, local copies, waits for them, and re-layouts: 8.12 us -> 9.5 us
  transfers between devices with their start and end apart: 20 -> 20, of which waited for: 10 -> 10; matrix products, arithmetic and copies ran while one was open for 0% -> 0% of each run, Pallas kernels for 21% -> 22%
where the time goes in v5:
time: 137 us; the launch traced here: 136 us
  starting transfers between devices  45.4 us (33%)
  waiting for transfers between devices  36.2 us (26%)
  Pallas kernels  33.2 us (24%)
  blocking collectives  10.9 us (8%)
  local copies, waits for them, and re-layouts  9.62 us (7%)
    ppermute x3, waiting for transfers between devices, per_device(): lax.ppermute(after(w_up[-1], w_down[max(step - 1, 0)]), 'z', UP)  15.1 us
    ppermute x3, starting transfers between devices, per_device(): w_down.append(lax.ppermute(after(w_down[-1], w_up[step]), 'z', DOWN))  12.4 us
    all_to_all x1, blocking collectives, per_device(): lax.all_to_all(after(past, received), 'head', 0, 0, tiled=True)  10.9 us
    pallas_call x1, Pallas kernels, per_device(): pl.pallas_call(weigh_kernel, out_shape=[jax.ShapeDtypeStruct((QPER * SEL,...  10.4 us
    unnamed x39, local copies, waits for them, and re-layouts  9.5 us
    ppermute x1, waiting for transfers between devices, per_device(): up.append(lax.ppermute(after(up[2], down[2]), 'z', UP))  9.3 us
    all_to_all x1, waiting for transfers between devices, per_device(): raw = lax.all_to_all(pick(z, block_lists, held, 0), 'x', 0, 0, tiled=True)  6.65 us
    pallas_call x2, Pallas kernels, pick(): pl.pallas_call(functools.partial(pick_kernel, kind), out_shape=jax.ShapeD...  6.23 us
  transfers between devices with their start and end apart: 20, of which 10 were waited for; matrix products, arithmetic and copies ran while one was open for 0% of the time, Pallas kernels for 22%

profile of v5, /device:TPU:8, one launch (start us, length us, event | category | flops | bytes accessed | tf_op | source)
XLA Modules:
  0.0 136.3 jit_solution(11278183369127679190)
XLA Ops:
  1.7 5.9 %collective-permute-start.1 = (bf16[256,768]{1,0:T(8,128)(2,1)}, bf16[256,768]{1,0:T(8,128)(2,1)S(1)}, u32[]{:S(2)}, u32[]{:S(2)}) collective-permute-start(bf16[256,768]{1,0:T(8,128)(2,1)} %shard_map.91.refs_0_), channel_id=1, source_target_pairs={{0,224},{32,0},{64,32},{96,64},{128,96},{160,128},{192,160},{224,1... | collective-permute-start | bytes 1179656 | tf_op jit(solution)/shard_map/ppermute | solution.py:335
  7.7 2.4 %shard_map.92 = (bf16[4,2,2,128,128]{4,3,2,1,0:T(8,128)(2,1)}, bf16[4,64,2048]{2,1,0:T(8,128)(2,1)}, bf16[8,64,256]{2,1,0:T(8,128)(2,1)}) custom-call(s32[1]{0:T(128)} %bitcast.1.z_ref, s32[1]{0:T(128)} %bitcast.head_ref, bf16[128,8192]{1,0:T(8,128)(2,1)} %bitcast.19, bf16[2,512,256]{2,1,0:T(8,128)(2,1)} %block.1, bf16[64,2048]{1,0:T(8,128)(2,1)} %bitcast.20), custom_call_target="tpu_custom_call" | custom-call | flops 49999998976 | bytes 1048576 | tf_op jit(solution)/shard_map/pallas_call | solution.py:320
  10.1 4.4 %all-to-all-start = ((bf16[4,2,2,128,128]{4,3,2,1,0:T(8,128)(2,1)}), bf16[4,2,2,128,128]{4,3,2,1,0:T(8,128)(2,1)S(1)}, u32[]{:S(2)}, u32[]{:S(2)}) async-start(bf16[4,2,2,128,128]{4,3,2,1,0:T(8,128)(2,1)} %get-tuple-element.37), calls=%async_computation | async-start | bytes 1048576 | tf_op jit(solution)/shard_map/all_to_all | solution.py:331
  14.6 5.1 %collective-permute-done.refs_7_ = bf16[256,768]{1,0:T(8,128)(2,1)S(1)} collective-permute-done((bf16[256,768]{1,0:T(8,128)(2,1)}, bf16[256,768]{1,0:T(8,128)(2,1)S(1)}, u32[]{:S(2)}, u32[]{:S(2)}) %collective-permute-start) | collective-permute-done | bytes 393248 | tf_op jit(solution)/shard_map/ppermute | solution.py:336
  19.7 3.2 %collective-permute-start.4 = (bf16[256,768]{1,0:T(8,128)(2,1)S(1)}, bf16[256,768]{1,0:T(8,128)(2,1)}, u32[]{:S(2)}, u32[]{:S(2)}) collective-permute-start(bf16[256,768]{1,0:T(8,128)(2,1)S(1)} %collective-permute-done.1.refs_1_), channel_id=1, source_target_pairs={{0,224},{32,0},{64,32},{96,64},{128,96},{160,128},{192,160},{224,1... | collective-permute-start | bytes 1179656 | tf_op jit(solution)/shard_map/ppermute | solution.py:335
  23.8 3.5 %all-to-all-start.1 = ((bf16[4,64,2048]{2,1,0:T(8,128)(2,1)}), bf16[4,64,2048]{2,1,0:T(8,128)(2,1)S(1)}, u32[]{:S(2)}, u32[]{:S(2)}) async-start(bf16[4,64,2048]{2,1,0:T(8,128)(2,1)} %get-tuple-element.39), calls=%async_computation.1 | async-start | bytes 2097152 | tf_op jit(solution)/shard_map/all_to_all | solution.py:339
  27.3 3.3 %collective-permute-done.2.refs_6_ = bf16[256,768]{1,0:T(8,128)(2,1)S(1)} collective-permute-done((bf16[256,768]{1,0:T(8,128)(2,1)S(1)}, bf16[256,768]{1,0:T(8,128)(2,1)S(1)}, u32[]{:S(2)}, u32[]{:S(2)}) %collective-permute-start.2) | collective-permute-done | bytes 393248 | tf_op jit(solution)/shard_map/ppermute | solution.py:336
  30.6 3.2 %collective-permute-start.5 = (bf16[256,768]{1,0:T(8,128)(2,1)}, bf16[256,768]{1,0:T(8,128)(2,1)}, u32[]{:S(2)}, u32[]{:S(2)}) collective-permute-start(bf16[256,768]{1,0:T(8,128)(2,1)} %collective-permute-done.4.refs_2_), channel_id=1, source_target_pairs={{0,224},{32,0},{64,32},{96,64},{128,96},{160,128},{192,160},{224,1... | collective-permute-start | bytes 1179656 | tf_op jit(solution)/shard_map/ppermute | solution.py:335
  33.8 6.7 %collective-permute-done.3.refs_5_ = bf16[256,768]{1,0:T(8,128)(2,1)S(1)} collective-permute-done((bf16[256,768]{1,0:T(8,128)(2,1)S(1)}, bf16[256,768]{1,0:T(8,128)(2,1)S(1)}, u32[]{:S(2)}, u32[]{:S(2)}) %collective-permute-start.3) | collective-permute-done | bytes 393248 | tf_op jit(solution)/shard_map/ppermute | solution.py:336
  41.4 2.5 %collective-permute-start.8 = (bf16[16,128,128]{2,1,0:T(8,128)(2,1)S(1)}, bf16[16,128,128]{2,1,0:T(8,128)(2,1)S(1)}, u32[]{:S(2)}, u32[]{:S(2)}) collective-permute-start(bf16[16,128,128]{2,1,0:T(8,128)(2,1)S(1)} %bitcast.12), channel_id=1, source_target_pairs={{0,224},{32,0},{64,32},{96,64},{128,96},{160,128},{192,160},{224,1... | collective-permute-start | bytes 1572872 | tf_op jit(solution)/shard_map/ppermute | solution.py:337
  43.9 10.9 %all_to_all.30 = bf16[8,64,256]{2,1,0:T(8,128)(2,1)} all-to-all(bf16[8,64,256]{2,1,0:T(8,128)(2,1)S(1)} %copy-done.11), channel_id=1, replica_groups=mesh['z'=8,'x'=4,'head'=8] {'head'}, dimensions={0} | all-to-all | bytes 524288 | tf_op jit(solution)/shard_map/all_to_all | solution.py:340
  56.5 3.2 %collective-permute-start.9 = (bf16[16,128,128]{2,1,0:T(8,128)(2,1)S(1)}, bf16[16,128,128]{2,1,0:T(8,128)(2,1)}, u32[]{:S(2)}, u32[]{:S(2)}) collective-permute-start(bf16[16,128,128]{2,1,0:T(8,128)(2,1)S(1)} %collective-permute-done.8.refs_1_), channel_id=1, source_target_pairs={{0,224},{32,0},{64,32},{96,64},{128,96},{160,128},{192,160},{224,1... | collective-permute-start | bytes 1572872 | tf_op jit(solution)/shard_map/ppermute | solution.py:344
  60.8 5.3 %shard_map.93 = f32[4,128,768]{2,1,0:T(8,128)} custom-call(s32[1]{0:T(128)} %bitcast.head_ref, bf16[4,64,2048]{2,1,0:T(8,128)(2,1)} %copy-done.10, bf16[4,64,2048]{2,1,0:T(8,128)(2,1)} %copy-done.13, bf16[256,768]{1,0:T(8,128)(2,1)} %shard_map.91.refs_0_, bf16[256,768]{1,0:T(8,128)(2,1)} %copy-done.14, bf16[256,768]{1,0:T(8,128)(2,1)} %collective-permute-done.4.refs_2_, ...), custom_call_target="tpu_custom_call" | custom-call | flops 49999998976 | bytes 1048576 | tf_op jit(solution)/shard_map/pallas_call | solution.py:347
  66.1 4.4 %all-to-all-start.3 = ((f32[4,128,768]{2,1,0:T(8,128)}), f32[4,128,768]{2,1,0:T(8,128)S(1)}, u32[]{:S(2)}, u32[]{:S(2)}) async-start(f32[4,128,768]{2,1,0:T(8,128)} %shard_map.93), calls=%async_computation.3 | async-start | bytes 3145728 | tf_op jit(solution)/shard_map/all_to_all | solution.py:381
  70.8 3.3 %collective-permute-start.11 = (bf16[16,128,128]{2,1,0:T(8,128)(2,1)}, bf16[16,128,128]{2,1,0:T(8,128)(2,1)}, u32[]{:S(2)}, u32[]{:S(2)}) collective-permute-start(bf16[16,128,128]{2,1,0:T(8,128)(2,1)} %collective-permute-done.9.refs_2_), channel_id=1, source_target_pairs={{0,224},{32,0},{64,32},{96,64},{128,96},{160,128},{192,160},{224,1... | collective-permute-start | bytes 1572872 | tf_op jit(solution)/shard_map/ppermute | solution.py:363
  74.9 5.0 %shard_map.95 = (f32[2,4096,128]{2,1,0:T(8,128)S(1)}, s32[1,4736]{1,0:T(1,128)S(1)}) custom-call(s32[1]{0:T(128)S(6)} %copy.15.length_ref, s32[1,128]{1,0:T(1,128)S(1)} %copy-done.8, s32[128,1]{1,0:T(8,128)S(1)} %copy.10.column_ref, f32[1,128]{1,0:T(1,128)S(1)} %copy-done.9), custom_call_target="tpu_custom_call" | custom-call | tf_op jit(solution)/shard_map/pallas_call | solution.py:364
  84.4 3.5 %collective-permute-start.13 = (bf16[16,128,128]{2,1,0:T(8,128)(2,1)}, bf16[16,128,128]{2,1,0:T(8,128)(2,1)}, u32[]{:S(2)}, u32[]{:S(2)}) collective-permute-start(bf16[16,128,128]{2,1,0:T(8,128)(2,1)} %collective-permute-done.11.refs_3_), channel_id=1, source_target_pairs={{0,224},{32,0},{64,32},{96,64},{128,96},{160,128},{192,160},{224,1... | collective-permute-start | bytes 1572872 | tf_op jit(solution)/shard_map/ppermute | solution.py:379
  87.9 9.3 %collective-permute-done.14.refs_5_ = bf16[16,128,128]{2,1,0:T(8,128)(2,1)} collective-permute-done((bf16[16,128,128]{2,1,0:T(8,128)(2,1)}, bf16[16,128,128]{2,1,0:T(8,128)(2,1)}, u32[]{:S(2)}, u32[]{:S(2)}) %collective-permute-start.14) | collective-permute-done | bytes 524320 | tf_op jit(solution)/shard_map/ppermute | solution.py:362
  97.2 3.1 %shard_map.96 = bf16[32,128,128]{2,1,0:T(8,128)(2,1)} custom-call(s32[1]{0:T(128)} %bitcast.1.z_ref, s32[32,8]{1,0:T(8,128)S(1)} %copy.12.lists_ref, bf16[16,128,128]{2,1,0:T(8,128)(2,1)S(1)} %bitcast.14, bf16[16,128,128]{2,1,0:T(8,128)(2,1)S(1)} %collective-permute-done.8.refs_1_, bf16[16,128,128]{2,1,0:T(8,128)(2,1)} %collective-permute-done.9.refs_2_, ...), custom_call_target="tpu_custom_call" | custom-call | tf_op jit(solution)/shard_map/pallas_call | solution.py:160
  100.3 4.6 %all-to-all-start.4 = ((bf16[4,8,128,128]{3,2,1,0:T(8,128)(2,1)}), bf16[4,8,128,128]{3,2,1,0:T(8,128)(2,1)}, u32[]{:S(2)}, u32[]{:S(2)}) async-start(bf16[4,8,128,128]{3,2,1,0:T(8,128)(2,1)} %bitcast.7), calls=%async_computation.4 | async-start | bytes 2097152 | tf_op jit(solution)/shard_map/all_to_all | solution.py:393
  107.0 3.2 %shard_map.98 = bf16[32,128,128]{2,1,0:T(8,128)(2,1)} custom-call(s32[1]{0:T(128)} %bitcast.1.z_ref, s32[32,8]{1,0:T(8,128)S(1)} %copy.12.lists_ref, bf16[16,128,128]{2,1,0:T(8,128)(2,1)S(1)} %bitcast.15, bf16[16,128,128]{2,1,0:T(8,128)(2,1)S(1)} %collective-permute-done.8.refs_1_, bf16[16,128,128]{2,1,0:T(8,128)(2,1)} %collective-permute-done.9.refs_2_, ...), custom_call_target="tpu_custom_call" | custom-call | tf_op jit(solution)/shard_map/pallas_call | solution.py:160
  110.2 6.7 %all-to-all-done.4 = bf16[4,8,128,128]{3,2,1,0:T(8,128)(2,1)} async-done(((bf16[4,8,128,128]{3,2,1,0:T(8,128)(2,1)}), bf16[4,8,128,128]{3,2,1,0:T(8,128)(2,1)}, u32[]{:S(2)}, u32[]{:S(2)}) %all-to-all-start.4) | async-done | bytes 1048608 | tf_op jit(solution)/shard_map/all_to_all | solution.py:393
  116.8 3.5 %all-to-all-start.5 = ((bf16[4,8,128,128]{3,2,1,0:T(8,128)(2,1)}), bf16[4,8,128,128]{3,2,1,0:T(8,128)(2,1)S(1)}, u32[]{:S(2)}, u32[]{:S(2)}) async-start(bf16[4,8,128,128]{3,2,1,0:T(8,128)(2,1)} %bitcast.9), calls=%async_computation.5 | async-start | bytes 2097152 | tf_op jit(solution)/shard_map/all_to_all | solution.py:413
  120.4 10.4 %shard_map.97 = (bf16[512,4096]{1,0:T(8,128)(2,1)}, f32[512,128]{1,0:T(8,128)}) custom-call(bf16[512,128]{1,0:T(8,128)(2,1)} %copy-done.4, bf16[4096,128]{1,0:T(8,128)(2,1)} %bitcast.8.raw_ref, f32[2,4096,128]{2,1,0:T(8,128)} %copy-done, s32[1,4736]{1,0:T(1,128)} %copy-done.7, bf16[512,256]{1,0:T(8,128)(2,1)} %bitcast.18, bf16[128,128]{1,0:T(8,128)(2,1)} %copy-done.5, ...), custom_call_target="tpu_custom_call" | custom-call | tf_op jit(solution)/shard_map/pallas_call | solution.py:394
  (66 shorter events, 18.8 us)
Async XLA Ops:
  1.7 17.9 %collective-permute-start.1 = (bf16[256,768]{1,0:T(8,128)(2,1)}, bf16[256,768]{1,0:T(8,128)(2,1)S(1)}, u32[]{:S(2)}, u32[]{:S(2)}) collective-permute-start(bf16[256,768]{1,0:T(8,128)(2,1)} %shard_map.91.refs_0_), channel_id=1, source_target_pairs={{0,224},{32,0},{64,32},{96,64},{128,96},{160,128},{192,160},{224,1... | collective-permute-start | bytes 1179656 | tf_op jit(solution)/shard_map/ppermute | solution.py:335
  7.7 12.0 %collective-permute-start = (bf16[256,768]{1,0:T(8,128)(2,1)}, bf16[256,768]{1,0:T(8,128)(2,1)S(1)}, u32[]{:S(2)}, u32[]{:S(2)}) collective-permute-start(bf16[256,768]{1,0:T(8,128)(2,1)} %shard_map.91.refs_0_), channel_id=1, source_target_pairs={{0,32},{32,64},{64,96},{96,128},{128,160},{160,192},{192,224},{224... | collective-permute-start | bytes 1179656 | tf_op jit(solution)/shard_map/ppermute | solution.py:336
  10.1 33.8 %copy-start.11 = (bf16[8,64,256]{2,1,0:T(8,128)(2,1)S(1)}, bf16[8,64,256]{2,1,0:T(8,128)(2,1)}, u32[]{:S(2)}) copy-start(bf16[8,64,256]{2,1,0:T(8,128)(2,1)} %get-tuple-element.46) | copy-start | bytes 786436
  10.1 13.6 %all-to-all-start = ((bf16[4,2,2,128,128]{4,3,2,1,0:T(8,128)(2,1)}), bf16[4,2,2,128,128]{4,3,2,1,0:T(8,128)(2,1)S(1)}, u32[]{:S(2)}, u32[]{:S(2)}) async-start(bf16[4,2,2,128,128]{4,3,2,1,0:T(8,128)(2,1)} %get-tuple-element.37), calls=%async_computation | async-start | bytes 1048576 | tf_op jit(solution)/shard_map/all_to_all | solution.py:331
  19.7 40.1 %copy-start.15 = (bf16[256,768]{1,0:T(8,128)(2,1)}, bf16[256,768]{1,0:T(8,128)(2,1)S(1)}, u32[]{:S(2)}) copy-start(bf16[256,768]{1,0:T(8,128)(2,1)S(1)} %collective-permute-done.refs_7_) | copy-start | bytes 1179652
  19.7 10.9 %collective-permute-start.2 = (bf16[256,768]{1,0:T(8,128)(2,1)S(1)}, bf16[256,768]{1,0:T(8,128)(2,1)S(1)}, u32[]{:S(2)}, u32[]{:S(2)}) collective-permute-start(bf16[256,768]{1,0:T(8,128)(2,1)S(1)} %collective-permute-done.refs_7_), channel_id=1, source_target_pairs={{0,32},{32,64},{64,96},{96,128},{128,160},{160,192},{192,224},{224... | collective-permute-start | bytes 1179656 | tf_op jit(solution)/shard_map/ppermute | solution.py:336
  19.7 40.0 %copy-start.14 = (bf16[256,768]{1,0:T(8,128)(2,1)}, bf16[256,768]{1,0:T(8,128)(2,1)S(1)}, u32[]{:S(2)}) copy-start(bf16[256,768]{1,0:T(8,128)(2,1)S(1)} %collective-permute-done.1.refs_1_) | copy-start | bytes 1179652
  19.7 10.9 %collective-permute-start.4 = (bf16[256,768]{1,0:T(8,128)(2,1)S(1)}, bf16[256,768]{1,0:T(8,128)(2,1)}, u32[]{:S(2)}, u32[]{:S(2)}) collective-permute-start(bf16[256,768]{1,0:T(8,128)(2,1)S(1)} %collective-permute-done.1.refs_1_), channel_id=1, source_target_pairs={{0,224},{32,0},{64,32},{96,64},{128,96},{160,128},{192,160},{224,1... | collective-permute-start | bytes 1179656 | tf_op jit(solution)/shard_map/ppermute | solution.py:335
  23.8 17.5 %all-to-all-start.1 = ((bf16[4,64,2048]{2,1,0:T(8,128)(2,1)}), bf16[4,64,2048]{2,1,0:T(8,128)(2,1)S(1)}, u32[]{:S(2)}, u32[]{:S(2)}) async-start(bf16[4,64,2048]{2,1,0:T(8,128)(2,1)} %get-tuple-element.39), calls=%async_computation.1 | async-start | bytes 2097152 | tf_op jit(solution)/shard_map/all_to_all | solution.py:339
  30.5 10.0 %collective-permute-start.3 = (bf16[256,768]{1,0:T(8,128)(2,1)S(1)}, bf16[256,768]{1,0:T(8,128)(2,1)S(1)}, u32[]{:S(2)}, u32[]{:S(2)}) collective-permute-start(bf16[256,768]{1,0:T(8,128)(2,1)S(1)} %collective-permute-done.2.refs_6_), channel_id=1, source_target_pairs={{0,32},{32,64},{64,96},{96,128},{128,160},{160,192},{192,224},{224... | collective-permute-start | bytes 1179656 | tf_op jit(solution)/shard_map/ppermute | solution.py:336
  30.6 10.7 %collective-permute-start.5 = (bf16[256,768]{1,0:T(8,128)(2,1)}, bf16[256,768]{1,0:T(8,128)(2,1)}, u32[]{:S(2)}, u32[]{:S(2)}) collective-permute-start(bf16[256,768]{1,0:T(8,128)(2,1)} %collective-permute-done.4.refs_2_), channel_id=1, source_target_pairs={{0,224},{32,0},{64,32},{96,64},{128,96},{160,128},{192,160},{224,1... | collective-permute-start | bytes 1179656 | tf_op jit(solution)/shard_map/ppermute | solution.py:335
  41.3 18.5 %collective-permute-start.6 = (bf16[4,64,2048]{2,1,0:T(8,128)(2,1)S(1)}, bf16[4,64,2048]{2,1,0:T(8,128)(2,1)S(1)}, u32[]{:S(2)}, u32[]{:S(2)}) collective-permute-start(bf16[4,64,2048]{2,1,0:T(8,128)(2,1)S(1)} %all-to-all-done.1.received), channel_id=1, source_target_pairs={{0,1},{1,0},{2,3},{3,2},{4,5},{5,4},{6,7},{7,6},{8,9},{9,8},{10,11... | collective-permute-start | bytes 3145736 | tf_op jit(solution)/shard_map/ppermute | solution.py:342
  41.4 15.1 %collective-permute-start.8 = (bf16[16,128,128]{2,1,0:T(8,128)(2,1)S(1)}, bf16[16,128,128]{2,1,0:T(8,128)(2,1)S(1)}, u32[]{:S(2)}, u32[]{:S(2)}) collective-permute-start(bf16[16,128,128]{2,1,0:T(8,128)(2,1)S(1)} %bitcast.12), channel_id=1, source_target_pairs={{0,224},{32,0},{64,32},{96,64},{128,96},{160,128},{192,160},{224,1... | collective-permute-start | bytes 1572872 | tf_op jit(solution)/shard_map/ppermute | solution.py:337
  43.9 12.6 %collective-permute-start.7 = (bf16[256,768]{1,0:T(8,128)(2,1)}, bf16[256,768]{1,0:T(8,128)(2,1)S(1)}, u32[]{:S(2)}, u32[]{:S(2)}) collective-permute-start(bf16[256,768]{1,0:T(8,128)(2,1)} %copy-done.17), channel_id=1, source_target_pairs={{0,32},{32,64},{64,96},{96,128},{128,160},{160,192},{192,224},{224... | collective-permute-start | bytes 1179656 | tf_op jit(solution)/shard_map/ppermute | solution.py:338
  56.5 14.4 %collective-permute-start.10 = (bf16[16,128,128]{2,1,0:T(8,128)(2,1)S(1)}, bf16[16,128,128]{2,1,0:T(8,128)(2,1)S(1)}, u32[]{:S(2)}, u32[]{:S(2)}) collective-permute-start(bf16[16,128,128]{2,1,0:T(8,128)(2,1)S(1)} %bitcast.13), channel_id=1, source_target_pairs={{0,32},{32,64},{64,96},{96,128},{128,160},{160,192},{192,224},{224... | collective-permute-start | bytes 1572872 | tf_op jit(solution)/shard_map/ppermute | solution.py:345
  56.5 14.4 %collective-permute-start.9 = (bf16[16,128,128]{2,1,0:T(8,128)(2,1)S(1)}, bf16[16,128,128]{2,1,0:T(8,128)(2,1)}, u32[]{:S(2)}, u32[]{:S(2)}) collective-permute-start(bf16[16,128,128]{2,1,0:T(8,128)(2,1)S(1)} %collective-permute-done.8.refs_1_), channel_id=1, source_target_pairs={{0,224},{32,0},{64,32},{96,64},{128,96},{160,128},{192,160},{224,1... | collective-permute-start | bytes 1572872 | tf_op jit(solution)/shard_map/ppermute | solution.py:344
  66.1 34.2 %all-to-all-start.3 = ((f32[4,128,768]{2,1,0:T(8,128)}), f32[4,128,768]{2,1,0:T(8,128)S(1)}, u32[]{:S(2)}, u32[]{:S(2)}) async-start(f32[4,128,768]{2,1,0:T(8,128)} %shard_map.93), calls=%async_computation.3 | async-start | bytes 3145728 | tf_op jit(solution)/shard_map/all_to_all | solution.py:381
  70.8 13.5 %collective-permute-start.12 = (bf16[16,128,128]{2,1,0:T(8,128)(2,1)S(1)}, bf16[16,128,128]{2,1,0:T(8,128)(2,1)}, u32[]{:S(2)}, u32[]{:S(2)}) collective-permute-start(bf16[16,128,128]{2,1,0:T(8,128)(2,1)S(1)} %collective-permute-done.10.refs_7_), channel_id=1, source_target_pairs={{0,32},{32,64},{64,96},{96,128},{128,160},{160,192},{192,224},{224... | collective-permute-start | bytes 1572872 | tf_op jit(solution)/shard_map/ppermute | solution.py:361
  70.8 13.5 %collective-permute-start.11 = (bf16[16,128,128]{2,1,0:T(8,128)(2,1)}, bf16[16,128,128]{2,1,0:T(8,128)(2,1)}, u32[]{:S(2)}, u32[]{:S(2)}) collective-permute-start(bf16[16,128,128]{2,1,0:T(8,128)(2,1)} %collective-permute-done.9.refs_2_), channel_id=1, source_target_pairs={{0,224},{32,0},{64,32},{96,64},{128,96},{160,128},{192,160},{224,1... | collective-permute-start | bytes 1572872 | tf_op jit(solution)/shard_map/ppermute | solution.py:363
  74.9 30.0 %copy-start.2 = (s32[128,1]{1,0:T(8,128)}, s32[128,1]{1,0:T(8,128)S(1)}, u32[]{:S(2)}) copy-start(s32[128,1]{1,0:T(8,128)S(1)} %copy.10.column_ref) | copy-start | bytes 1540
  84.4 12.8 %collective-permute-start.14 = (bf16[16,128,128]{2,1,0:T(8,128)(2,1)}, bf16[16,128,128]{2,1,0:T(8,128)(2,1)}, u32[]{:S(2)}, u32[]{:S(2)}) collective-permute-start(bf16[16,128,128]{2,1,0:T(8,128)(2,1)} %collective-permute-done.12.refs_6_), channel_id=1, source_target_pairs={{0,32},{32,64},{64,96},{96,128},{128,160},{160,192},{192,224},{224... | collective-permute-start | bytes 1572872 | tf_op jit(solution)/shard_map/ppermute | solution.py:362
  84.4 12.8 %collective-permute-start.13 = (bf16[16,128,128]{2,1,0:T(8,128)(2,1)}, bf16[16,128,128]{2,1,0:T(8,128)(2,1)}, u32[]{:S(2)}, u32[]{:S(2)}) collective-permute-start(bf16[16,128,128]{2,1,0:T(8,128)(2,1)} %collective-permute-done.11.refs_3_), channel_id=1, source_target_pairs={{0,224},{32,0},{64,32},{96,64},{128,96},{160,128},{192,160},{224,1... | collective-permute-start | bytes 1572872 | tf_op jit(solution)/shard_map/ppermute | solution.py:379
  100.3 16.5 %all-to-all-start.4 = ((bf16[4,8,128,128]{3,2,1,0:T(8,128)(2,1)}), bf16[4,8,128,128]{3,2,1,0:T(8,128)(2,1)}, u32[]{:S(2)}, u32[]{:S(2)}) async-start(bf16[4,8,128,128]{3,2,1,0:T(8,128)(2,1)} %bitcast.7), calls=%async_computation.4 | async-start | bytes 2097152 | tf_op jit(solution)/shard_map/all_to_all | solution.py:393
  116.8 14.4 %all-to-all-start.5 = ((bf16[4,8,128,128]{3,2,1,0:T(8,128)(2,1)}), bf16[4,8,128,128]{3,2,1,0:T(8,128)(2,1)S(1)}, u32[]{:S(2)}, u32[]{:S(2)}) async-start(bf16[4,8,128,128]{3,2,1,0:T(8,128)(2,1)} %bitcast.9), calls=%async_computation.5 | async-start | bytes 2097152 | tf_op jit(solution)/shard_map/all_to_all | solution.py:413
  (15 other events, 81.3 us)

commit v6 on v4

--- a/solution.py
+++ b/solution.py
@@ -320,7 +320,7 @@
         scratch_shapes=[pltpu.VMEM(shape, bf16) for shape in shapes]
         + [pltpu.SemaphoreType.DMA((6,))],
         compiler_params=grant(56),
-        cost_estimate=COST,
+        cost_estimate=FREE,
     )(z, head, after(hidden[0], both), block_kv, history_kv[0])
 
     pieces = lax.all_to_all(pieces, "x", 0, 0, tiled=True)
@@ -351,7 +351,7 @@
             pltpu.SemaphoreType.DMA((2,)),
         ],
         compiler_params=grant(56),
-        cost_estimate=COST,
+        cost_estimate=FREE,
     )(head, after(received, past), swapped, *weights)
     up.append(lax.ppermute(after(up[1], down[1], partial), "z", UP))
     up.append(lax.ppermute(after(up[2], down[2]), "z", UP))

time: 136 us -> 136 us (level)
    unnamed x37 -> x39, local copies, waits for them, and re-layouts: 8.12 us -> 8.12 us
where the time goes in v6:
time: 136 us; the launch traced here: 135 us
  starting transfers between devices  45.1 us (33%)
  waiting for transfers between devices  37.9 us (28%)
  Pallas kernels  32.3 us (24%)
  blocking collectives  10.9 us (8%)
  local copies, waits for them, and re-layouts  8.23 us (6%)
    ppermute x3, waiting for transfers between devices, per_device(): lax.ppermute(after(w_up[-1], w_down[max(step - 1, 0)]), 'z', UP)  15 us
    ppermute x3, starting transfers between devices, per_device(): w_down.append(lax.ppermute(after(w_down[-1], w_up[step]), 'z', DOWN))  12.4 us
    all_to_all x1, blocking collectives, per_device(): lax.all_to_all(after(past, received), 'head', 0, 0, tiled=True)  10.9 us
    pallas_call x1, Pallas kernels, per_device(): pl.pallas_call(weigh_kernel, out_shape=jax.ShapeDtypeStruct((QPER * SEL,...  9.36 us
    ppermute x1, waiting for transfers between devices, per_device(): up.append(lax.ppermute(after(up[2], down[2]), 'z', UP))  9.29 us
    unnamed x39, local copies, waits for them, and re-layouts  8.12 us
    all_to_all x1, waiting for transfers between devices, per_device(): raw = lax.all_to_all(pick(z, block_lists, held, 0), 'x', 0, 0, tiled=True)  7.27 us
    pallas_call x2, Pallas kernels, pick(): pl.pallas_call(functools.partial(pick_kernel, kind), out_shape=jax.ShapeD...  6.23 us
  transfers between devices with their start and end apart: 20, of which 10 were waited for; matrix products, arithmetic and copies ran while one was open for 0% of the time, Pallas kernels for 21%

profile of v6, /device:TPU:8, one launch (start us, length us, event | category | flops | bytes accessed | tf_op | source)
XLA Modules:
  0.0 135.4 jit_solution(6853722621140545903)
XLA Ops:
  1.7 5.9 %collective-permute-start.1 = (bf16[256,768]{1,0:T(8,128)(2,1)}, bf16[256,768]{1,0:T(8,128)(2,1)S(1)}, u32[]{:S(2)}, u32[]{:S(2)}) collective-permute-start(bf16[256,768]{1,0:T(8,128)(2,1)} %shard_map.91.refs_0_), channel_id=1, source_target_pairs={{0,224},{32,0},{64,32},{96,64},{128,96},{160,128},{192,160},{224,1... | collective-permute-start | bytes 1179656 | tf_op jit(solution)/shard_map/ppermute | solution.py:330
  7.7 2.5 %shard_map.92 = (bf16[4,2,2,128,128]{4,3,2,1,0:T(8,128)(2,1)}, bf16[4,64,2048]{2,1,0:T(8,128)(2,1)}, bf16[8,64,256]{2,1,0:T(8,128)(2,1)}) custom-call(s32[1]{0:T(128)} %bitcast.1.z_ref, s32[1]{0:T(128)} %bitcast.head_ref, bf16[128,8192]{1,0:T(8,128)(2,1)} %bitcast.20, bf16[2,512,256]{2,1,0:T(8,128)(2,1)} %block.1, bf16[64,2048]{1,0:T(8,128)(2,1)} %bitcast.21), custom_call_target="tpu_custom_call" | custom-call | tf_op jit(solution)/shard_map/pallas_call | solution.py:315
  10.2 4.4 %all-to-all-start = ((bf16[4,2,2,128,128]{4,3,2,1,0:T(8,128)(2,1)}), bf16[4,2,2,128,128]{4,3,2,1,0:T(8,128)(2,1)S(1)}, u32[]{:S(2)}, u32[]{:S(2)}) async-start(bf16[4,2,2,128,128]{4,3,2,1,0:T(8,128)(2,1)} %get-tuple-element.35), calls=%async_computation | async-start | bytes 1048576 | tf_op jit(solution)/shard_map/all_to_all | solution.py:326
  14.6 5.1 %collective-permute-done.refs_7_ = bf16[256,768]{1,0:T(8,128)(2,1)S(1)} collective-permute-done((bf16[256,768]{1,0:T(8,128)(2,1)}, bf16[256,768]{1,0:T(8,128)(2,1)S(1)}, u32[]{:S(2)}, u32[]{:S(2)}) %collective-permute-start) | collective-permute-done | bytes 393248 | tf_op jit(solution)/shard_map/ppermute | solution.py:331
  19.7 3.2 %collective-permute-start.4 = (bf16[256,768]{1,0:T(8,128)(2,1)S(1)}, bf16[256,768]{1,0:T(8,128)(2,1)S(1)}, u32[]{:S(2)}, u32[]{:S(2)}) collective-permute-start(bf16[256,768]{1,0:T(8,128)(2,1)S(1)} %collective-permute-done.1.refs_1_), channel_id=1, source_target_pairs={{0,224},{32,0},{64,32},{96,64},{128,96},{160,128},{192,160},{224,1... | collective-permute-start | bytes 1179656 | tf_op jit(solution)/shard_map/ppermute | solution.py:330
  23.8 3.5 %all-to-all-start.1 = ((bf16[4,64,2048]{2,1,0:T(8,128)(2,1)}), bf16[4,64,2048]{2,1,0:T(8,128)(2,1)S(1)}, u32[]{:S(2)}, u32[]{:S(2)}) async-start(bf16[4,64,2048]{2,1,0:T(8,128)(2,1)} %get-tuple-element.37), calls=%async_computation.1 | async-start | bytes 2097152 | tf_op jit(solution)/shard_map/all_to_all | solution.py:334
  27.3 3.2 %collective-permute-done.2.refs_6_ = bf16[256,768]{1,0:T(8,128)(2,1)S(1)} collective-permute-done((bf16[256,768]{1,0:T(8,128)(2,1)S(1)}, bf16[256,768]{1,0:T(8,128)(2,1)S(1)}, u32[]{:S(2)}, u32[]{:S(2)}) %collective-permute-start.2) | collective-permute-done | bytes 393248 | tf_op jit(solution)/shard_map/ppermute | solution.py:331
  30.6 3.2 %collective-permute-start.5 = (bf16[256,768]{1,0:T(8,128)(2,1)S(1)}, bf16[256,768]{1,0:T(8,128)(2,1)}, u32[]{:S(2)}, u32[]{:S(2)}) collective-permute-start(bf16[256,768]{1,0:T(8,128)(2,1)S(1)} %collective-permute-done.4.refs_2_), channel_id=1, source_target_pairs={{0,224},{32,0},{64,32},{96,64},{128,96},{160,128},{192,160},{224,1... | collective-permute-start | bytes 1179656 | tf_op jit(solution)/shard_map/ppermute | solution.py:330
  33.8 6.7 %collective-permute-done.3.refs_5_ = bf16[256,768]{1,0:T(8,128)(2,1)S(1)} collective-permute-done((bf16[256,768]{1,0:T(8,128)(2,1)S(1)}, bf16[256,768]{1,0:T(8,128)(2,1)S(1)}, u32[]{:S(2)}, u32[]{:S(2)}) %collective-permute-start.3) | collective-permute-done | bytes 393248 | tf_op jit(solution)/shard_map/ppermute | solution.py:331
  43.7 10.9 %all_to_all.30 = bf16[8,64,256]{2,1,0:T(8,128)(2,1)} all-to-all(bf16[8,64,256]{2,1,0:T(8,128)(2,1)S(1)} %copy-done.17), channel_id=1, replica_groups=mesh['z'=8,'x'=4,'head'=8] {'head'}, dimensions={0} | all-to-all | bytes 524288 | tf_op jit(solution)/shard_map/all_to_all | solution.py:335
  56.3 3.2 %collective-permute-start.9 = (bf16[16,128,128]{2,1,0:T(8,128)(2,1)S(1)}, bf16[16,128,128]{2,1,0:T(8,128)(2,1)}, u32[]{:S(2)}, u32[]{:S(2)}) collective-permute-start(bf16[16,128,128]{2,1,0:T(8,128)(2,1)S(1)} %collective-permute-done.8.refs_1_), channel_id=1, source_target_pairs={{0,224},{32,0},{64,32},{96,64},{128,96},{160,128},{192,160},{224,1... | collective-permute-start | bytes 1572872 | tf_op jit(solution)/shard_map/ppermute | solution.py:339
  60.5 5.2 %shard_map.93 = f32[4,128,768]{2,1,0:T(8,128)} custom-call(s32[1]{0:T(128)} %bitcast.head_ref, bf16[4,64,2048]{2,1,0:T(8,128)(2,1)} %copy-done.9, bf16[4,64,2048]{2,1,0:T(8,128)(2,1)} %copy-done.10, bf16[256,768]{1,0:T(8,128)(2,1)} %shard_map.91.refs_0_, bf16[256,768]{1,0:T(8,128)(2,1)} %copy-done.11, bf16[256,768]{1,0:T(8,128)(2,1)} %copy-done.14, ...), custom_call_target="tpu_custom_call" | custom-call | tf_op jit(solution)/shard_map/pallas_call | solution.py:342
  65.8 4.4 %all-to-all-start.3 = ((f32[4,128,768]{2,1,0:T(8,128)}), f32[4,128,768]{2,1,0:T(8,128)S(1)}, u32[]{:S(2)}, u32[]{:S(2)}) async-start(f32[4,128,768]{2,1,0:T(8,128)} %shard_map.93), calls=%async_computation.3 | async-start | bytes 3145728 | tf_op jit(solution)/shard_map/all_to_all | solution.py:376
  70.6 3.3 %collective-permute-start.11 = (bf16[16,128,128]{2,1,0:T(8,128)(2,1)}, bf16[16,128,128]{2,1,0:T(8,128)(2,1)}, u32[]{:S(2)}, u32[]{:S(2)}) collective-permute-start(bf16[16,128,128]{2,1,0:T(8,128)(2,1)} %collective-permute-done.9.refs_2_), channel_id=1, source_target_pairs={{0,224},{32,0},{64,32},{96,64},{128,96},{160,128},{192,160},{224,1... | collective-permute-start | bytes 1572872 | tf_op jit(solution)/shard_map/ppermute | solution.py:358
  74.7 5.0 %shard_map.95 = (f32[2,4096,128]{2,1,0:T(8,128)S(1)}, s32[1,4736]{1,0:T(1,128)S(1)}) custom-call(s32[1]{0:T(128)S(6)} %copy.15.length_ref, s32[1,128]{1,0:T(1,128)S(1)} %copy-done.7, s32[128,1]{1,0:T(8,128)S(1)} %copy.10.column_ref, f32[1,128]{1,0:T(1,128)S(1)} %copy-done.8), custom_call_target="tpu_custom_call" | custom-call | tf_op jit(solution)/shard_map/pallas_call | solution.py:359
  84.2 3.5 %collective-permute-start.13 = (bf16[16,128,128]{2,1,0:T(8,128)(2,1)}, bf16[16,128,128]{2,1,0:T(8,128)(2,1)}, u32[]{:S(2)}, u32[]{:S(2)}) collective-permute-start(bf16[16,128,128]{2,1,0:T(8,128)(2,1)} %collective-permute-done.11.refs_3_), channel_id=1, source_target_pairs={{0,224},{32,0},{64,32},{96,64},{128,96},{160,128},{192,160},{224,1... | collective-permute-start | bytes 1572872 | tf_op jit(solution)/shard_map/ppermute | solution.py:374
  87.7 9.3 %collective-permute-done.14.refs_5_ = bf16[16,128,128]{2,1,0:T(8,128)(2,1)} collective-permute-done((bf16[16,128,128]{2,1,0:T(8,128)(2,1)}, bf16[16,128,128]{2,1,0:T(8,128)(2,1)}, u32[]{:S(2)}, u32[]{:S(2)}) %collective-permute-start.14) | collective-permute-done | bytes 524320 | tf_op jit(solution)/shard_map/ppermute | solution.py:357
  97.0 3.1 %shard_map.96 = bf16[32,128,128]{2,1,0:T(8,128)(2,1)} custom-call(s32[1]{0:T(128)} %bitcast.1.z_ref, s32[32,8]{1,0:T(8,128)S(1)} %copy.12.lists_ref, bf16[16,128,128]{2,1,0:T(8,128)(2,1)S(1)} %bitcast.14, bf16[16,128,128]{2,1,0:T(8,128)(2,1)S(1)} %collective-permute-done.8.refs_1_, bf16[16,128,128]{2,1,0:T(8,128)(2,1)} %collective-permute-done.9.refs_2_, ...), custom_call_target="tpu_custom_call" | custom-call | tf_op jit(solution)/shard_map/pallas_call | solution.py:160
  100.1 4.5 %all-to-all-start.4 = ((bf16[4,8,128,128]{3,2,1,0:T(8,128)(2,1)}), bf16[4,8,128,128]{3,2,1,0:T(8,128)(2,1)}, u32[]{:S(2)}, u32[]{:S(2)}) async-start(bf16[4,8,128,128]{3,2,1,0:T(8,128)(2,1)} %bitcast.7), calls=%async_computation.4 | async-start | bytes 2097152 | tf_op jit(solution)/shard_map/all_to_all | solution.py:388
  106.1 3.2 %shard_map.98 = bf16[32,128,128]{2,1,0:T(8,128)(2,1)} custom-call(s32[1]{0:T(128)} %bitcast.1.z_ref, s32[32,8]{1,0:T(8,128)S(1)} %copy.12.lists_ref, bf16[16,128,128]{2,1,0:T(8,128)(2,1)S(1)} %bitcast.15, bf16[16,128,128]{2,1,0:T(8,128)(2,1)S(1)} %collective-permute-done.8.refs_1_, bf16[16,128,128]{2,1,0:T(8,128)(2,1)} %collective-permute-done.9.refs_2_, ...), custom_call_target="tpu_custom_call" | custom-call | tf_op jit(solution)/shard_map/pallas_call | solution.py:160
  109.3 7.3 %all-to-all-done.4 = bf16[4,8,128,128]{3,2,1,0:T(8,128)(2,1)} async-done(((bf16[4,8,128,128]{3,2,1,0:T(8,128)(2,1)}), bf16[4,8,128,128]{3,2,1,0:T(8,128)(2,1)}, u32[]{:S(2)}, u32[]{:S(2)}) %all-to-all-start.4) | async-done | bytes 1048608 | tf_op jit(solution)/shard_map/all_to_all | solution.py:388
  116.6 3.5 %all-to-all-start.5 = ((bf16[4,8,128,128]{3,2,1,0:T(8,128)(2,1)}), bf16[4,8,128,128]{3,2,1,0:T(8,128)(2,1)S(1)}, u32[]{:S(2)}, u32[]{:S(2)}) async-start(bf16[4,8,128,128]{3,2,1,0:T(8,128)(2,1)} %bitcast.9), calls=%async_computation.5 | async-start | bytes 2097152 | tf_op jit(solution)/shard_map/all_to_all | solution.py:405
  120.1 9.4 %shard_map.97.mass_ref = bf16[512,4736]{1,0:T(8,128)(2,1)} custom-call(bf16[512,128]{1,0:T(8,128)(2,1)} %copy-done.4, bf16[4096,128]{1,0:T(8,128)(2,1)} %bitcast.8.raw_ref, f32[2,4096,128]{2,1,0:T(8,128)} %copy-done.1, s32[1,4736]{1,0:T(1,128)} %copy-done.6, bf16[512,256]{1,0:T(8,128)(2,1)} %bitcast.17, bf16[128,128]{1,0:T(8,128)(2,1)} %copy-done.5, ...), custom_call_target="tpu_custom_call" | custom-call | tf_op jit(solution)/shard_map/pallas_call | solution.py:389
  130.9 2.4 %copy-done = bf16[512,4736]{1,0:T(8,128)(2,1)S(1)} copy-done((bf16[512,4736]{1,0:T(8,128)(2,1)S(1)}, bf16[512,4736]{1,0:T(8,128)(2,1)}, u32[]{:S(2)}) %copy-start) | copy-done | bytes 4849688
  (66 shorter events, 18.6 us)
Async XLA Ops:
  1.7 17.9 %collective-permute-start.1 = (bf16[256,768]{1,0:T(8,128)(2,1)}, bf16[256,768]{1,0:T(8,128)(2,1)S(1)}, u32[]{:S(2)}, u32[]{:S(2)}) collective-permute-start(bf16[256,768]{1,0:T(8,128)(2,1)} %shard_map.91.refs_0_), channel_id=1, source_target_pairs={{0,224},{32,0},{64,32},{96,64},{128,96},{160,128},{192,160},{224,1... | collective-permute-start | bytes 1179656 | tf_op jit(solution)/shard_map/ppermute | solution.py:330
  7.7 12.0 %collective-permute-start = (bf16[256,768]{1,0:T(8,128)(2,1)}, bf16[256,768]{1,0:T(8,128)(2,1)S(1)}, u32[]{:S(2)}, u32[]{:S(2)}) collective-permute-start(bf16[256,768]{1,0:T(8,128)(2,1)} %shard_map.91.refs_0_), channel_id=1, source_target_pairs={{0,32},{32,64},{64,96},{96,128},{128,160},{160,192},{192,224},{224... | collective-permute-start | bytes 1179656 | tf_op jit(solution)/shard_map/ppermute | solution.py:331
  10.2 33.5 %copy-start.17 = (bf16[8,64,256]{2,1,0:T(8,128)(2,1)S(1)}, bf16[8,64,256]{2,1,0:T(8,128)(2,1)}, u32[]{:S(2)}) copy-start(bf16[8,64,256]{2,1,0:T(8,128)(2,1)} %get-tuple-element.44) | copy-start | bytes 786436
  10.2 13.6 %all-to-all-start = ((bf16[4,2,2,128,128]{4,3,2,1,0:T(8,128)(2,1)}), bf16[4,2,2,128,128]{4,3,2,1,0:T(8,128)(2,1)S(1)}, u32[]{:S(2)}, u32[]{:S(2)}) async-start(bf16[4,2,2,128,128]{4,3,2,1,0:T(8,128)(2,1)} %get-tuple-element.35), calls=%async_computation | async-start | bytes 1048576 | tf_op jit(solution)/shard_map/all_to_all | solution.py:326
  19.7 39.8 %copy-start.12 = (bf16[256,768]{1,0:T(8,128)(2,1)}, bf16[256,768]{1,0:T(8,128)(2,1)S(1)}, u32[]{:S(2)}) copy-start(bf16[256,768]{1,0:T(8,128)(2,1)S(1)} %collective-permute-done.refs_7_) | copy-start | bytes 1179652
  19.7 10.9 %collective-permute-start.2 = (bf16[256,768]{1,0:T(8,128)(2,1)S(1)}, bf16[256,768]{1,0:T(8,128)(2,1)S(1)}, u32[]{:S(2)}, u32[]{:S(2)}) collective-permute-start(bf16[256,768]{1,0:T(8,128)(2,1)S(1)} %collective-permute-done.refs_7_), channel_id=1, source_target_pairs={{0,32},{32,64},{64,96},{96,128},{128,160},{160,192},{192,224},{224... | collective-permute-start | bytes 1179656 | tf_op jit(solution)/shard_map/ppermute | solution.py:331
  19.7 39.8 %copy-start.11 = (bf16[256,768]{1,0:T(8,128)(2,1)}, bf16[256,768]{1,0:T(8,128)(2,1)S(1)}, u32[]{:S(2)}) copy-start(bf16[256,768]{1,0:T(8,128)(2,1)S(1)} %collective-permute-done.1.refs_1_) | copy-start | bytes 1179652
  19.7 10.9 %collective-permute-start.4 = (bf16[256,768]{1,0:T(8,128)(2,1)S(1)}, bf16[256,768]{1,0:T(8,128)(2,1)S(1)}, u32[]{:S(2)}, u32[]{:S(2)}) collective-permute-start(bf16[256,768]{1,0:T(8,128)(2,1)S(1)} %collective-permute-done.1.refs_1_), channel_id=1, source_target_pairs={{0,224},{32,0},{64,32},{96,64},{128,96},{160,128},{192,160},{224,1... | collective-permute-start | bytes 1179656 | tf_op jit(solution)/shard_map/ppermute | solution.py:330
  23.8 17.5 %all-to-all-start.1 = ((bf16[4,64,2048]{2,1,0:T(8,128)(2,1)}), bf16[4,64,2048]{2,1,0:T(8,128)(2,1)S(1)}, u32[]{:S(2)}, u32[]{:S(2)}) async-start(bf16[4,64,2048]{2,1,0:T(8,128)(2,1)} %get-tuple-element.37), calls=%async_computation.1 | async-start | bytes 2097152 | tf_op jit(solution)/shard_map/all_to_all | solution.py:334
  30.6 10.0 %collective-permute-start.3 = (bf16[256,768]{1,0:T(8,128)(2,1)S(1)}, bf16[256,768]{1,0:T(8,128)(2,1)S(1)}, u32[]{:S(2)}, u32[]{:S(2)}) collective-permute-start(bf16[256,768]{1,0:T(8,128)(2,1)S(1)} %collective-permute-done.2.refs_6_), channel_id=1, source_target_pairs={{0,32},{32,64},{64,96},{96,128},{128,160},{160,192},{192,224},{224... | collective-permute-start | bytes 1179656 | tf_op jit(solution)/shard_map/ppermute | solution.py:331
  30.6 10.7 %collective-permute-start.5 = (bf16[256,768]{1,0:T(8,128)(2,1)S(1)}, bf16[256,768]{1,0:T(8,128)(2,1)}, u32[]{:S(2)}, u32[]{:S(2)}) collective-permute-start(bf16[256,768]{1,0:T(8,128)(2,1)S(1)} %collective-permute-done.4.refs_2_), channel_id=1, source_target_pairs={{0,224},{32,0},{64,32},{96,64},{128,96},{160,128},{192,160},{224,1... | collective-permute-start | bytes 1179656 | tf_op jit(solution)/shard_map/ppermute | solution.py:330
  41.3 18.2 %collective-permute-start.6 = (bf16[4,64,2048]{2,1,0:T(8,128)(2,1)S(1)}, bf16[4,64,2048]{2,1,0:T(8,128)(2,1)S(1)}, u32[]{:S(2)}, u32[]{:S(2)}) collective-permute-start(bf16[4,64,2048]{2,1,0:T(8,128)(2,1)S(1)} %all-to-all-done.1.received), channel_id=1, source_target_pairs={{0,1},{1,0},{2,3},{3,2},{4,5},{5,4},{6,7},{7,6},{8,9},{9,8},{10,11... | collective-permute-start | bytes 3145736 | tf_op jit(solution)/shard_map/ppermute | solution.py:337
  41.4 14.9 %collective-permute-start.8 = (bf16[16,128,128]{2,1,0:T(8,128)(2,1)S(1)}, bf16[16,128,128]{2,1,0:T(8,128)(2,1)S(1)}, u32[]{:S(2)}, u32[]{:S(2)}) collective-permute-start(bf16[16,128,128]{2,1,0:T(8,128)(2,1)S(1)} %bitcast.12), channel_id=1, source_target_pairs={{0,224},{32,0},{64,32},{96,64},{128,96},{160,128},{192,160},{224,1... | collective-permute-start | bytes 1572872 | tf_op jit(solution)/shard_map/ppermute | solution.py:332
  43.7 12.6 %collective-permute-start.7 = (bf16[256,768]{1,0:T(8,128)(2,1)}, bf16[256,768]{1,0:T(8,128)(2,1)S(1)}, u32[]{:S(2)}, u32[]{:S(2)}) collective-permute-start(bf16[256,768]{1,0:T(8,128)(2,1)} %copy-done.15), channel_id=1, source_target_pairs={{0,32},{32,64},{64,96},{96,128},{128,160},{160,192},{192,224},{224... | collective-permute-start | bytes 1179656 | tf_op jit(solution)/shard_map/ppermute | solution.py:333
  56.3 14.4 %collective-permute-start.10 = (bf16[16,128,128]{2,1,0:T(8,128)(2,1)S(1)}, bf16[16,128,128]{2,1,0:T(8,128)(2,1)S(1)}, u32[]{:S(2)}, u32[]{:S(2)}) collective-permute-start(bf16[16,128,128]{2,1,0:T(8,128)(2,1)S(1)} %bitcast.13), channel_id=1, source_target_pairs={{0,32},{32,64},{64,96},{96,128},{128,160},{160,192},{192,224},{224... | collective-permute-start | bytes 1572872 | tf_op jit(solution)/shard_map/ppermute | solution.py:340
  56.3 14.4 %collective-permute-start.9 = (bf16[16,128,128]{2,1,0:T(8,128)(2,1)S(1)}, bf16[16,128,128]{2,1,0:T(8,128)(2,1)}, u32[]{:S(2)}, u32[]{:S(2)}) collective-permute-start(bf16[16,128,128]{2,1,0:T(8,128)(2,1)S(1)} %collective-permute-done.8.refs_1_), channel_id=1, source_target_pairs={{0,224},{32,0},{64,32},{96,64},{128,96},{160,128},{192,160},{224,1... | collective-permute-start | bytes 1572872 | tf_op jit(solution)/shard_map/ppermute | solution.py:339
  65.8 34.3 %all-to-all-start.3 = ((f32[4,128,768]{2,1,0:T(8,128)}), f32[4,128,768]{2,1,0:T(8,128)S(1)}, u32[]{:S(2)}, u32[]{:S(2)}) async-start(f32[4,128,768]{2,1,0:T(8,128)} %shard_map.93), calls=%async_computation.3 | async-start | bytes 3145728 | tf_op jit(solution)/shard_map/all_to_all | solution.py:376
  70.6 13.5 %collective-permute-start.12 = (bf16[16,128,128]{2,1,0:T(8,128)(2,1)S(1)}, bf16[16,128,128]{2,1,0:T(8,128)(2,1)}, u32[]{:S(2)}, u32[]{:S(2)}) collective-permute-start(bf16[16,128,128]{2,1,0:T(8,128)(2,1)S(1)} %collective-permute-done.10.refs_7_), channel_id=1, source_target_pairs={{0,32},{32,64},{64,96},{96,128},{128,160},{160,192},{192,224},{224... | collective-permute-start | bytes 1572872 | tf_op jit(solution)/shard_map/ppermute | solution.py:356
  70.6 13.5 %collective-permute-start.11 = (bf16[16,128,128]{2,1,0:T(8,128)(2,1)}, bf16[16,128,128]{2,1,0:T(8,128)(2,1)}, u32[]{:S(2)}, u32[]{:S(2)}) collective-permute-start(bf16[16,128,128]{2,1,0:T(8,128)(2,1)} %collective-permute-done.9.refs_2_), channel_id=1, source_target_pairs={{0,224},{32,0},{64,32},{96,64},{128,96},{160,128},{192,160},{224,1... | collective-permute-start | bytes 1572872 | tf_op jit(solution)/shard_map/ppermute | solution.py:358
  74.7 29.9 %copy-start.3 = (s32[128,1]{1,0:T(8,128)}, s32[128,1]{1,0:T(8,128)S(1)}, u32[]{:S(2)}) copy-start(s32[128,1]{1,0:T(8,128)S(1)} %copy.10.column_ref) | copy-start | bytes 1540
  84.2 12.8 %collective-permute-start.14 = (bf16[16,128,128]{2,1,0:T(8,128)(2,1)}, bf16[16,128,128]{2,1,0:T(8,128)(2,1)}, u32[]{:S(2)}, u32[]{:S(2)}) collective-permute-start(bf16[16,128,128]{2,1,0:T(8,128)(2,1)} %collective-permute-done.12.refs_6_), channel_id=1, source_target_pairs={{0,32},{32,64},{64,96},{96,128},{128,160},{160,192},{192,224},{224... | collective-permute-start | bytes 1572872 | tf_op jit(solution)/shard_map/ppermute | solution.py:357
  84.2 12.8 %collective-permute-start.13 = (bf16[16,128,128]{2,1,0:T(8,128)(2,1)}, bf16[16,128,128]{2,1,0:T(8,128)(2,1)}, u32[]{:S(2)}, u32[]{:S(2)}) collective-permute-start(bf16[16,128,128]{2,1,0:T(8,128)(2,1)} %collective-permute-done.11.refs_3_), channel_id=1, source_target_pairs={{0,224},{32,0},{64,32},{96,64},{128,96},{160,128},{192,160},{224,1... | collective-permute-start | bytes 1572872 | tf_op jit(solution)/shard_map/ppermute | solution.py:374
  100.1 16.4 %all-to-all-start.4 = ((bf16[4,8,128,128]{3,2,1,0:T(8,128)(2,1)}), bf16[4,8,128,128]{3,2,1,0:T(8,128)(2,1)}, u32[]{:S(2)}, u32[]{:S(2)}) async-start(bf16[4,8,128,128]{3,2,1,0:T(8,128)(2,1)} %bitcast.7), calls=%async_computation.4 | async-start | bytes 2097152 | tf_op jit(solution)/shard_map/all_to_all | solution.py:388
  116.6 14.4 %all-to-all-start.5 = ((bf16[4,8,128,128]{3,2,1,0:T(8,128)(2,1)}), bf16[4,8,128,128]{3,2,1,0:T(8,128)(2,1)S(1)}, u32[]{:S(2)}, u32[]{:S(2)}) async-start(bf16[4,8,128,128]{3,2,1,0:T(8,128)(2,1)} %bitcast.9), calls=%async_computation.5 | async-start | bytes 2097152 | tf_op jit(solution)/shard_map/all_to_all | solution.py:405
  (15 other events, 101.6 us)
